TPU v7x, 32 devices: a whole 2x2x4 slice. The times are simulated.
32 devices in a mesh: groups: 2 (over y), dp: 4 (over z), mp: 4 (over x, core).
Axes of the slice: x: 2, y: 2, z: 4, core: 2. Of those that a mesh axis runs over, the one named last changes fastest.
Arguments:
- qkv_home: bfloat16 [8, 764, 3, 3072], P(('groups', 'dp'), None, None, 'mp'), parts along dimension 0, may hold values from -6 to 6
- resid_home: bfloat16 [8, 764, 6144], P(('groups', 'dp'), None, 'mp'), parts along dimension 0, may hold values from -6 to 6
- out_weight: bfloat16 [3072, 6144], P('dp', 'mp'), may hold values from -0.109375 to 0.109375
- label_weight: bfloat16 [6144, 12288], P('mp', 'dp'), may hold values from -0.21875 to 0.21875
- label_bias: float32 [12288], P('dp'), may hold values from -5 to 5
- query_gain: float32 [128], replicated, may hold values from 0.25 to 1.75
- key_gain: float32 [128], replicated, may hold values from 0.25 to 1.75
- patch_counts: int32 [8, 4], P('groups'), parts along dimension 0, may hold values from 1 to 191, as said below
- move_plan: int32 [8, 4], P('groups'), parts along dimension 0, may hold values from 0 to 3, as said below
- segment_ids: int32 [8, 764], P(('groups', 'dp')), parts along dimension 0, may hold values from 0 to 4, as said below
Outputs:
- mixed: bfloat16 [8, 384, 6144], P(('groups', 'dp'), None, 'mp'), parts along dimension 0
- labels: float32 [8, 4, 12288], P(('groups', 'dp'), 'mp'), parts along dimension 0
There are 2 independent parts, one for each index of `groups`. A program takes and returns all parts, laid end to end along the dimension named above; an argument that names none is the same for every part. Nothing has to cross between parts.
Inputs may be any that keep to these rules, and one draw needn't show every extreme that they name: `patch_counts`: home row r holds its 4 images packed in the order j; every destination row receives exactly one image from every home row, 384 patches in all; every draw holds an image of 191 patches. Every row of move_plan is a permutation, and every destination row appears once in every column, so each destination receives one image from each home row. `segment_ids`: image j of home row r has id j on its patch_counts[r, j] slots, which follow those of image j - 1; slots after the last image have id 4.
All inputs are finite; a program needn't handle non-finite values.
Results may differ from a plain program's by a relative error of at most 0.0065.
Values may be sent and summed in bfloat16 or wider, within the bound.
No kernel may reach another device: no remote copies, remote signals or barrier semaphores. Data moves between devices by JAX's collectives and lax.ppermute only.
A program may use at most 64 MiB of HBM per device.

v0:
```python
import math

import jax
import jax.numpy as jnp
from jax import lax
from jax.sharding import PartitionSpec as P

TOK = 384


EPSILON = 1e-06


def head_norm(values, norm_gain):
    center = values - jnp.mean(values, axis=-1, keepdims=True)
    spread = jnp.mean(center * center, axis=-1, keepdims=True)
    return center * lax.rsqrt(spread + EPSILON) * norm_gain


def attend(qkv_rows, seg_rows, query_gain, key_gain):
    length = qkv_rows.shape[0]
    head_width = query_gain.shape[0]
    head_count = qkv_rows.shape[2] // head_width
    split_parts = qkv_rows.reshape(length, 3, head_count, head_width)
    queries = head_norm(split_parts[:, 0].astype(jnp.float32), query_gain).astype(jnp.bfloat16)
    key_rows = head_norm(split_parts[:, 1].astype(jnp.float32), key_gain).astype(jnp.bfloat16)
    scores = jnp.einsum(
        "qhd,khd->hqk", queries, key_rows, preferred_element_type=jnp.float32
    ) / math.sqrt(head_width)
    same_image = seg_rows[:, None] == seg_rows[None, :]
    raised = jnp.where(same_image[None], jnp.exp(scores), 0.0)
    weights = (raised / jnp.sum(raised, axis=-1, keepdims=True)).astype(jnp.bfloat16)
    head_out = jnp.einsum(
        "hqk,khd->qhd", weights, split_parts[:, 2], preferred_element_type=jnp.float32
    )
    return head_out.reshape(length, head_count * head_width).astype(jnp.bfloat16)


def project(heads_local, resid_rows, out_weight):
    gathered = lax.all_gather(heads_local, "mp", axis=1, tiled=True)
    running = resid_rows.astype(jnp.float32) + jnp.dot(
        gathered,
        lax.all_gather(out_weight, "dp", axis=0, tiled=True),
        preferred_element_type=jnp.float32,
    )
    return running.astype(jnp.bfloat16)


def pool(row_mixed, seg_rows, count_row):
    images = count_row.shape[0]
    member_ids = lax.broadcasted_iota(jnp.int32, (images, seg_rows.shape[0]), 0)
    member = (member_ids == seg_rows[None, :]).astype(jnp.bfloat16)
    image_sums = jnp.dot(member, row_mixed, preferred_element_type=jnp.float32)
    return (image_sums / count_row[:, None].astype(jnp.float32)).astype(jnp.bfloat16)


def label_terms(pooled, label_weight):
    return jnp.einsum(
        "abd,dc->abc",
        lax.all_gather(pooled[None], "dp", axis=0, tiled=True),
        label_weight,
        preferred_element_type=jnp.float32,
    )


def pick(values, row_index, is_valid):
    taken = jnp.take(values, row_index, axis=0)
    taken = taken.reshape(is_valid.shape + values.shape[1:])
    keep_mask = is_valid.reshape(is_valid.shape + (1,) * (values.ndim - 1))
    return jnp.where(keep_mask, taken, jnp.zeros_like(taken))


def on_device(
    qkv_home,
    resid_home,
    out_weight,
    label_weight,
    label_bias,
    query_gain,
    key_gain,
    patch_counts,
    move_plan,
    segment_ids,
):
    row_count = lax.axis_size("dp")
    my_index = lax.axis_index("dp")
    home_slots = segment_ids.shape[1]
    pair_slots = home_slots // row_count
    image_ids = lax.broadcasted_iota(jnp.int32, (row_count, row_count, row_count), 2)
    image_ends = jnp.cumsum(patch_counts, axis=1)
    starts = image_ends - patch_counts
    matches = (move_plan[:, :, None] == image_ids).astype(jnp.int32)
    image_sizes = jnp.sum(patch_counts[:, :, None] * matches, axis=1)
    firsts = jnp.sum(starts[:, :, None] * matches, axis=1)
    send_sizes = lax.dynamic_index_in_dim(image_sizes, my_index, 0, keepdims=False)
    send_firsts = lax.dynamic_index_in_dim(firsts, my_index, 0, keepdims=False)
    within = lax.broadcasted_iota(jnp.int32, (row_count, pair_slots), 1)
    send_valid = within < send_sizes[:, None]
    send_index = jnp.minimum(send_firsts[:, None] + within, home_slots - 1).reshape(-1)
    arrive_sizes = lax.dynamic_index_in_dim(image_sizes, my_index, 1, keepdims=False)
    arrive_ends = jnp.cumsum(arrive_sizes)
    arrive_starts = arrive_ends - arrive_sizes
    slot_grid = lax.broadcasted_iota(jnp.int32, (TOK, row_count), 0)
    source = jnp.sum((slot_grid >= arrive_ends[None, :]).astype(jnp.int32), axis=1)
    chosen = (source[:, None] == lax.broadcasted_iota(jnp.int32, (TOK, row_count), 1)).astype(
        jnp.int32
    )
    arrive_index = (
        source * pair_slots + slot_grid[:, 0] - jnp.sum(chosen * arrive_starts[None, :], axis=1)
    )
    home_mixed = project(
        attend(qkv_home[0], segment_ids[0], query_gain, key_gain), resid_home[0], out_weight
    )
    count_row = lax.dynamic_index_in_dim(patch_counts, my_index, 0, keepdims=False)
    pooled = pool(home_mixed, segment_ids[0], count_row)
    partial_value = label_terms(pooled, label_weight)
    send_mixed = pick(home_mixed, send_index, send_valid)
    got_mixed = lax.all_to_all(send_mixed, "dp", split_axis=0, concat_axis=0, tiled=True)
    mixed = jnp.take(got_mixed.reshape(row_count * pair_slots, -1), arrive_index, axis=0)
    logit_sums = lax.psum_scatter(
        partial_value.astype(jnp.bfloat16), "mp", scatter_dimension=1, tiled=True
    ).astype(jnp.float32)
    class_probs = jax.nn.sigmoid(logit_sums + label_bias[None, None, :])
    labels = lax.all_to_all(
        class_probs.astype(jnp.bfloat16), "dp", split_axis=0, concat_axis=2, tiled=True
    ).astype(class_probs.dtype)
    return (mixed[None], labels)


def solution(mesh):
    return jax.shard_map(
        on_device,
        mesh=mesh,
        in_specs=(
            P(("groups", "dp"), None, None, "mp"),
            P(("groups", "dp"), None, "mp"),
            P("dp", "mp"),
            P("mp", "dp"),
            P("dp"),
            P(),
            P(),
            P("groups", None),
            P("groups", None),
            P(("groups", "dp"), None),
        ),
        out_specs=(P(("groups", "dp"), None, "mp"), P(("groups", "dp"), "mp", None)),
        check_vma=False,
    )
```

profile of v0, /device:TPU:0, one launch (start us, length us, event | category | flops | bytes accessed | tf_op | source)
XLA Modules:
  0.0 383.1 jit_solution(16641087347745729092)
XLA Ops:
  7.2 4.3 %copy.31 = bf16[1,764,3,768]{1,3,2,0:T(8,128)(2,1)S(1)} copy(bf16[1,764,3,768]{3,1,2,0:T(8,128)(2,1)} %param.10) | data formatting | bytes 7041024 | tf_op args[0]
  12.0 0.7 fusion.11
  14.4 8.7 %fusion = (f32[6,764]{1,0:T(8,128)}, f32[6,764,764]{1,2,0:T(8,128)}) fusion(pred[764,764]{0,1:T(8,128)(4,1)S(1)} %broadcast_compare_fusion, f32[128]{0:T(128)S(1)} %copy-done.7, f32[764,6]{0,1:T(8,128)} %add_rsqrt_fusion, f32[764,6]{0,1:T(8,128)} %copy-done.1, bf16[764,3,6,128]{0,3,2,1:T(8,128)(2,1)S(1)} %bitcast.68, f32[128]{0:T(128)S(1)} %copy-done.8, ...), kind=kOutput, calls=%fused_computation.4 | convolution fusion | flops 912926592 | bytes 17050528 | tf_op jit(solution)/shard_map/qhd,khd->hqk/dot_general | solution.py:27
  23.0 8.3 %fusion.22 = bf16[6,764,128]{1,2,0:T(8,128)(2,1)} fusion(f32[6,764,764]{1,2,0:T(8,128)} %get-tuple-element.13, f32[6,764]{1,0:T(8,128)} %get-tuple-element.12, pred[764,764]{0,1:T(8,128)(4,1)} %copy-done, bf16[764,3,6,128]{0,3,2,1:T(8,128)(2,1)S(1)} %bitcast.69), kind=kOutput, calls=%fused_computation.31 | convolution fusion | flops 911152512 | bytes 16963888 | tf_op jit(solution)/shard_map/hqk,khd->qhd/dot_general | solution.py:33
  31.4 0.7 all-gather.7.cloned.1.call-update
  32.8 38.9 %all-gather.5.cloned.1.call-done = bf16[764,3072]{0,1:T(8,128)(2,1)} async-done(((bf16[764,768]{0,1:T(8,128)(2,1)}), bf16[764,3072]{0,1:T(8,128)(2,1)}) %all-gather.5.cloned.1.call-update) | async-done | bytes 4694032 | tf_op jit(solution)/shard_map/all_gather | solution.py:40
  71.7 168.4 %all-gather.7.cloned.1.call-done = bf16[3072,1536]{1,0:T(8,128)(2,1)} async-done(((bf16[768,1536]{1,0:T(8,128)(2,1)}), bf16[3072,1536]{1,0:T(8,128)(2,1)}) %all-gather.7.cloned.1.call-update) | async-done | bytes 9437200 | tf_op jit(solution)/shard_map/all_gather | solution.py:43
  240.1 12.0 %fusion.4 = bf16[764,1536]{1,0:T(8,128)(2,1)S(1)} fusion(bf16[764,3072]{0,1:T(8,128)(2,1)} %all-gather.5.cloned.1.call-done, bf16[3072,1536]{1,0:T(8,128)(2,1)} %all-gather.7.cloned.1.call-done, bf16[1,764,1536]{2,1,0:T(8,128)(2,1)} %param.11), kind=kOutput, calls=%fused_computation.9 | convolution fusion | flops 7213529088 | bytes 18825216 | tf_op jit(solution)/shard_map/dot_general | solution.py:41
  252.5 13.3 %all-gather.1 = bf16[4,4,1536]{2,1,0:T(4,128)(2,1)S(1)} all-gather(bf16[1,4,1536]{2,1,0:T(4,128)(2,1)S(1)} %fusion.21), channel_id=2, replica_groups=mesh['groups'=2,'dp'=4,'mp'=4] {'dp'}, dimensions={0}, use_global_device_ids=true | all-gather | bytes 61440 | tf_op jit(solution)/shard_map/all_gather | solution.py:60
  265.8 5.1 %fusion.5 = bf16[4,4,3072]{2,1,0:T(4,128)(2,1)S(1)} fusion(bf16[4,4,1536]{2,1,0:T(4,128)(2,1)S(1)} %all-gather.1, bf16[1536,3072]{1,0:T(8,128)(2,1)} %param.13), kind=kOutput, calls=%fused_computation.10 | convolution fusion | flops 151044096 | bytes 9584640 | tf_op jit(solution)/shard_map/abd,dc->abc/dot_general | solution.py:58
  270.9 0.7 copy.35
  272.2 3.8 gather_fusion
  276.0 2.3 gather.13
  278.3 22.9 %all-reduce.3.cloned.1.call-done = bf16[4,4,3072]{2,0,1:T(4,128)(2,1)} async-done(((bf16[4,4,3072]{2,0,1:T(4,128)(2,1)}), bf16[4,4,3072]{2,0,1:T(4,128)(2,1)}) %all-reduce.3.cloned.1.call-update) | async-done | bytes 98320
  301.2 1.4 fusion.34
  304.4 4.6 %all-to-all-start.1 = ((bf16[4,2,1536]{2,1,0:T(2,128)(2,1)}), bf16[4,2,1536]{2,1,0:T(2,128)(2,1)S(1)}, u32[]{:S(2)}, u32[]{:S(2)}) async-start(bf16[4,2,1536]{2,1,0:T(2,128)(2,1)} %reshape.285), calls=%async_computation.1 | async-start | bytes 49152 | tf_op jit(solution)/shard_map/all_to_all | solution.py:124
  309.0 1.7 select_select_fusion
  310.8 3.9 %all-to-all-done.1 = bf16[4,2,1536]{2,1,0:T(2,128)(2,1)S(1)} async-done(((bf16[4,2,1536]{2,1,0:T(2,128)(2,1)}), bf16[4,2,1536]{2,1,0:T(2,128)(2,1)S(1)}, u32[]{:S(2)}, u32[]{:S(2)}) %all-to-all-start.1) | async-done | bytes 24608 | tf_op jit(solution)/shard_map/all_to_all | solution.py:124
  314.6 4.5 %all-to-all-start = ((bf16[4,191,1536]{2,1,0:T(8,128)(2,1)}), bf16[4,191,1536]{2,1,0:T(8,128)(2,1)}, u32[]{:S(2)}, u32[]{:S(2)}) async-start(bf16[4,191,1536]{2,1,0:T(8,128)(2,1)} %select_select_fusion), calls=%async_computation | async-start | bytes 4718592 | tf_op jit(solution)/shard_map/all_to_all | solution.py:118
  319.8 0.7 convert.3
  320.4 50.4 %all-to-all-done = bf16[4,191,1536]{2,1,0:T(8,128)(2,1)} async-done(((bf16[4,191,1536]{2,1,0:T(8,128)(2,1)}), bf16[4,191,1536]{2,1,0:T(8,128)(2,1)}, u32[]{:S(2)}, u32[]{:S(2)}) %all-to-all-start) | async-done | bytes 2347040 | tf_op jit(solution)/shard_map/all_to_all | solution.py:118
  370.8 2.3 reshape.254
  373.1 2.2 gather_fusion.1
  375.3 1.2 bitcast_select_fusion
  (58 shorter events, 6.3 us)
Async XLA Ops:
  7.2 64.5 %all-gather.5.cloned.1.call-start = ((), (), s32[]{:S(2)}) async-start(), calls=%async_computation.2 | async-start | bytes 5898240 | tf_op jit(solution)/shard_map/all_gather | solution.py:40
  11.5 2.4 copy-start.5
  11.5 2.8 copy-start.7
  11.5 2.8 copy-start.8
  11.9 1.4 copy-start.1
  12.0 1.3 copy-start.2
  14.4 8.7 %copy-start = (pred[764,764]{0,1:T(8,128)(4,1)}, pred[764,764]{0,1:T(8,128)(4,1)S(1)}, u32[]{:S(2)}) copy-start(pred[764,764]{0,1:T(8,128)(4,1)S(1)} %broadcast_compare_fusion) | copy-start | bytes 1751092
  31.3 0.8 copy-start.3
  31.3 1.0 copy-start.6
  31.3 208.8 %all-gather.7.cloned.1.call-start = ((), (), s32[]{:S(2)}) async-start(), calls=%async_computation.3 | async-start | bytes 11796480 | tf_op jit(solution)/shard_map/all_gather | solution.py:43
  32.1 269.1 %all-reduce.3.cloned.1.call-start = ((), (), s32[]{:S(2)}) async-start(), calls=%async_computation.4 | async-start | bytes 196608
  265.8 5.8 %copy-start.9 = (u32[32]{0:T(128)S(1)}, u32[32]{0:T(128)}, u32[]{:S(2)}) copy-start(u32[32]{0:T(128)} %constant.81) | copy-start | bytes 388
  276.0 25.2 %copy-start.4 = (f32[3072]{0:T(1024)S(1)}, f32[3072]{0:T(1024)}, u32[]{:S(2)}) copy-start(f32[3072]{0:T(1024)} %param.14) | copy-start | bytes 36868
  304.4 10.2 %all-to-all-start.1 = ((bf16[4,2,1536]{2,1,0:T(2,128)(2,1)}), bf16[4,2,1536]{2,1,0:T(2,128)(2,1)S(1)}, u32[]{:S(2)}, u32[]{:S(2)}) async-start(bf16[4,2,1536]{2,1,0:T(2,128)(2,1)} %reshape.285), calls=%async_computation.1 | async-start | bytes 49152 | tf_op jit(solution)/shard_map/all_to_all | solution.py:124
  314.6 56.2 %all-to-all-start = ((bf16[4,191,1536]{2,1,0:T(8,128)(2,1)}), bf16[4,191,1536]{2,1,0:T(8,128)(2,1)}, u32[]{:S(2)}, u32[]{:S(2)}) async-start(bf16[4,191,1536]{2,1,0:T(8,128)(2,1)} %select_select_fusion), calls=%async_computation | async-start | bytes 4718592 | tf_op jit(solution)/shard_map/all_to_all | solution.py:118
Sparse Core Ops, SparseCore 0:
  31.4 40.2 all-gather.4
  73.3 166.7 all-gather.6
  271.7 29.4 all-reduce.2
where the time goes:
time: 384 us; the launch traced here: 383 us
  waiting for transfers between devices  285 us (74%)
  matrix products  34.4 us (9%)
  local copies, waits for them, and re-layouts  17.7 us (5%)
  between operations  14 us (4%)
  blocking collectives  13.3 us (3%)
  other arithmetic  9.38 us (2%)
  starting transfers between devices  9.2 us (2%)
    all_gather x1, waiting for transfers between devices, project(): lax.all_gather(out_weight, 'dp', axis=0, tiled=True)  168 us
    all_to_all x1, waiting for transfers between devices, on_device(): lax.all_to_all(send_mixed, 'dp', split_axis=0, concat_axis=0, tiled=True)  50.4 us
    all_gather x1, waiting for transfers between devices, project(): gathered = lax.all_gather(heads_local, 'mp', axis=1, tiled=True)  38.9 us
    unnamed x4, waiting for transfers between devices  23.6 us
    all_gather x1, blocking collectives, label_terms(): lax.all_gather(pooled[None], 'dp', axis=0, tiled=True)  13.3 us
    dot_general x1, matrix products, project(): jnp.dot(gathered, lax.all_gather(out_weight, 'dp', axis=0, tiled=True), p...  12 us
    dot_general x1, matrix products, attend(): jnp.einsum('qhd,khd->hqk', queries, key_rows, preferred_element_type=jnp....  8.66 us
    dot_general x1, matrix products, attend(): jnp.einsum('hqk,khd->qhd', weights, split_parts[:, 2], preferred_element_...  8.27 us
  transfers between devices with their start and end apart: 5, of which 5 were waited for; matrix products, arithmetic and copies ran while one was open for 3% of the time, Pallas kernels for 0%

commit v1 on v0

--- a/solution.py
+++ b/solution.py
@@ -3,9 +3,13 @@
 import jax
 import jax.numpy as jnp
 from jax import lax
+from jax.experimental import pallas as pl
+from jax.experimental.pallas import tpu as pltpu
 from jax.sharding import PartitionSpec as P
 
 TOK = 384
+CHUNKS = 2
+VMEM_BYTES = 48 * 1024 * 1024
 
 
 EPSILON = 1e-06
@@ -17,7 +21,320 @@
     return center * lax.rsqrt(spread + EPSILON) * norm_gain
 
 
-def attend(qkv_rows, seg_rows, query_gain, key_gain):
+def shifted(count, by):
+    return [(i, (i + by) % count) for i in range(count)]
+
+
+def crossed(count, by):
+    return [(i, i ^ by) for i in range(count)]
+
+
+def dot32(left, right):
+    return jnp.dot(left, right, preferred_element_type=jnp.float32)
+
+
+def at(values, index, axis=0):
+    return lax.dynamic_index_in_dim(values, index, axis, keepdims=False)
+
+
+def image_for(counts_ref, plan_ref, row, dest, images):
+    image, first, size, before = 0, 0, 0, 0
+    for j in range(images):
+        count = counts_ref[row, j]
+        hit = plan_ref[row, j] == dest
+        image = jnp.where(hit, j, image)
+        first = jnp.where(hit, before, first)
+        size = jnp.where(hit, count, size)
+        before = before + count
+    return image, first, size
+
+
+def attend_kernel(
+    rows,
+    span,
+    place_ref,
+    counts_ref,
+    plan_ref,
+    qkv_ref,
+    resid_ref,
+    query_gain_ref,
+    key_gain_ref,
+    *rest,
+):
+    heads_ref, sent_ref, head_means_ref, resid_means_ref, means_ref = rest[-5:]
+    k = pl.program_id(0)
+    my_row = place_ref[0]
+    image, first, size = image_for(
+        counts_ref, plan_ref, my_row, lax.rem(my_row + k, rows), rows
+    )
+    window = span + 16
+    begin = pl.multiple_of(first // 16 * 16, 16)
+    shift = first - begin
+    taken = lax.broadcasted_iota(jnp.int32, (span, window), 0)
+    slot = lax.broadcasted_iota(jnp.int32, (span, window), 1)
+    select = ((slot - taken == shift) & (taken < size)).astype(jnp.float32).astype(jnp.bfloat16)
+    count = size.astype(jnp.float32)
+    resid = dot32(select, resid_ref[pl.ds(begin, window), :])
+    sent_ref[...] = resid.astype(jnp.bfloat16)
+    here = lax.broadcasted_iota(jnp.int32, (rows, 1), 0) == image
+    resid_mean = jnp.sum(resid, axis=0, keepdims=True) / count
+    resid_means_ref[...] = jnp.where(here, resid_mean, resid_means_ref[...])
+    queries = dot32(select, qkv_ref[0, pl.ds(begin, window), :])
+    keys = dot32(select, qkv_ref[1, pl.ds(begin, window), :])
+    values = dot32(select, qkv_ref[2, pl.ds(begin, window), :]).astype(jnp.bfloat16)
+    head_width = query_gain_ref.shape[1]
+    inside = lax.broadcasted_iota(jnp.int32, (span, span), 1) < size
+    kept = lax.broadcasted_iota(jnp.int32, (span, 1), 0) < size
+    for h in range(heads_ref.shape[1] // head_width):
+        columns = slice(h * head_width, (h + 1) * head_width)
+        query = head_norm(queries[:, columns], query_gain_ref[...]).astype(jnp.bfloat16)
+        key = head_norm(keys[:, columns], key_gain_ref[...]).astype(jnp.bfloat16)
+        scores = lax.dot_general(
+            query, key, (((1,), (1,)), ((), ())), preferred_element_type=jnp.float32
+        ) * (1.0 / math.sqrt(head_width))
+        raised = jnp.where(inside, jnp.exp(scores), 0.0)
+        scale = jnp.where(kept, 1.0 / jnp.sum(raised, axis=-1, keepdims=True), 0.0)
+        weights = (raised * scale).astype(jnp.bfloat16)
+        head = dot32(weights, values[:, columns]).astype(jnp.bfloat16)
+        heads_ref[:, columns] = head
+        head_mean = jnp.sum(head.astype(jnp.float32), axis=0, keepdims=True) / count
+        means_ref[:, columns] = jnp.where(here, head_mean, means_ref[:, columns])
+
+    @pl.when(k == rows - 1)
+    def _():
+        head_means_ref[...] = means_ref[...].astype(jnp.bfloat16)
+
+
+def attend(place, counts, plan, qkv, resid, query_gain, key_gain, span, after):
+    rows = counts.shape[0]
+    local, features = qkv.shape[2], resid.shape[1]
+    whole = pl.BlockSpec(memory_space=pltpu.VMEM)
+    fixed = lambda shape: pl.BlockSpec(shape, lambda k, *_: (0,) * len(shape))
+    return pl.pallas_call(
+        lambda *refs: attend_kernel(rows, span, *refs),
+        grid_spec=pltpu.PrefetchScalarGridSpec(
+            num_scalar_prefetch=3,
+            grid=(rows,),
+            in_specs=[fixed(x.shape) for x in (qkv, resid, query_gain, key_gain)]
+            + [pl.BlockSpec(memory_space=pl.ANY)] * len(after),
+            out_specs=[
+                pl.BlockSpec((span, local), lambda k, *_: (k, 0)),
+                pl.BlockSpec((span, features), lambda k, *_: (k, 0)),
+                fixed((rows, local)),
+                fixed((rows, features)),
+            ],
+            scratch_shapes=[pltpu.VMEM((rows, local), jnp.float32)],
+        ),
+        out_shape=[
+            jax.ShapeDtypeStruct((rows * span, local), jnp.bfloat16),
+            jax.ShapeDtypeStruct((rows * span, features), jnp.bfloat16),
+            jax.ShapeDtypeStruct((rows, local), jnp.bfloat16),
+            jax.ShapeDtypeStruct((rows, features), jnp.float32),
+        ],
+        compiler_params=pltpu.CompilerParams(vmem_limit_bytes=VMEM_BYTES),
+        cost_estimate=pl.CostEstimate(
+            flops=10_000_000_000, bytes_accessed=12_000_000, transcendentals=1_000_000
+        ),
+        name="attend",
+    )(place, counts, plan, qkv, resid, query_gain, key_gain, *after)
+
+
+def project_kernel(rows, place_ref, *refs):
+    head_refs = refs[:rows]
+    own_ref = refs[rows]
+    piece_refs = refs[rows + 1 : rows + 1 + 2 * (rows - 1)]
+    resid_ref = refs[3 * rows - 1]
+    out_refs = refs[3 * rows : 4 * rows]
+    held_ref, sems = refs[4 * rows :]
+    my_row, my_part, my_group = place_ref[0], place_ref[1], place_ref[2]
+    half = held_ref.shape[2]
+
+    @pl.when(pl.program_id(0) == 0)
+    def _():
+        copies = [
+            pltpu.make_async_copy(
+                head_refs[x].at[:, s * half : (s + 1) * half],
+                held_ref.at[2 * (x ^ my_part) + s],
+                sems.at[x, s],
+            )
+            for x in range(rows)
+            for s in range(2)
+        ]
+        for copy in copies:
+            copy.start()
+        for copy in copies:
+            copy.wait()
+
+    total = resid_ref[...].astype(jnp.float32)
+    for s in range(2):
+        total = total + dot32(held_ref[2 * my_row + s], own_ref[s * half : (s + 1) * half, :])
+    for step in range(1, rows):
+        row = lax.rem(my_row - step + rows, rows)
+        for which in range(2):
+            piece_ref = piece_refs[2 * (step - 1) + which]
+            total = total + dot32(held_ref[2 * row + (my_group ^ which)], piece_ref[...])
+    span = out_refs[0].shape[0]
+    for k in range(rows):
+        out_refs[k][...] = total[k * span : (k + 1) * span].astype(jnp.bfloat16)
+
+
+def project(place, heads, out_weight, pieces, resid, chunk, width, span):
+    rows = len(heads)
+    length, depth = heads[0].shape
+    half = depth // 2
+    tile = 256
+    tiles = width // tile
+    first = chunk * tiles
+    return pl.pallas_call(
+        lambda *refs: project_kernel(rows, *refs),
+        grid_spec=pltpu.PrefetchScalarGridSpec(
+            num_scalar_prefetch=1,
+            grid=(tiles,),
+            in_specs=[pl.BlockSpec(memory_space=pl.ANY)] * rows
+            + [pl.BlockSpec((depth, tile), lambda i, *_: (0, first + i))]
+            + [pl.BlockSpec((half, tile), lambda i, *_: (0, i))] * len(pieces)
+            + [pl.BlockSpec((length, tile), lambda i, *_: (0, first + i))],
+            out_specs=[pl.BlockSpec((span, tile), lambda i, *_: (0, i))] * rows,
+            scratch_shapes=[
+                pltpu.VMEM((2 * rows, length, half), jnp.bfloat16),
+                pltpu.SemaphoreType.DMA((rows, 2)),
+            ],
+        ),
+        out_shape=[jax.ShapeDtypeStruct((span, width), jnp.bfloat16)] * rows,
+        compiler_params=pltpu.CompilerParams(vmem_limit_bytes=VMEM_BYTES),
+        cost_estimate=pl.CostEstimate(
+            flops=2 * length * depth * rows * width, bytes_accessed=12_000_000, transcendentals=0
+        ),
+        name="project",
+    )(place, *heads, out_weight, *pieces, resid)
+
+
+def settle_kernel(rows, place_ref, counts_ref, plan_ref, *refs):
+    block_refs = refs[:rows]
+    out_ref = refs[-1]
+    my_row = place_ref[0]
+    tokens, span = out_ref.shape[0], block_refs[0].shape[0]
+    token = lax.broadcasted_iota(jnp.int32, (tokens, span), 0)
+    slot = lax.broadcasted_iota(jnp.int32, (tokens, span), 1)
+    sizes = [image_for(counts_ref, plan_ref, r, my_row, rows)[2] for r in range(rows)]
+    total = None
+    for k in range(rows):
+        source = lax.rem(my_row - k + rows, rows)
+        start, size = 0, 0
+        for r in range(rows):
+            start = start + jnp.where(r < source, sizes[r], 0)
+            size = jnp.where(r == source, sizes[r], size)
+        select = ((token - slot == start) & (slot < size)).astype(jnp.float32).astype(jnp.bfloat16)
+        term = dot32(select, block_refs[k][...])
+        total = term if total is None else total + term
+    out_ref[...] = total.astype(jnp.bfloat16)
+
+
+def settle(place, counts, plan, blocks, chunk, features, earlier):
+    rows = len(blocks)
+    span, width = blocks[0].shape
+    tile = 256
+    tiles = width // tile
+    first = chunk * tiles
+    more = [] if earlier is None else [earlier]
+    return pl.pallas_call(
+        lambda *refs: settle_kernel(rows, *refs),
+        grid_spec=pltpu.PrefetchScalarGridSpec(
+            num_scalar_prefetch=3,
+            grid=(tiles,),
+            in_specs=[pl.BlockSpec((span, tile), lambda i, *_: (0, i))] * rows
+            + [pl.BlockSpec(memory_space=pl.ANY)] * len(more),
+            out_specs=pl.BlockSpec((TOK, tile), lambda i, *_: (0, first + i)),
+        ),
+        out_shape=jax.ShapeDtypeStruct((TOK, features), jnp.bfloat16),
+        input_output_aliases={3 + rows: 0} if more else {},
+        compiler_params=pltpu.CompilerParams(vmem_limit_bytes=VMEM_BYTES),
+        cost_estimate=pl.CostEstimate(
+            flops=2 * TOK * rows * span * width, bytes_accessed=2_000_000, transcendentals=0
+        ),
+        name="settle",
+    )(place, counts, plan, *blocks, *more)
+
+
+def on_device_rings(
+    qkv_home,
+    resid_home,
+    out_weight,
+    label_weight,
+    label_bias,
+    query_gain,
+    key_gain,
+    patch_counts,
+    move_plan,
+    segment_ids,
+):
+    rows = lax.axis_size("dp")
+    parts = lax.axis_size("mp")
+    sharers = lax.axis_size("groups")
+    my_row = lax.axis_index("dp")
+    my_part = lax.axis_index("mp")
+    my_group = lax.axis_index("groups")
+    slots = segment_ids.shape[1]
+    span = -(-(slots // rows) // 16) * 16
+    padded = -(-slots // 16) * 16 + span
+    depth, features = out_weight.shape
+    half = depth // sharers
+    width = features // CHUNKS
+    image_ids = jnp.arange(rows, dtype=jnp.int32)
+    place = jnp.stack([my_row, my_part, my_group]).astype(jnp.int32)
+
+    mine = lax.dynamic_slice_in_dim(out_weight, my_group * half, half, 0)
+    moving = [mine[:, c * width : (c + 1) * width] for c in range(CHUNKS)]
+    pieces = [[] for _ in range(CHUNKS)]
+    for _ in range(1, rows):
+        for c in range(CHUNKS):
+            moving[c] = lax.ppermute(moving[c], "dp", shifted(rows, 1))
+            other = lax.ppermute(moving[c], "groups", crossed(sharers, 1))
+            pieces[c] += [moving[c], other]
+
+    qkv = jnp.pad(jnp.transpose(qkv_home[0], (1, 0, 2)), ((0, 0), (0, padded - slots), (0, 0)))
+    heads, resid, head_means, resid_means = attend(
+        place,
+        patch_counts,
+        move_plan,
+        qkv,
+        jnp.pad(resid_home[0], ((0, padded - slots), (0, 0))),
+        query_gain[None],
+        key_gain[None],
+        span,
+        [pieces[0][0]],
+    )
+    across = lax.ppermute(heads, "mp", crossed(parts, 2))
+    beside = lax.ppermute(heads, "mp", crossed(parts, 1))
+    beyond = lax.ppermute(across, "mp", crossed(parts, 1))
+
+    got = lax.all_gather(head_means, ("dp", "mp"), axis=0)
+    got = at(got.reshape(rows, parts, rows, depth), my_row, 1).reshape(rows * rows, depth)
+    share = dot32(got, out_weight).reshape(rows, rows, features)
+    share = share + jnp.where((image_ids == my_row)[:, None, None], resid_means[None], 0.0)
+    share = share.reshape(rows * rows, features).astype(jnp.bfloat16)
+    pooled = jnp.sum(lax.all_gather(share, "dp", axis=0).astype(jnp.float32), axis=0)
+    terms = dot32(pooled.astype(jnp.bfloat16), label_weight)
+    classes = label_weight.shape[1]
+    terms = terms.reshape(rows, rows, classes).astype(jnp.bfloat16)
+    terms = lax.all_to_all(terms, "mp", split_axis=1, concat_axis=1, tiled=True)
+    logits = jnp.sum(terms.astype(jnp.float32), axis=1)
+    probs = jax.nn.sigmoid(logits + label_bias[None, :]).astype(jnp.bfloat16)
+    labels = lax.all_to_all(probs, "dp", split_axis=0, concat_axis=0, tiled=True)
+    labels = labels.reshape(1, 1, rows * classes).astype(jnp.float32)
+
+    mixed = None
+    for c in range(CHUNKS):
+        blocks = project(
+            place, [heads, beside, across, beyond], out_weight, pieces[c], resid, c, width, span
+        )
+        arrived = [blocks[0]]
+        for k in range(1, rows):
+            arrived.append(lax.ppermute(blocks[k], "dp", shifted(rows, k)))
+        mixed = settle(place, patch_counts, move_plan, arrived, c, features, mixed)
+    return (mixed[None], labels)
+
+def attend_home(qkv_rows, seg_rows, query_gain, key_gain):
     length = qkv_rows.shape[0]
     head_width = query_gain.shape[0]
     head_count = qkv_rows.shape[2] // head_width
@@ -36,7 +353,7 @@
     return head_out.reshape(length, head_count * head_width).astype(jnp.bfloat16)
 
 
-def project(heads_local, resid_rows, out_weight):
+def project_home(heads_local, resid_rows, out_weight):
     gathered = lax.all_gather(heads_local, "mp", axis=1, tiled=True)
     running = resid_rows.astype(jnp.float32) + jnp.dot(
         gathered,
@@ -108,8 +425,8 @@
     arrive_index = (
         source * pair_slots + slot_grid[:, 0] - jnp.sum(chosen * arrive_starts[None, :], axis=1)
     )
-    home_mixed = project(
-        attend(qkv_home[0], segment_ids[0], query_gain, key_gain), resid_home[0], out_weight
+    home_mixed = project_home(
+        attend_home(qkv_home[0], segment_ids[0], query_gain, key_gain), resid_home[0], out_weight
     )
     count_row = lax.dynamic_index_in_dim(patch_counts, my_index, 0, keepdims=False)
     pooled = pool(home_mixed, segment_ids[0], count_row)
@@ -126,10 +443,11 @@
     ).astype(class_probs.dtype)
     return (mixed[None], labels)
 
-
 def solution(mesh):
+    rows, parts, sharers = (mesh.shape[name] for name in ("dp", "mp", "groups"))
+    small = rows == parts == 4 and sharers == 2
     return jax.shard_map(
-        on_device,
+        on_device_rings if small else on_device,
         mesh=mesh,
         in_specs=(
             P(("groups", "dp"), None, None, "mp"),

time: 384 us -> 227 us (0.59)
  waiting for transfers between devices: 285 us -> 59.2 us
  blocking collectives: 13.3 us -> 84.6 us
  Pallas kernels: 0 us -> 36.5 us
  matrix products: 34.4 us -> 7.18 us
  starting transfers between devices: 9.2 us -> 23.8 us
  between operations: 14 us -> 0.84 us
  other arithmetic: 9.38 us -> 1.54 us
  local copies, waits for them, and re-layouts: 17.7 us -> 12.4 us
    all_gather x2 -> x0, waiting for transfers between devices: 207 us -> none  [the longest x1 168 us: project(): lax.all_gather(out_weight, 'dp', axis=0, tiled=True)]
    ppermute x0 -> x21, waiting for transfers between devices: none -> 59.2 us  [the longest x6 33.6 us: on_device_rings(): moving[c] = lax.ppermute(moving[c], 'dp', shifted(rows, 1))]
    all_to_all x2 -> x0, waiting for transfers between devices: 54.3 us -> none  [the longest x1 50.4 us: on_device(): lax.all_to_all(send_mixed, 'dp', split_axis=0, concat_axis=0, tiled=True)]
    all_gather x1 -> x2, blocking collectives: 13.3 us -> 50.6 us  [the longest x1 36.7 us: on_device_rings(): got = lax.all_gather(head_means, ('dp', 'mp'), axis=0)]
    pallas_call x0 -> x5, Pallas kernels: none -> 36.5 us  [the longest x2 20.7 us: project(): pl.pallas_call(lambda *refs: project_kernel(rows, *refs), grid_spec=pltpu...]
    all_to_all x0 -> x2, blocking collectives: none -> 33.9 us  [the longest x1 27.3 us: on_device_rings(): lax.all_to_all(probs, 'dp', split_axis=0, concat_axis=0, tiled=True)]
    dot_general x5 -> x2, matrix products: 34.4 us -> 7.18 us  [dot32(): return jnp.dot(left, right, preferred_element_type=jnp.float32)]
    ppermute x0 -> x21, starting transfers between devices: none -> 23.8 us  [the longest x6 8.87 us: on_device_rings(): arrived.append(lax.ppermute(blocks[k], 'dp', shifted(rows, k)))]
  transfers between devices with their start and end apart: 5 -> 21, of which waited for: 5 -> 4; matrix products, arithmetic and copies ran while one was open for 3% -> 7% of each run, Pallas kernels for 0% -> 15%
where the time goes in v1:
time: 227 us; the launch traced here: 226 us
  blocking collectives  84.6 us (37%)
  waiting for transfers between devices  59.2 us (26%)
  Pallas kernels  36.5 us (16%)
  starting transfers between devices  23.8 us (10%)
  local copies, waits for them, and re-layouts  12.4 us (5%)
  matrix products  7.18 us (3%)
    all_gather x1, blocking collectives, on_device_rings(): got = lax.all_gather(head_means, ('dp', 'mp'), axis=0)  36.7 us
    ppermute x6, waiting for transfers between devices, on_device_rings(): moving[c] = lax.ppermute(moving[c], 'dp', shifted(rows, 1))  33.6 us
    all_to_all x1, blocking collectives, on_device_rings(): lax.all_to_all(probs, 'dp', split_axis=0, concat_axis=0, tiled=True)  27.3 us
    ppermute x6, waiting for transfers between devices, on_device_rings(): other = lax.ppermute(moving[c], 'groups', crossed(sharers, 1))  25.6 us
    pallas_call x2, Pallas kernels, project(): pl.pallas_call(lambda *refs: project_kernel(rows, *refs), grid_spec=pltpu...  20.7 us
    all_gather x1, blocking collectives, on_device_rings(): lax.all_gather(share, 'dp', axis=0).astype(jnp.float32)  13.9 us
    pallas_call x1, Pallas kernels, attend(): pl.pallas_call(lambda *refs: attend_kernel(rows, span, *refs), grid_spec=...  10.2 us
    ppermute x6, starting transfers between devices, on_device_rings(): arrived.append(lax.ppermute(blocks[k], 'dp', shifted(rows, k)))  8.87 us
  transfers between devices with their start and end apart: 21, of which 4 were waited for; matrix products, arithmetic and copies ran while one was open for 7% of the time, Pallas kernels for 15%

profile of v1, /device:TPU:0, one launch (start us, length us, event | category | flops | bytes accessed | tf_op | source)
XLA Modules:
  0.0 226.2 jit_solution(7259230720809016005)
XLA Ops:
  0.6 2.1 fusion.19
  2.8 3.0 %collective-permute-start = (bf16[384,768]{1,0:T(8,128)(2,1)S(1)}, bf16[384,768]{1,0:T(8,128)(2,1)S(1)}, u32[]{:S(2)}, u32[]{:S(2)}) collective-permute-start(bf16[384,768]{1,0:T(8,128)(2,1)S(1)} %get-tuple-element.27), channel_id=1, source_target_pairs={{0,4},{4,8},{8,12},{12,0},{1,5},{5,9},{9,13},{13,1},{2,6},{6,10},{... | collective-permute-start | bytes 1769480 | tf_op jit(solution)/shard_map/ppermute | solution.py:291
  5.8 1.6 collective-permute-start.4
  7.4 4.5 %pad.8.refs_3_ = bf16[3,960,768]{2,1,0:T(8,128)(2,1)} pad(bf16[3,764,768]{2,1,0:T(8,128)(2,1)} %bitcast.48, bf16[]{:T(256)} %constant.24.clone.1), padding=0_0x0_196x0_0 | pad | bytes 7944194 | tf_op jit(solution)/shard_map/jit(_pad)/pad | solution.py:295
  11.9 1.8 pad.9.refs_4_
  13.8 8.2 %collective-permute-done.refs_7_.refs_6_ = bf16[384,768]{1,0:T(8,128)(2,1)S(1)} collective-permute-done((bf16[384,768]{1,0:T(8,128)(2,1)S(1)}, bf16[384,768]{1,0:T(8,128)(2,1)S(1)}, u32[]{:S(2)}, u32[]{:S(2)}) %collective-permute-start) | collective-permute-done | bytes 589856 | tf_op jit(solution)/shard_map/ppermute | solution.py:291
  22.0 10.2 %attend.1 = (bf16[768,768]{1,0:T(8,128)(2,1)S(1)}, bf16[768,1536]{1,0:T(8,128)(2,1)S(1)}, bf16[4,768]{1,0:T(4,128)(2,1)S(1)}, f32[4,1536]{1,0:T(4,128)S(1)}) custom-call(s32[3]{0:T(128)S(1)} %pad_add_fusion.refs_0_, s32[4,4]{1,0:T(4,128)S(1)} %copy-done, s32[4,4]{1,0:T(4,128)S(1)} %copy-done.1, bf16[3,960,768]{2,1,0:T(8,128)(2,1)} %pad.8.refs_3_, ...), custom_call_target="tpu_custom_call" | custom-call | flops 10000000000 | bytes 12000000 | tf_op jit(solution)/shard_map/attend/pallas_call | solution.py:113
  33.6 1.7 collective-permute-start.2
  38.3 15.0 %collective-permute-done.14.refs_8_ = bf16[384,768]{1,0:T(8,128)(2,1)S(1)} collective-permute-done((bf16[384,768]{1,0:T(8,128)(2,1)S(1)}, bf16[384,768]{1,0:T(8,128)(2,1)S(1)}, u32[]{:S(2)}, u32[]{:S(2)}) %collective-permute-start.14) | collective-permute-done | bytes 589856 | tf_op jit(solution)/shard_map/ppermute | solution.py:291
  55.7 10.3 %collective-permute-done.6.refs_8_ = bf16[384,768]{1,0:T(8,128)(2,1)} collective-permute-done((bf16[384,768]{1,0:T(8,128)(2,1)S(1)}, bf16[384,768]{1,0:T(8,128)(2,1)}, u32[]{:S(2)}, u32[]{:S(2)}) %collective-permute-start.6) | collective-permute-done | bytes 589856 | tf_op jit(solution)/shard_map/ppermute | solution.py:291
  66.1 36.7 %all-gather.1 = bf16[16,4,768]{2,1,0:T(4,128)(2,1)S(1)} all-gather(bf16[1,4,768]{2,1,0:T(4,128)(2,1)S(1)} %bitcast.44), channel_id=2, replica_groups=mesh['groups'=2,'dp'=4,'mp'=4] {'dp','mp'}, dimensions={0}, use_global_device_ids=true | all-gather | bytes 104448 | tf_op jit(solution)/shard_map/all_gather | solution.py:311
  102.9 2.1 add_convert_fusion
  105.0 13.9 %all_gather.12 = bf16[4,16,1536]{2,1,0:T(8,128)(2,1)S(1)} all-gather(bf16[1,16,1536]{2,1,0:T(8,128)(2,1)S(1)} %convert_element_type.50), channel_id=1, replica_groups=mesh['groups'=2,'dp'=4,'mp'=4] {'dp'}, dimensions={0}, use_global_device_ids=true | all-gather | bytes 245760 | tf_op jit(solution)/shard_map/all_gather | solution.py:316
  119.0 1.6 collective-permute-start.5
  123.1 5.1 %fusion.2 = bf16[4,4,3072]{2,1,0:T(4,128)(2,1)S(1)} fusion(bf16[4,4,1536]{2,1,0:T(4,128)(2,1)S(1)} %dot_general.12, bf16[1536,3072]{1,0:T(8,128)(2,1)} %param.13), kind=kOutput, calls=%fused_computation.2 | convolution fusion | flops 151044096 | bytes 9584640 | tf_op jit(solution)/shard_map/dot_general | solution.py:33
  128.3 6.7 %all_to_all.11 = bf16[4,4,3072]{2,0,1:T(4,128)(2,1)S(1)} all-to-all(bf16[4,4,3072]{2,0,1:T(4,128)(2,1)S(1)} %copy.15), channel_id=1, replica_groups=mesh['groups'=2,'dp'=4,'mp'=4] {'mp'}, dimensions={1} | all-to-all | bytes 196608 | tf_op jit(solution)/shard_map/all_to_all | solution.py:320
  135.0 25.6 %collective-permute-done.17.refs_11_ = bf16[384,768]{1,0:T(8,128)(2,1)S(1)} collective-permute-done((bf16[384,768]{1,0:T(8,128)(2,1)}, bf16[384,768]{1,0:T(8,128)(2,1)S(1)}, u32[]{:S(2)}, u32[]{:S(2)}) %collective-permute-start.17) | collective-permute-done | bytes 589856 | tf_op jit(solution)/shard_map/ppermute | solution.py:292
  161.7 10.3 %project.3 = (bf16[192,768]{1,0:T(8,128)(2,1)S(1)}, bf16[192,768]{1,0:T(8,128)(2,1)S(1)}, bf16[192,768]{1,0:T(8,128)(2,1)}, bf16[192,768]{1,0:T(8,128)(2,1)}) custom-call(s32[3]{0:T(128)S(1)} %pad_add_fusion.refs_0_, bf16[768,768]{1,0:T(8,128)(2,1)S(1)} %get-tuple-element.14.refs_1_, bf16[768,768]{1,0:T(8,128)(2,1)} %collective-permute-done.1.refs_2_, ...), custom_call_target="tpu_custom_call" | custom-call | flops 3623878656 | bytes 12000000 | tf_op jit(solution)/shard_map/project/pallas_call | solution.py:188
  172.7 3.2 %collective-permute-start.20 = (bf16[192,768]{1,0:T(8,128)(2,1)}, bf16[192,768]{1,0:T(8,128)(2,1)S(1)}, u32[]{:S(2)}, u32[]{:S(2)}) collective-permute-start(bf16[192,768]{1,0:T(8,128)(2,1)} %get-tuple-element.23), channel_id=1, source_target_pairs={{0,12},{4,0},{8,4},{12,8},{1,13},{5,1},{9,5},{13,9},{2,14},{6,2},{... | collective-permute-start | bytes 884744 | tf_op jit(solution)/shard_map/ppermute | solution.py:333
  175.9 10.4 %project.2 = (bf16[192,768]{1,0:T(8,128)(2,1)S(1)}, bf16[192,768]{1,0:T(8,128)(2,1)}, bf16[192,768]{1,0:T(8,128)(2,1)}, bf16[192,768]{1,0:T(8,128)(2,1)}) custom-call(s32[3]{0:T(128)S(1)} %pad_add_fusion.refs_0_, bf16[768,768]{1,0:T(8,128)(2,1)S(1)} %get-tuple-element.14.refs_1_, bf16[768,768]{1,0:T(8,128)(2,1)} %collective-permute-done.1.refs_2_, ...), custom_call_target="tpu_custom_call" | custom-call | flops 3623878656 | bytes 12000000 | tf_op jit(solution)/shard_map/project/pallas_call | solution.py:188
  188.4 2.8 %collective-permute-start.12 = (bf16[192,768]{1,0:T(8,128)(2,1)}, bf16[192,768]{1,0:T(8,128)(2,1)S(1)}, u32[]{:S(2)}, u32[]{:S(2)}) collective-permute-start(bf16[192,768]{1,0:T(8,128)(2,1)} %get-tuple-element.19), channel_id=1, source_target_pairs={{0,12},{4,0},{8,4},{12,8},{1,13},{5,1},{9,5},{13,9},{2,14},{6,2},{... | collective-permute-start | bytes 884744 | tf_op jit(solution)/shard_map/ppermute | solution.py:333
  192.5 27.3 %all_to_all.12 = bf16[4,2,1536]{2,1,0:T(2,128)(2,1)S(1)} all-to-all(bf16[4,2,1536]{2,1,0:T(2,128)(2,1)S(1)} %reshape.98), channel_id=1, replica_groups=mesh['groups'=2,'dp'=4,'mp'=4] {'dp'}, dimensions={0} | all-to-all | bytes 49152 | tf_op jit(solution)/shard_map/all_to_all | solution.py:323
  220.5 2.8 %settle.2.refs_7_ = bf16[384,1536]{1,0:T(8,128)(2,1)} custom-call(s32[3]{0:T(128)S(1)} %pad_add_fusion.refs_0_, s32[4,4]{1,0:T(4,128)S(1)} %copy-done, s32[4,4]{1,0:T(4,128)S(1)} %copy-done.1, bf16[192,768]{1,0:T(8,128)(2,1)S(1)} %get-tuple-element.20.refs_3_, bf16[192,768]{1,0:T(8,128)(2,1)S(1)} %collective-permute-done.18.refs_4_, ...), custom_call_target="tpu_custom_call" | custom-call | flops 452984832 | bytes 2000000 | tf_op jit(solution)/shard_map/settle/pallas_call | solution.py:240
  223.3 2.9 %settle.3 = bf16[384,1536]{1,0:T(8,128)(2,1)} custom-call(s32[3]{0:T(128)S(1)} %pad_add_fusion.refs_0_, s32[4,4]{1,0:T(4,128)S(1)} %copy-done, s32[4,4]{1,0:T(4,128)S(1)} %copy-done.1, bf16[192,768]{1,0:T(8,128)(2,1)S(1)} %get-tuple-element.16.refs_3_, bf16[192,768]{1,0:T(8,128)(2,1)S(1)} %collective-permute-done.10.refs_4_, ...), custom_call_target="tpu_custom_call", output_to_operand_aliasing={{}: (7, {})} | custom-call | flops 452984832 | bytes 2000000 | tf_op jit(solution)/shard_map/settle/pallas_call | solution.py:240
  (67 shorter events, 15.4 us)
Async XLA Ops:
  2.8 19.2 %collective-permute-start = (bf16[384,768]{1,0:T(8,128)(2,1)S(1)}, bf16[384,768]{1,0:T(8,128)(2,1)S(1)}, u32[]{:S(2)}, u32[]{:S(2)}) collective-permute-start(bf16[384,768]{1,0:T(8,128)(2,1)S(1)} %get-tuple-element.27), channel_id=1, source_target_pairs={{0,4},{4,8},{8,12},{12,0},{1,5},{5,9},{9,13},{13,1},{2,6},{6,10},{... | collective-permute-start | bytes 1769480 | tf_op jit(solution)/shard_map/ppermute | solution.py:291
  5.8 31.1 %collective-permute-start.4 = (bf16[384,768]{1,0:T(8,128)(2,1)}, bf16[384,768]{1,0:T(8,128)(2,1)S(1)}, u32[]{:S(2)}, u32[]{:S(2)}) collective-permute-start(bf16[384,768]{1,0:T(8,128)(2,1)} %get-tuple-element.26), channel_id=1, source_target_pairs={{0,4},{4,8},{8,12},{12,0},{1,5},{5,9},{9,13},{13,1},{2,6},{6,10},{... | collective-permute-start | bytes 1769480 | tf_op jit(solution)/shard_map/ppermute | solution.py:291
  33.6 32.4 %collective-permute-start.2 = (bf16[768,768]{1,0:T(8,128)(2,1)S(1)}, bf16[768,768]{1,0:T(8,128)(2,1)}, u32[]{:S(2)}, u32[]{:S(2)}) collective-permute-start(bf16[768,768]{1,0:T(8,128)(2,1)S(1)} %get-tuple-element.14.refs_1_), channel_id=1, source_target_pairs={{0,2},{1,3},{2,0},{3,1},{4,6},{5,7},{6,4},{7,5},{8,10},{9,11},{10,... | collective-permute-start | bytes 3538952 | tf_op jit(solution)/shard_map/ppermute | solution.py:307
  35.4 83.6 %collective-permute-start.1 = (bf16[768,768]{1,0:T(8,128)(2,1)S(1)}, bf16[768,768]{1,0:T(8,128)(2,1)}, u32[]{:S(2)}, u32[]{:S(2)}) collective-permute-start(bf16[768,768]{1,0:T(8,128)(2,1)S(1)} %get-tuple-element.14.refs_1_), channel_id=1, source_target_pairs={{0,1},{1,0},{2,3},{3,2},{4,5},{5,4},{6,7},{7,6},{8,9},{9,8},{10,11... | collective-permute-start | bytes 3538952 | tf_op jit(solution)/shard_map/ppermute | solution.py:308
  35.4 17.9 %collective-permute-start.14 = (bf16[384,768]{1,0:T(8,128)(2,1)S(1)}, bf16[384,768]{1,0:T(8,128)(2,1)S(1)}, u32[]{:S(2)}, u32[]{:S(2)}) collective-permute-start(bf16[384,768]{1,0:T(8,128)(2,1)S(1)} %collective-permute-done.refs_7_.refs_6_), channel_id=1, source_target_pairs={{0,4},{4,8},{8,12},{12,0},{1,5},{5,9},{9,13},{13,1},{2,6},{6,10},{... | collective-permute-start | bytes 1769480 | tf_op jit(solution)/shard_map/ppermute | solution.py:291
  35.4 17.9 %collective-permute-start.13 = (bf16[384,768]{1,0:T(8,128)(2,1)S(1)}, bf16[384,768]{1,0:T(8,128)(2,1)S(1)}, u32[]{:S(2)}, u32[]{:S(2)}) collective-permute-start(bf16[384,768]{1,0:T(8,128)(2,1)S(1)} %collective-permute-done.refs_7_.refs_6_), channel_id=1, source_target_pairs={{0,16},{16,0},{1,17},{17,1},{2,18},{18,2},{3,19},{19,3},{4,20},{20... | collective-permute-start | bytes 1769480 | tf_op jit(solution)/shard_map/ppermute | solution.py:292
  36.9 29.1 %collective-permute-start.6 = (bf16[384,768]{1,0:T(8,128)(2,1)S(1)}, bf16[384,768]{1,0:T(8,128)(2,1)}, u32[]{:S(2)}, u32[]{:S(2)}) collective-permute-start(bf16[384,768]{1,0:T(8,128)(2,1)S(1)} %collective-permute-done.4.refs_6_), channel_id=1, source_target_pairs={{0,4},{4,8},{8,12},{12,0},{1,5},{5,9},{9,13},{13,1},{2,6},{6,10},{... | collective-permute-start | bytes 1769480 | tf_op jit(solution)/shard_map/ppermute | solution.py:291
  53.3 74.9 %copy-start.2 = (bf16[384,768]{1,0:T(8,128)(2,1)}, bf16[384,768]{1,0:T(8,128)(2,1)S(1)}, u32[]{:S(2)}) copy-start(bf16[384,768]{1,0:T(8,128)(2,1)S(1)} %collective-permute-done.14.refs_8_) | copy-start | bytes 1769476
  53.3 67.3 %collective-permute-start.16 = (bf16[384,768]{1,0:T(8,128)(2,1)S(1)}, bf16[384,768]{1,0:T(8,128)(2,1)}, u32[]{:S(2)}, u32[]{:S(2)}) collective-permute-start(bf16[384,768]{1,0:T(8,128)(2,1)S(1)} %collective-permute-done.14.refs_8_), channel_id=1, source_target_pairs={{0,4},{4,8},{8,12},{12,0},{1,5},{5,9},{9,13},{13,1},{2,6},{6,10},{... | collective-permute-start | bytes 1769480 | tf_op jit(solution)/shard_map/ppermute | solution.py:291
  54.1 66.9 %collective-permute-start.15 = (bf16[384,768]{1,0:T(8,128)(2,1)S(1)}, bf16[384,768]{1,0:T(8,128)(2,1)}, u32[]{:S(2)}, u32[]{:S(2)}) collective-permute-start(bf16[384,768]{1,0:T(8,128)(2,1)S(1)} %collective-permute-done.14.refs_8_), channel_id=1, source_target_pairs={{0,16},{16,0},{1,17},{17,1},{2,18},{18,2},{3,19},{19,3},{4,20},{20... | collective-permute-start | bytes 1769480 | tf_op jit(solution)/shard_map/ppermute | solution.py:292
  66.0 56.6 %collective-permute-start.8 = (bf16[384,768]{1,0:T(8,128)(2,1)}, bf16[384,768]{1,0:T(8,128)(2,1)}, u32[]{:S(2)}, u32[]{:S(2)}) collective-permute-start(bf16[384,768]{1,0:T(8,128)(2,1)} %collective-permute-done.6.refs_8_), channel_id=1, source_target_pairs={{0,4},{4,8},{8,12},{12,0},{1,5},{5,9},{9,13},{13,1},{2,6},{6,10},{... | collective-permute-start | bytes 1769480 | tf_op jit(solution)/shard_map/ppermute | solution.py:291
  66.0 94.5 %collective-permute-start.3 = (bf16[768,768]{1,0:T(8,128)(2,1)}, bf16[768,768]{1,0:T(8,128)(2,1)}, u32[]{:S(2)}, u32[]{:S(2)}) collective-permute-start(bf16[768,768]{1,0:T(8,128)(2,1)} %collective-permute-done.2.refs_3_), channel_id=1, source_target_pairs={{0,1},{1,0},{2,3},{3,2},{4,5},{5,4},{6,7},{7,6},{8,9},{9,8},{10,11... | collective-permute-start | bytes 3538952 | tf_op jit(solution)/shard_map/ppermute | solution.py:309
  119.0 41.6 %copy-start.5 = (bf16[384,768]{1,0:T(8,128)(2,1)S(1)}, bf16[384,768]{1,0:T(8,128)(2,1)}, u32[]{:S(2)}) copy-start(bf16[384,768]{1,0:T(8,128)(2,1)} %copy-done.4) | copy-start | bytes 1769476
  119.0 53.8 %collective-permute-start.5 = (bf16[384,768]{1,0:T(8,128)(2,1)S(1)}, bf16[384,768]{1,0:T(8,128)(2,1)S(1)}, u32[]{:S(2)}, u32[]{:S(2)}) collective-permute-start(bf16[384,768]{1,0:T(8,128)(2,1)S(1)} %collective-permute-done.4.refs_6_), channel_id=1, source_target_pairs={{0,16},{16,0},{1,17},{17,1},{2,18},{18,2},{3,19},{19,3},{4,20},{20... | collective-permute-start | bytes 1769480 | tf_op jit(solution)/shard_map/ppermute | solution.py:292
  120.6 55.3 %collective-permute-start.7 = (bf16[384,768]{1,0:T(8,128)(2,1)}, bf16[384,768]{1,0:T(8,128)(2,1)S(1)}, u32[]{:S(2)}, u32[]{:S(2)}) collective-permute-start(bf16[384,768]{1,0:T(8,128)(2,1)} %collective-permute-done.6.refs_8_), channel_id=1, source_target_pairs={{0,16},{16,0},{1,17},{17,1},{2,18},{18,2},{3,19},{19,3},{4,20},{20... | collective-permute-start | bytes 1769480 | tf_op jit(solution)/shard_map/ppermute | solution.py:292
  121.1 39.5 %collective-permute-start.17 = (bf16[384,768]{1,0:T(8,128)(2,1)}, bf16[384,768]{1,0:T(8,128)(2,1)S(1)}, u32[]{:S(2)}, u32[]{:S(2)}) collective-permute-start(bf16[384,768]{1,0:T(8,128)(2,1)} %collective-permute-done.16.refs_10_), channel_id=1, source_target_pairs={{0,16},{16,0},{1,17},{17,1},{2,18},{18,2},{3,19},{19,3},{4,20},{20... | collective-permute-start | bytes 1769480 | tf_op jit(solution)/shard_map/ppermute | solution.py:292
  122.6 53.3 %collective-permute-start.9 = (bf16[384,768]{1,0:T(8,128)(2,1)}, bf16[384,768]{1,0:T(8,128)(2,1)S(1)}, u32[]{:S(2)}, u32[]{:S(2)}) collective-permute-start(bf16[384,768]{1,0:T(8,128)(2,1)} %collective-permute-done.8.refs_10_), channel_id=1, source_target_pairs={{0,16},{16,0},{1,17},{17,1},{2,18},{18,2},{3,19},{19,3},{4,20},{20... | collective-permute-start | bytes 1769480 | tf_op jit(solution)/shard_map/ppermute | solution.py:292
  172.0 16.4 %collective-permute-start.18 = (bf16[192,768]{1,0:T(8,128)(2,1)S(1)}, bf16[192,768]{1,0:T(8,128)(2,1)S(1)}, u32[]{:S(2)}, u32[]{:S(2)}) collective-permute-start(bf16[192,768]{1,0:T(8,128)(2,1)S(1)} %get-tuple-element.21), channel_id=1, source_target_pairs={{0,4},{4,8},{8,12},{12,0},{1,5},{5,9},{9,13},{13,1},{2,6},{6,10},{... | collective-permute-start | bytes 884744 | tf_op jit(solution)/shard_map/ppermute | solution.py:333
  172.0 48.5 %collective-permute-start.19 = (bf16[192,768]{1,0:T(8,128)(2,1)}, bf16[192,768]{1,0:T(8,128)(2,1)S(1)}, u32[]{:S(2)}, u32[]{:S(2)}) collective-permute-start(bf16[192,768]{1,0:T(8,128)(2,1)} %get-tuple-element.22), channel_id=1, source_target_pairs={{0,8},{4,12},{8,0},{12,4},{1,9},{5,13},{9,1},{13,5},{2,10},{6,14},... | collective-permute-start | bytes 884744 | tf_op jit(solution)/shard_map/ppermute | solution.py:333
  172.7 18.5 %copy-start.10 = (f32[3072]{0:T(1024)S(1)}, f32[3072]{0:T(1024)}, u32[]{:S(2)}) copy-start(f32[3072]{0:T(1024)} %param.14) | copy-start | bytes 36868
  172.7 47.8 %collective-permute-start.20 = (bf16[192,768]{1,0:T(8,128)(2,1)}, bf16[192,768]{1,0:T(8,128)(2,1)S(1)}, u32[]{:S(2)}, u32[]{:S(2)}) collective-permute-start(bf16[192,768]{1,0:T(8,128)(2,1)} %get-tuple-element.23), channel_id=1, source_target_pairs={{0,12},{4,0},{8,4},{12,8},{1,13},{5,1},{9,5},{13,9},{2,14},{6,2},{... | collective-permute-start | bytes 884744 | tf_op jit(solution)/shard_map/ppermute | solution.py:333
  186.3 37.0 %collective-permute-start.10 = (bf16[192,768]{1,0:T(8,128)(2,1)}, bf16[192,768]{1,0:T(8,128)(2,1)S(1)}, u32[]{:S(2)}, u32[]{:S(2)}) collective-permute-start(bf16[192,768]{1,0:T(8,128)(2,1)} %get-tuple-element.17), channel_id=1, source_target_pairs={{0,4},{4,8},{8,12},{12,0},{1,5},{5,9},{9,13},{13,1},{2,6},{6,10},{... | collective-permute-start | bytes 884744 | tf_op jit(solution)/shard_map/ppermute | solution.py:333
  186.9 36.4 %collective-permute-start.11 = (bf16[192,768]{1,0:T(8,128)(2,1)}, bf16[192,768]{1,0:T(8,128)(2,1)S(1)}, u32[]{:S(2)}, u32[]{:S(2)}) collective-permute-start(bf16[192,768]{1,0:T(8,128)(2,1)} %get-tuple-element.18), channel_id=1, source_target_pairs={{0,8},{4,12},{8,0},{12,4},{1,9},{5,13},{9,1},{13,5},{2,10},{6,14},... | collective-permute-start | bytes 884744 | tf_op jit(solution)/shard_map/ppermute | solution.py:333
  188.4 34.9 %collective-permute-start.12 = (bf16[192,768]{1,0:T(8,128)(2,1)}, bf16[192,768]{1,0:T(8,128)(2,1)S(1)}, u32[]{:S(2)}, u32[]{:S(2)}) collective-permute-start(bf16[192,768]{1,0:T(8,128)(2,1)} %get-tuple-element.19), channel_id=1, source_target_pairs={{0,12},{4,0},{8,4},{12,8},{1,13},{5,1},{9,5},{13,9},{2,14},{6,2},{... | collective-permute-start | bytes 884744 | tf_op jit(solution)/shard_map/ppermute | solution.py:333
  (8 other events, 48.3 us)

commit v2 on v1

--- a/solution.py
+++ b/solution.py
@@ -27,6 +27,11 @@
 
 def crossed(count, by):
     return [(i, i ^ by) for i in range(count)]
+
+
+def send(values, axis, pairs, name):
+    with jax.named_scope(name):
+        return lax.ppermute(values, axis, pairs)
 
 
 def dot32(left, right):
@@ -61,8 +66,9 @@
     key_gain_ref,
     *rest,
 ):
-    heads_ref, sent_ref, head_means_ref, resid_means_ref, means_ref = rest[-5:]
+    heads_ref, sent_ref, resid_means_ref, means_ref = rest[-4:]
     k = pl.program_id(0)
+    lines = pl.ds(pl.multiple_of(k * span, 16), span)
     my_row = place_ref[0]
     image, first, size = image_for(
         counts_ref, plan_ref, my_row, lax.rem(my_row + k, rows), rows
@@ -76,9 +82,13 @@
     count = size.astype(jnp.float32)
     resid = dot32(select, resid_ref[pl.ds(begin, window), :])
     sent_ref[...] = resid.astype(jnp.bfloat16)
-    here = lax.broadcasted_iota(jnp.int32, (rows, 1), 0) == image
+    here = lax.broadcasted_iota(jnp.int32, (means_ref.shape[0], 1), 0) == image
     resid_mean = jnp.sum(resid, axis=0, keepdims=True) / count
     resid_means_ref[...] = jnp.where(here, resid_mean, resid_means_ref[...])
+
+    @pl.when(k == 0)
+    def _():
+        means_ref[...] = jnp.zeros_like(means_ref)
     queries = dot32(select, qkv_ref[0, pl.ds(begin, window), :])
     keys = dot32(select, qkv_ref[1, pl.ds(begin, window), :])
     values = dot32(select, qkv_ref[2, pl.ds(begin, window), :]).astype(jnp.bfloat16)
@@ -96,19 +106,19 @@
         scale = jnp.where(kept, 1.0 / jnp.sum(raised, axis=-1, keepdims=True), 0.0)
         weights = (raised * scale).astype(jnp.bfloat16)
         head = dot32(weights, values[:, columns]).astype(jnp.bfloat16)
-        heads_ref[:, columns] = head
+        heads_ref[lines, columns] = head
         head_mean = jnp.sum(head.astype(jnp.float32), axis=0, keepdims=True) / count
         means_ref[:, columns] = jnp.where(here, head_mean, means_ref[:, columns])
 
     @pl.when(k == rows - 1)
     def _():
-        head_means_ref[...] = means_ref[...].astype(jnp.bfloat16)
+        heads_ref[rows * span :, :] = means_ref[...].astype(jnp.bfloat16)
 
 
 def attend(place, counts, plan, qkv, resid, query_gain, key_gain, span, after):
     rows = counts.shape[0]
     local, features = qkv.shape[2], resid.shape[1]
-    whole = pl.BlockSpec(memory_space=pltpu.VMEM)
+    extra = -(-rows // 16) * 16
     fixed = lambda shape: pl.BlockSpec(shape, lambda k, *_: (0,) * len(shape))
     return pl.pallas_call(
         lambda *refs: attend_kernel(rows, span, *refs),
@@ -118,95 +128,318 @@
             in_specs=[fixed(x.shape) for x in (qkv, resid, query_gain, key_gain)]
             + [pl.BlockSpec(memory_space=pl.ANY)] * len(after),
             out_specs=[
-                pl.BlockSpec((span, local), lambda k, *_: (k, 0)),
+                fixed((rows * span + extra, local)),
                 pl.BlockSpec((span, features), lambda k, *_: (k, 0)),
-                fixed((rows, local)),
-                fixed((rows, features)),
+                fixed((extra, features)),
             ],
-            scratch_shapes=[pltpu.VMEM((rows, local), jnp.float32)],
+            scratch_shapes=[pltpu.VMEM((extra, local), jnp.float32)],
         ),
         out_shape=[
-            jax.ShapeDtypeStruct((rows * span, local), jnp.bfloat16),
+            jax.ShapeDtypeStruct((rows * span + extra, local), jnp.bfloat16),
             jax.ShapeDtypeStruct((rows * span, features), jnp.bfloat16),
-            jax.ShapeDtypeStruct((rows, local), jnp.bfloat16),
-            jax.ShapeDtypeStruct((rows, features), jnp.float32),
+            jax.ShapeDtypeStruct((extra, features), jnp.float32),
         ],
         compiler_params=pltpu.CompilerParams(vmem_limit_bytes=VMEM_BYTES),
         cost_estimate=pl.CostEstimate(
-            flops=10_000_000_000, bytes_accessed=12_000_000, transcendentals=1_000_000
+            flops=10_000_000_000, bytes_accessed=12_000_000, transcendentals=0
         ),
         name="attend",
     )(place, counts, plan, qkv, resid, query_gain, key_gain, *after)
 
 
-def project_kernel(rows, place_ref, *refs):
+def early_kernel(rows, chunks, place_ref, *refs):
     head_refs = refs[:rows]
     own_ref = refs[rows]
-    piece_refs = refs[rows + 1 : rows + 1 + 2 * (rows - 1)]
-    resid_ref = refs[3 * rows - 1]
-    out_refs = refs[3 * rows : 4 * rows]
-    held_ref, sems = refs[4 * rows :]
+    piece_refs = refs[rows + 1 : rows + 1 + 3 * chunks]
+    resid_ref, total_ref, late_ref = refs[rows + 1 + 3 * chunks :][:3]
+    held_ref, weight_ref, head_sems, weight_sems, late_sem = refs[-5:]
     my_row, my_part, my_group = place_ref[0], place_ref[1], place_ref[2]
-    half = held_ref.shape[2]
-
-    @pl.when(pl.program_id(0) == 0)
+    tiles, used, tile = weight_ref.shape
+    depth = held_ref.shape[1] // rows
+    half = depth // 2
+
+    def head_copies():
+        copies = []
+        for x in range(rows):
+            step = lax.rem(my_row - (x ^ my_part) + rows, rows)
+            for s in range(2):
+                turned = jnp.where(step == 0, s, s ^ my_group)
+                start = pl.multiple_of(step * depth + turned * half, 128)
+                copies.append(
+                    pltpu.make_async_copy(
+                        head_refs[x].at[: held_ref.shape[0], s * half : (s + 1) * half],
+                        held_ref.at[:, pl.ds(start, half)],
+                        head_sems.at[x, s],
+                    )
+                )
+        return copies
+
+    def weight_copies(i):
+        chunk, column = i * chunks // tiles, i % (tiles // chunks) * tile
+        sources = [own_ref.at[:, i * tile : (i + 1) * tile]]
+        sources += [piece_refs[3 * chunk + n].at[:, column : column + tile] for n in range(3)]
+        starts = [0, depth, depth + half, depth + 2 * half]
+        return [
+            pltpu.make_async_copy(
+                source, weight_ref.at[i, pl.ds(start, source.shape[0])], weight_sems.at[i, n]
+            )
+            for n, (source, start) in enumerate(zip(sources, starts))
+        ]
+
+    i = pl.program_id(0)
+    late_copy = pltpu.make_async_copy(held_ref.at[:, used:], late_ref, late_sem)
+
+    @pl.when(i == 0)
     def _():
-        copies = [
-            pltpu.make_async_copy(
-                head_refs[x].at[:, s * half : (s + 1) * half],
-                held_ref.at[2 * (x ^ my_part) + s],
-                sems.at[x, s],
-            )
-            for x in range(rows)
-            for s in range(2)
-        ]
-        for copy in copies:
+        for copy in head_copies():
             copy.start()
-        for copy in copies:
+        for j in range(tiles):
+            for copy in weight_copies(j):
+                copy.start()
+        for copy in head_copies():
             copy.wait()
-
-    total = resid_ref[...].astype(jnp.float32)
-    for s in range(2):
-        total = total + dot32(held_ref[2 * my_row + s], own_ref[s * half : (s + 1) * half, :])
-    for step in range(1, rows):
-        row = lax.rem(my_row - step + rows, rows)
-        for which in range(2):
-            piece_ref = piece_refs[2 * (step - 1) + which]
-            total = total + dot32(held_ref[2 * row + (my_group ^ which)], piece_ref[...])
+        late_copy.start()
+
+    for j in range(tiles):
+
+        @pl.when(i == j)
+        def _():
+            for copy in weight_copies(j):
+                copy.wait()
+
+    length = resid_ref.shape[0]
+    for start in range(0, length, 256):
+        lines = slice(start, min(start + 256, length))
+        total = dot32(held_ref[lines, :used], weight_ref[i])
+        total_ref[lines] = total + resid_ref[lines].astype(jnp.float32)
+
+    @pl.when(i == tiles - 1)
+    def _():
+        late_copy.wait()
+
+
+def project_early(place, heads, out_weight, pieces, resid):
+    rows, chunks = len(heads), len(pieces)
+    length, features = resid.shape
+    depth = heads[0].shape[1]
+    used = depth * 5 // 2
+    tile = 256
+    tiles = features // tile
+    flat = [piece for chunk in pieces for piece in chunk[:3]]
+    anywhere = pl.BlockSpec(memory_space=pl.ANY)
+    column = lambda x: pl.BlockSpec((x, tile), lambda i: (0, i))
+    return pl.pallas_call(
+        lambda *refs: early_kernel(rows, chunks, *refs),
+        grid=(tiles,),
+        in_specs=[pl.BlockSpec(memory_space=pltpu.SMEM)]
+        + [anywhere] * (rows + 1 + len(flat))
+        + [column(length)],
+        out_specs=[column(length), anywhere],
+        scratch_shapes=[
+            pltpu.VMEM((length, rows * depth), jnp.bfloat16),
+            pltpu.VMEM((tiles, used, tile), jnp.bfloat16),
+            pltpu.SemaphoreType.DMA((rows, 2)),
+            pltpu.SemaphoreType.DMA((tiles, 4)),
+            pltpu.SemaphoreType.DMA,
+        ],
+        out_shape=[
+            jax.ShapeDtypeStruct((length, features), jnp.float32),
+            jax.ShapeDtypeStruct((length, rows * depth - used), jnp.bfloat16),
+        ],
+        compiler_params=pltpu.CompilerParams(vmem_limit_bytes=VMEM_BYTES),
+        cost_estimate=pl.CostEstimate(
+            flops=2 * length * used * features, bytes_accessed=12_000_000, transcendentals=0
+        ),
+        name="project_early",
+    )(place, *heads, out_weight, *flat, resid)
+
+
+def late_kernel(rows, total_ref, late_ref, *refs):
+    piece_refs, out_refs = refs[:3], refs[-rows:]
+    half = piece_refs[0].shape[0]
     span = out_refs[0].shape[0]
     for k in range(rows):
-        out_refs[k][...] = total[k * span : (k + 1) * span].astype(jnp.bfloat16)
-
-
-def project(place, heads, out_weight, pieces, resid, chunk, width, span):
-    rows = len(heads)
-    length, depth = heads[0].shape
-    half = depth // 2
+        lines = slice(k * span, (k + 1) * span)
+        total = total_ref[lines, :]
+        for n in range(3):
+            total = total + dot32(late_ref[lines, n * half : (n + 1) * half], piece_refs[n][...])
+        out_refs[k][...] = total.astype(jnp.bfloat16)
+
+
+def project_late(total, late, pieces, chunk, rows, span, after):
+    half, width = pieces[0].shape
+    length = total.shape[0]
     tile = 256
     tiles = width // tile
     first = chunk * tiles
     return pl.pallas_call(
-        lambda *refs: project_kernel(rows, *refs),
-        grid_spec=pltpu.PrefetchScalarGridSpec(
-            num_scalar_prefetch=1,
-            grid=(tiles,),
-            in_specs=[pl.BlockSpec(memory_space=pl.ANY)] * rows
-            + [pl.BlockSpec((depth, tile), lambda i, *_: (0, first + i))]
-            + [pl.BlockSpec((half, tile), lambda i, *_: (0, i))] * len(pieces)
-            + [pl.BlockSpec((length, tile), lambda i, *_: (0, first + i))],
-            out_specs=[pl.BlockSpec((span, tile), lambda i, *_: (0, i))] * rows,
-            scratch_shapes=[
-                pltpu.VMEM((2 * rows, length, half), jnp.bfloat16),
-                pltpu.SemaphoreType.DMA((rows, 2)),
-            ],
-        ),
+        lambda *refs: late_kernel(rows, *refs),
+        grid=(tiles,),
+        in_specs=[
+            pl.BlockSpec((length, tile), lambda i: (0, first + i)),
+            pl.BlockSpec(late.shape, lambda i: (0, 0)),
+        ]
+        + [pl.BlockSpec((half, tile), lambda i: (0, i))] * 3
+        + [pl.BlockSpec(memory_space=pl.ANY)] * len(after),
+        out_specs=[pl.BlockSpec((span, tile), lambda i: (0, i))] * rows,
         out_shape=[jax.ShapeDtypeStruct((span, width), jnp.bfloat16)] * rows,
         compiler_params=pltpu.CompilerParams(vmem_limit_bytes=VMEM_BYTES),
         cost_estimate=pl.CostEstimate(
-            flops=2 * length * depth * rows * width, bytes_accessed=12_000_000, transcendentals=0
-        ),
-        name="project",
-    )(place, *heads, out_weight, *pieces, resid)
+            flops=6 * length * half * width, bytes_accessed=6_000_000, transcendentals=0
+        ),
+        name="project_late",
+    )(total, late, *pieces, *after)
+
+
+def one_hot(hits):
+    return hits.astype(jnp.float32).astype(jnp.bfloat16)
+
+
+def parts_kernel(rows, start, place_ref, *refs):
+    head_refs, out_refs = refs[:rows], refs[rows : 2 * rows]
+    tail_ref, sems = refs[2 * rows :]
+    copies = [
+        pltpu.make_async_copy(
+            head_refs[x].at[start : start + tail_ref.shape[1]], tail_ref.at[x], sems.at[x]
+        )
+        for x in range(rows)
+    ]
+    for copy in copies:
+        copy.start()
+    for copy in copies:
+        copy.wait()
+    for k in range(rows):
+        row = lax.rem(place_ref[0] + k, rows)
+        out_refs[k][...] = tail_ref[row ^ place_ref[1]][:rows]
+
+
+def head_parts(place, heads, start):
+    rows, (length, depth) = len(heads), heads[0].shape
+    return pl.pallas_call(
+        lambda *refs: parts_kernel(rows, start, *refs),
+        in_specs=[pl.BlockSpec(memory_space=pltpu.SMEM)]
+        + [pl.BlockSpec(memory_space=pl.ANY)] * rows,
+        out_specs=[pl.BlockSpec(memory_space=pltpu.VMEM)] * rows,
+        out_shape=[jax.ShapeDtypeStruct((rows, depth), jnp.bfloat16)] * rows,
+        scratch_shapes=[
+            pltpu.VMEM((rows, length - start, depth), jnp.bfloat16),
+            pltpu.SemaphoreType.DMA((rows,)),
+        ],
+        cost_estimate=pl.CostEstimate(flops=1000, bytes_accessed=1000, transcendentals=0),
+        compiler_params=pltpu.CompilerParams(vmem_limit_bytes=VMEM_BYTES),
+        name="head_parts",
+    )(place, *heads)
+
+
+def share_kernel(rows, place_ref, *refs):
+    got_refs = refs[:rows]
+    weight_ref, resid_ref = refs[rows : rows + 2]
+    share_ref = refs[-1]
+    my_row = place_ref[0]
+    count = rows * rows
+    image = lax.broadcasted_iota(jnp.int32, (count, rows), 0)
+    entry = lax.broadcasted_iota(jnp.int32, (count, rows), 1)
+    got = None
+    for k in range(rows):
+        row = lax.rem(my_row - k + rows, rows)
+        term = dot32(one_hot(image == row * rows + entry), got_refs[k][...])
+        got = term if got is None else got + term
+    mine = lax.broadcasted_iota(jnp.int32, (count, 1), 0) // rows == my_row
+    resid = jnp.concatenate([resid_ref[:rows]] * rows, axis=0)
+    share = dot32(got.astype(jnp.bfloat16), weight_ref[...]) + jnp.where(mine, resid, 0.0)
+    share_ref[...] = share.astype(jnp.bfloat16)
+
+
+def local_call(kernel, out_shape, operands, after, place, name, flops):
+    whole = pl.BlockSpec(memory_space=pltpu.VMEM)
+    return pl.pallas_call(
+        kernel,
+        in_specs=[pl.BlockSpec(memory_space=pltpu.SMEM)]
+        + [whole] * len(operands)
+        + [pl.BlockSpec(memory_space=pl.ANY)] * len(after),
+        out_specs=jax.tree.map(lambda _: whole, out_shape),
+        out_shape=out_shape,
+        compiler_params=pltpu.CompilerParams(vmem_limit_bytes=VMEM_BYTES),
+        cost_estimate=pl.CostEstimate(flops=flops, bytes_accessed=1000, transcendentals=0),
+        name=name,
+    )(place, *operands, *after)
+
+
+def after_all(values, after):
+    return lax.optimization_barrier((list(values), list(after)))[0]
+
+
+def terms_kernel(rows, place_ref, *refs):
+    share_refs = refs[:rows]
+    weight_ref = refs[rows]
+    out_refs = refs[-rows - 1 : -1]
+    pooled_ref = refs[-1]
+    count = rows * rows
+
+    @pl.when(pl.program_id(0) == 0)
+    def _():
+        pooled = share_refs[0][...].astype(jnp.float32)
+        for k in range(1, rows):
+            pooled = pooled + share_refs[k][...].astype(jnp.float32)
+        wanted = lax.broadcasted_iota(jnp.int32, (count, count), 0)
+        image = lax.broadcasted_iota(jnp.int32, (count, count), 1)
+        part = wanted // rows ^ place_ref[1]
+        order = one_hot(image == wanted % rows * rows + part)
+        pooled_ref[...] = dot32(order, pooled.astype(jnp.bfloat16)).astype(jnp.bfloat16)
+
+    terms = dot32(pooled_ref[...], weight_ref[...]).astype(jnp.bfloat16)
+    for k in range(rows):
+        out_refs[k][...] = terms[k * rows : (k + 1) * rows]
+
+
+def label_terms_by_part(place, shares, label_weight, after):
+    rows = len(shares)
+    count, features = shares[0].shape
+    classes = label_weight.shape[1]
+    tile = 512
+    fixed = pl.BlockSpec((count, features), lambda i, *_: (0, 0))
+    return pl.pallas_call(
+        lambda *refs: terms_kernel(rows, *refs),
+        grid_spec=pltpu.PrefetchScalarGridSpec(
+            num_scalar_prefetch=1,
+            grid=(classes // tile,),
+            in_specs=[fixed] * rows
+            + [pl.BlockSpec((features, tile), lambda i, *_: (0, i))]
+            + [pl.BlockSpec(memory_space=pl.ANY)] * len(after),
+            out_specs=[pl.BlockSpec((rows, tile), lambda i, *_: (0, i))] * rows,
+            scratch_shapes=[pltpu.VMEM((count, features), jnp.bfloat16)],
+        ),
+        out_shape=[jax.ShapeDtypeStruct((rows, classes), jnp.bfloat16)] * rows,
+        compiler_params=pltpu.CompilerParams(vmem_limit_bytes=VMEM_BYTES),
+        cost_estimate=pl.CostEstimate(
+            flops=2 * count * features * classes, bytes_accessed=12_000_000, transcendentals=0
+        ),
+        name="label_terms",
+    )(place, *shares, label_weight, *after)
+
+
+def probs_kernel(rows, place_ref, *refs):
+    term_refs = refs[:rows]
+    bias_ref = refs[rows]
+    out_refs = refs[-rows:]
+    logits = term_refs[0][...].astype(jnp.float32)
+    for k in range(1, rows):
+        logits = logits + term_refs[k][...].astype(jnp.float32)
+    probs = jax.nn.sigmoid(logits + bias_ref[...])
+    line = lax.broadcasted_iota(jnp.int32, (rows, 1), 0)
+    for k in range(rows):
+        row = lax.rem(place_ref[0] + k, rows)
+        picked = jnp.sum(jnp.where(line == row, probs, 0.0), axis=0, keepdims=True)
+        out_refs[k][...] = picked.astype(jnp.bfloat16)
+
+
+def labels_kernel(rows, place_ref, *refs):
+    out_ref = refs[-1]
+    classes = refs[0].shape[1]
+    for k in range(rows):
+        row = lax.rem(place_ref[0] - k + rows, rows)
+        columns = pl.ds(pl.multiple_of(row * classes, 128), classes)
+        out_ref[:, columns] = refs[k][...].astype(jnp.float32)
 
 
 def settle_kernel(rows, place_ref, counts_ref, plan_ref, *refs):
@@ -230,7 +463,7 @@
     out_ref[...] = total.astype(jnp.bfloat16)
 
 
-def settle(place, counts, plan, blocks, chunk, features, earlier):
+def settle(place, counts, plan, blocks, chunk, features, earlier, after):
     rows = len(blocks)
     span, width = blocks[0].shape
     tile = 256
@@ -243,7 +476,7 @@
             num_scalar_prefetch=3,
             grid=(tiles,),
             in_specs=[pl.BlockSpec((span, tile), lambda i, *_: (0, i))] * rows
-            + [pl.BlockSpec(memory_space=pl.ANY)] * len(more),
+            + [pl.BlockSpec(memory_space=pl.ANY)] * (len(more) + len(after)),
             out_specs=pl.BlockSpec((TOK, tile), lambda i, *_: (0, first + i)),
         ),
         out_shape=jax.ShapeDtypeStruct((TOK, features), jnp.bfloat16),
@@ -253,7 +486,7 @@
             flops=2 * TOK * rows * span * width, bytes_accessed=2_000_000, transcendentals=0
         ),
         name="settle",
-    )(place, counts, plan, *blocks, *more)
+    )(place, counts, plan, *blocks, *more, *after)
 
 
 def on_device_rings(
@@ -280,20 +513,14 @@
     depth, features = out_weight.shape
     half = depth // sharers
     width = features // CHUNKS
-    image_ids = jnp.arange(rows, dtype=jnp.int32)
     place = jnp.stack([my_row, my_part, my_group]).astype(jnp.int32)
 
     mine = lax.dynamic_slice_in_dim(out_weight, my_group * half, half, 0)
     moving = [mine[:, c * width : (c + 1) * width] for c in range(CHUNKS)]
-    pieces = [[] for _ in range(CHUNKS)]
-    for _ in range(1, rows):
-        for c in range(CHUNKS):
-            moving[c] = lax.ppermute(moving[c], "dp", shifted(rows, 1))
-            other = lax.ppermute(moving[c], "groups", crossed(sharers, 1))
-            pieces[c] += [moving[c], other]
+    moving = [send(x, "dp", shifted(rows, 1), f"w{c}_1") for c, x in enumerate(moving)]
 
     qkv = jnp.pad(jnp.transpose(qkv_home[0], (1, 0, 2)), ((0, 0), (0, padded - slots), (0, 0)))
-    heads, resid, head_means, resid_means = attend(
+    heads, resid, resid_means = attend(
         place,
         patch_counts,
         move_plan,
@@ -302,36 +529,86 @@
         query_gain[None],
         key_gain[None],
         span,
-        [pieces[0][0]],
-    )
-    across = lax.ppermute(heads, "mp", crossed(parts, 2))
-    beside = lax.ppermute(heads, "mp", crossed(parts, 1))
-    beyond = lax.ppermute(across, "mp", crossed(parts, 1))
-
-    got = lax.all_gather(head_means, ("dp", "mp"), axis=0)
-    got = at(got.reshape(rows, parts, rows, depth), my_row, 1).reshape(rows * rows, depth)
-    share = dot32(got, out_weight).reshape(rows, rows, features)
-    share = share + jnp.where((image_ids == my_row)[:, None, None], resid_means[None], 0.0)
-    share = share.reshape(rows * rows, features).astype(jnp.bfloat16)
-    pooled = jnp.sum(lax.all_gather(share, "dp", axis=0).astype(jnp.float32), axis=0)
-    terms = dot32(pooled.astype(jnp.bfloat16), label_weight)
+        moving[:1],
+    )
+    heads = after_all([heads], moving[1:])[0]
+    across = send(heads, "mp", crossed(parts, 2), "h_2")
+    beside = send(heads, "mp", crossed(parts, 1), "h_1")
+
+    following = [send(x, "dp", shifted(rows, 1), f"w{c}_2") for c, x in enumerate(moving)]
+    others = [
+        send(x, "groups", crossed(sharers, 1), f"y{c}_1") for c, x in enumerate(moving)
+    ]
+    pieces = [[x, y, z] for x, y, z in zip(moving, others, following)]
+    turned = after_all([across], [*following, *others])[0]
+    beyond = send(turned, "mp", crossed(parts, 1), "h_3")
+    every_head = [heads, beside, across, beyond]
+
+    gathered = head_parts(place, every_head, rows * span)
+    gathered = [gathered[0]] + [
+        send(gathered[k], "dp", shifted(rows, k), f"g_{k}") for k in range(1, rows)
+    ]
+    image_count = rows * rows
+    share = local_call(
+        lambda *refs: share_kernel(rows, *refs),
+        jax.ShapeDtypeStruct((image_count, features), jnp.bfloat16),
+        [*gathered, out_weight, resid_means],
+        [],
+        place,
+        "share",
+        1000,
+    )
+    shares = [share] + [send(share, "dp", shifted(rows, k), f"s_{k}") for k in range(1, rows)]
+
+    total, late = project_early(place, every_head, out_weight, pieces, resid)
+    pieces, moving = [], following
+    for c in range(CHUNKS):
+        x = after_all([moving[c]], [total, *gathered[1:]])[0] if c else moving[c]
+        x = send(x, "dp", shifted(rows, 1), f"w{c}_3")
+        y = after_all([moving[c]], [x, *shares[1:]])[0] if c else moving[c]
+        y = send(y, "groups", crossed(sharers, 1), f"y{c}_2")
+        z = after_all([x], [y, total, share])[0] if c == 0 else x
+        z = send(z, "groups", crossed(sharers, 1), f"y{c}_3")
+        pieces.append([y, x, z])
+
     classes = label_weight.shape[1]
-    terms = terms.reshape(rows, rows, classes).astype(jnp.bfloat16)
-    terms = lax.all_to_all(terms, "mp", split_axis=1, concat_axis=1, tiled=True)
-    logits = jnp.sum(terms.astype(jnp.float32), axis=1)
-    probs = jax.nn.sigmoid(logits + label_bias[None, :]).astype(jnp.bfloat16)
-    labels = lax.all_to_all(probs, "dp", split_axis=0, concat_axis=0, tiled=True)
-    labels = labels.reshape(1, 1, rows * classes).astype(jnp.float32)
-
+    arrived = []
+    for c in range(CHUNKS):
+        after = [terms[0], arrived[0][3]] if c else shares[1:]
+        blocks = project_late(total, late, pieces[c], c, rows, span, after)
+        arrived.append(
+            [blocks[0]] + [send(blocks[k], "dp", shifted(rows, k), f"m{c}_{k}") for k in range(1, rows)]
+        )
+        if c == 0:
+            terms = label_terms_by_part(place, shares, label_weight, arrived[0][1:2])
+
+    terms = [terms[0]] + [
+        send(terms[k], "mp", crossed(parts, k), f"t_{k}") for k in range(1, parts)
+    ]
+    probs = local_call(
+        lambda *refs: probs_kernel(rows, *refs),
+        [jax.ShapeDtypeStruct((1, classes), jnp.bfloat16)] * rows,
+        [*terms, label_bias[None]],
+        [],
+        place,
+        "probs",
+        1000,
+    )
+    probs = [probs[0]] + [send(probs[k], "dp", shifted(rows, k), f"l_{k}") for k in range(1, rows)]
+    labels = local_call(
+        lambda *refs: labels_kernel(rows, *refs),
+        jax.ShapeDtypeStruct((1, rows * classes), jnp.float32),
+        probs,
+        [],
+        place,
+        "labels",
+        1000,
+    )
     mixed = None
     for c in range(CHUNKS):
-        blocks = project(
-            place, [heads, beside, across, beyond], out_weight, pieces[c], resid, c, width, span
-        )
-        arrived = [blocks[0]]
-        for k in range(1, rows):
-            arrived.append(lax.ppermute(blocks[k], "dp", shifted(rows, k)))
-        mixed = settle(place, patch_counts, move_plan, arrived, c, features, mixed)
+        after = [labels] if c == CHUNKS - 1 else []
+        mixed = settle(place, patch_counts, move_plan, arrived[c], c, features, mixed, after)
+    labels = labels[None]
     return (mixed[None], labels)
 
 def attend_home(qkv_rows, seg_rows, query_gain, key_gain):

time: 227 us -> 169 us (0.74)
  blocking collectives: 84.6 us -> 0 us
  waiting for transfers between devices: 59.2 us -> 74.6 us
  starting transfers between devices: 23.8 us -> 36.9 us
  Pallas kernels: 36.5 us -> 45.9 us
  matrix products: 7.18 us -> 0 us
  local copies, waits for them, and re-layouts: 12.4 us -> 10.1 us
    all_gather x2 -> x0, blocking collectives: 50.6 us -> none  [the longest x1 36.7 us: on_device_rings(): got = lax.all_gather(head_means, ('dp', 'mp'), axis=0)]
    all_to_all x2 -> x0, blocking collectives: 33.9 us -> none  [the longest x1 27.3 us: on_device_rings(): lax.all_to_all(probs, 'dp', split_axis=0, concat_axis=0, tiled=True)]
    ppermute x21 -> x33, waiting for transfers between devices: 59.2 us -> 74.6 us  [send(): return lax.ppermute(values, axis, pairs)]
    ppermute x21 -> x33, starting transfers between devices: 23.8 us -> 36.9 us  [send(): return lax.ppermute(values, axis, pairs)]
    pallas_call x2 -> x8, Pallas kernels: 20.7 us -> 29.5 us  [the longest x1 11.4 us: project_early(): pl.pallas_call(lambda *refs: early_kernel(rows, chunks, *refs), grid=(til...]
    dot_general x2 -> x0, matrix products: 7.18 us -> none  [dot32(): return jnp.dot(left, right, preferred_element_type=jnp.float32)]
  transfers between devices with their start and end apart: 21 -> 33, of which waited for: 4 -> 13; matrix products, arithmetic and copies ran while one was open for 7% -> 4% of each run, Pallas kernels for 15% -> 26%
where the time goes in v2:
time: 169 us; the launch traced here: 168 us
  waiting for transfers between devices  74.6 us (44%)
  Pallas kernels  45.9 us (27%)
  starting transfers between devices  36.9 us (22%)
  local copies, waits for them, and re-layouts  10.1 us (6%)
    ppermute x33, waiting for transfers between devices, send(): return lax.ppermute(values, axis, pairs)  74.6 us
    ppermute x33, starting transfers between devices, send(): return lax.ppermute(values, axis, pairs)  36.9 us
    pallas_call x1, Pallas kernels, project_early(): pl.pallas_call(lambda *refs: early_kernel(rows, chunks, *refs), grid=(til...  11.4 us
    pallas_call x1, Pallas kernels, attend(): pl.pallas_call(lambda *refs: attend_kernel(rows, span, *refs), grid_spec=...  10.7 us
    pallas_call x2, Pallas kernels, project_late(): pl.pallas_call(lambda *refs: late_kernel(rows, *refs), grid=(tiles,), in_...  7.88 us
    pallas_call x1, Pallas kernels, label_terms_by_part(): pl.pallas_call(lambda *refs: terms_kernel(rows, *refs), grid_spec=pltpu.P...  6.55 us
    pallas_call x2, Pallas kernels, settle(): pl.pallas_call(lambda *refs: settle_kernel(rows, *refs), grid_spec=pltpu....  5.65 us
    pad x1, local copies, waits for them, and re-layouts, on_device_rings(): jnp.pad(jnp.transpose(qkv_home[0], (1, 0, 2)), ((0, 0), (0, padded - slot...  4.49 us
  transfers between devices with their start and end apart: 33, of which 13 were waited for; matrix products, arithmetic and copies ran while one was open for 4% of the time, Pallas kernels for 26%

profile of v2, /device:TPU:0, one launch (start us, length us, event | category | flops | bytes accessed | tf_op | source)
XLA Modules:
  0.0 168.3 jit_solution(2473726804207368447)
XLA Ops:
  2.0 3.1 %collective-permute-start = (bf16[384,768]{1,0:T(8,128)(2,1)S(1)}, bf16[384,768]{1,0:T(8,128)(2,1)S(1)}, u32[]{:S(2)}, u32[]{:S(2)}) collective-permute-start(bf16[384,768]{1,0:T(8,128)(2,1)S(1)} %get-tuple-element.63), channel_id=1, source_target_pairs={{0,4},{4,8},{8,12},{12,0},{1,5},{5,9},{9,13},{13,1},{2,6},{6,10},{... | collective-permute-start | bytes 1769480 | tf_op jit(solution)/shard_map/w0_1/ppermute | solution.py:34
  6.6 4.5 %pad.8.refs_3_ = bf16[3,960,768]{2,1,0:T(8,128)(2,1)} pad(bf16[3,764,768]{2,1,0:T(8,128)(2,1)} %bitcast.17, bf16[]{:T(256)} %constant.17.clone.1), padding=0_0x0_196x0_0 | pad | bytes 7944194 | tf_op jit(solution)/shard_map/jit(_pad)/pad | solution.py:522
  13.0 8.2 %collective-permute-done.refs_7_.refs_6_ = bf16[384,768]{1,0:T(8,128)(2,1)S(1)} collective-permute-done((bf16[384,768]{1,0:T(8,128)(2,1)S(1)}, bf16[384,768]{1,0:T(8,128)(2,1)S(1)}, u32[]{:S(2)}, u32[]{:S(2)}) %collective-permute-start) | collective-permute-done | bytes 589856 | tf_op jit(solution)/shard_map/w0_1/ppermute | solution.py:34
  21.2 10.7 %attend.1 = (bf16[784,768]{1,0:T(8,128)(2,1)S(1)}, bf16[768,1536]{1,0:T(8,128)(2,1)S(1)}, f32[16,1536]{1,0:T(8,128)S(1)}) custom-call(s32[3]{0:T(128)S(1)} %pad_add_fusion.refs_0_, s32[4,4]{1,0:T(4,128)S(1)} %copy-done.6, s32[4,4]{1,0:T(4,128)S(1)} %copy-done.7, bf16[3,960,768]{2,1,0:T(8,128)(2,1)} %pad.8.refs_3_, bf16[960,1536]{1,0:T(8,128)(2,1)} %pad.9.refs_4_, ...), custom_call_target="tpu_custom_call" | custom-call | flops 10000000000 | bytes 12000000 | tf_op jit(solution)/shard_map/attend/pallas_call | solution.py:123
  38.5 14.7 %collective-permute-done.4.refs_8_ = bf16[384,768]{1,0:T(8,128)(2,1)S(1)} collective-permute-done((bf16[384,768]{1,0:T(8,128)(2,1)S(1)}, bf16[384,768]{1,0:T(8,128)(2,1)S(1)}, u32[]{:S(2)}, u32[]{:S(2)}) %collective-permute-start.4) | collective-permute-done | bytes 589856 | tf_op jit(solution)/shard_map/w0_2/ppermute | solution.py:34
  53.2 9.8 %collective-permute-done.5.refs_11_ = bf16[384,768]{1,0:T(8,128)(2,1)S(1)} collective-permute-done((bf16[384,768]{1,0:T(8,128)(2,1)S(1)}, bf16[384,768]{1,0:T(8,128)(2,1)S(1)}, u32[]{:S(2)}, u32[]{:S(2)}) %collective-permute-start.5) | collective-permute-done | bytes 589856 | tf_op jit(solution)/shard_map/w1_2/ppermute | solution.py:34
  67.0 1.9 %collective-permute-start.10 = (bf16[4,768]{1,0:T(4,128)(2,1)S(1)}, bf16[4,768]{1,0:T(4,128)(2,1)S(1)}, u32[]{:S(2)}, u32[]{:S(2)}) collective-permute-start(bf16[4,768]{1,0:T(4,128)(2,1)S(1)} %get-tuple-element.39), channel_id=1, source_target_pairs={{0,8},{4,12},{8,0},{12,4},{1,9},{5,13},{9,1},{13,5},{2,10},{6,14},... | collective-permute-start | bytes 18440 | tf_op jit(solution)/shard_map/g_2/ppermute | solution.py:34
  70.9 11.4 %project_early.1 = (f32[768,1536]{1,0:T(8,128)}, bf16[768,1152]{1,0:T(8,128)(2,1)}) custom-call(s32[3]{0:T(128)S(1)} %pad_add_fusion.refs_0_, bf16[784,768]{1,0:T(8,128)(2,1)S(1)} %get-tuple-element.33.refs_1_, bf16[784,768]{1,0:T(8,128)(2,1)S(1)} %collective-permute-done.2.refs_2_, bf16[784,768]{1,0:T(8,128)(2,1)} %copy-done.2, bf16[784,768]{1,0:T(8,128)(2,1)} %copy-done.3, ...), custom_call_target="tpu_custom_call" | custom-call | flops 4529848320 | bytes 12000000 | tf_op jit(solution)/shard_map/project_early/pallas_call | solution.py:231
  86.6 2.9 %collective-permute-start.14 = (bf16[16,1536]{1,0:T(8,128)(2,1)S(1)}, bf16[16,1536]{1,0:T(8,128)(2,1)S(1)}, u32[]{:S(2)}, u32[]{:S(2)}) collective-permute-start(bf16[16,1536]{1,0:T(8,128)(2,1)S(1)} %share.1.refs_1_), channel_id=1, source_target_pairs={{0,8},{4,12},{8,0},{12,4},{1,9},{5,13},{9,1},{13,5},{2,10},{6,14},... | collective-permute-start | bytes 147464 | tf_op jit(solution)/shard_map/s_2/ppermute | solution.py:34
  91.1 9.9 %collective-permute-done.13.refs_5_.refs_2_ = bf16[16,1536]{1,0:T(8,128)(2,1)S(1)} collective-permute-done((bf16[16,1536]{1,0:T(8,128)(2,1)S(1)}, bf16[16,1536]{1,0:T(8,128)(2,1)S(1)}, u32[]{:S(2)}, u32[]{:S(2)}) %collective-permute-start.13) | collective-permute-done | bytes 49184 | tf_op jit(solution)/shard_map/s_1/ppermute | solution.py:34
  104.1 3.9 %project_late.2 = (bf16[192,768]{1,0:T(8,128)(2,1)S(1)}, bf16[192,768]{1,0:T(8,128)(2,1)S(1)}, bf16[192,768]{1,0:T(8,128)(2,1)S(1)}, bf16[192,768]{1,0:T(8,128)(2,1)S(1)}) custom-call(f32[768,1536]{1,0:T(8,128)} %get-tuple-element.36.refs_0_, bf16[768,1152]{1,0:T(8,128)(2,1)S(1)} %copy-done, bf16[384,768]{1,0:T(8,128)(2,1)S(1)} %collective-permute-done.18.refs_2_, ...), custom_call_target="tpu_custom_call" | custom-call | flops 1358954496 | bytes 6000000 | tf_op jit(solution)/shard_map/project_late/pallas_call | solution.py:275
  109.6 2.3 %collective-permute-start.22 = (bf16[192,768]{1,0:T(8,128)(2,1)S(1)}, bf16[192,768]{1,0:T(8,128)(2,1)S(1)}, u32[]{:S(2)}, u32[]{:S(2)}) collective-permute-start(bf16[192,768]{1,0:T(8,128)(2,1)S(1)} %get-tuple-element.48), channel_id=1, source_target_pairs={{0,12},{4,0},{8,4},{12,8},{1,13},{5,1},{9,5},{13,9},{2,14},{6,2},{... | collective-permute-start | bytes 884744 | tf_op jit(solution)/shard_map/m0_3/ppermute | solution.py:34
  111.9 7.9 %collective-permute-done.21.refs_6_.refs_4_ = bf16[192,768]{1,0:T(8,128)(2,1)S(1)} collective-permute-done((bf16[192,768]{1,0:T(8,128)(2,1)S(1)}, bf16[192,768]{1,0:T(8,128)(2,1)S(1)}, u32[]{:S(2)}, u32[]{:S(2)}) %collective-permute-start.21) | collective-permute-done | bytes 294944 | tf_op jit(solution)/shard_map/m0_1/ppermute | solution.py:34
  119.8 6.5 %label_terms.1 = (bf16[4,3072]{1,0:T(4,128)(2,1)S(1)}, bf16[4,3072]{1,0:T(4,128)(2,1)S(1)}, bf16[4,3072]{1,0:T(4,128)(2,1)S(1)}, bf16[4,3072]{1,0:T(4,128)(2,1)S(1)}) custom-call(s32[3]{0:T(128)S(1)} %pad_add_fusion.refs_0_, bf16[16,1536]{1,0:T(8,128)(2,1)S(1)} %share.1.refs_1_, bf16[16,1536]{1,0:T(8,128)(2,1)S(1)} %collective-permute-done.13.refs_5_.refs_2_, ...), custom_call_target="tpu_custom_call" | custom-call | flops 150994944 | bytes 12000000 | tf_op jit(solution)/shard_map/label_terms/pallas_call | solution.py:401
  126.4 3.5 %collective-permute-done.17.refs_4_ = bf16[384,768]{1,0:T(8,128)(2,1)S(1)} collective-permute-done((bf16[384,768]{1,0:T(8,128)(2,1)S(1)}, bf16[384,768]{1,0:T(8,128)(2,1)S(1)}, u32[]{:S(2)}, u32[]{:S(2)}) %collective-permute-start.17) | collective-permute-done | bytes 589856 | tf_op jit(solution)/shard_map/y1_3/ppermute | solution.py:34
  129.8 4.0 %project_late.3 = (bf16[192,768]{1,0:T(8,128)(2,1)S(1)}, bf16[192,768]{1,0:T(8,128)(2,1)S(1)}, bf16[192,768]{1,0:T(8,128)(2,1)S(1)}, bf16[192,768]{1,0:T(8,128)(2,1)S(1)}) custom-call(f32[768,1536]{1,0:T(8,128)} %get-tuple-element.36.refs_0_, bf16[768,1152]{1,0:T(8,128)(2,1)S(1)} %copy-done, bf16[384,768]{1,0:T(8,128)(2,1)S(1)} %collective-permute-done.16.refs_2_, ...), custom_call_target="tpu_custom_call" | custom-call | flops 1358954496 | bytes 6000000 | tf_op jit(solution)/shard_map/project_late/pallas_call | solution.py:275
  135.5 2.4 %collective-permute-start.25 = (bf16[192,768]{1,0:T(8,128)(2,1)S(1)}, bf16[192,768]{1,0:T(8,128)(2,1)S(1)}, u32[]{:S(2)}, u32[]{:S(2)}) collective-permute-start(bf16[192,768]{1,0:T(8,128)(2,1)S(1)} %get-tuple-element.52), channel_id=1, source_target_pairs={{0,12},{4,0},{8,4},{12,8},{1,13},{5,1},{9,5},{13,9},{2,14},{6,2},{... | collective-permute-start | bytes 884744 | tf_op jit(solution)/shard_map/m1_3/ppermute | solution.py:34
  140.0 3.0 %collective-permute-done.28.refs_3_ = bf16[4,3072]{1,0:T(4,128)(2,1)S(1)} collective-permute-done((bf16[4,3072]{1,0:T(4,128)(2,1)S(1)}, bf16[4,3072]{1,0:T(4,128)(2,1)S(1)}, u32[]{:S(2)}, u32[]{:S(2)}) %collective-permute-start.28) | collective-permute-done | bytes 24608 | tf_op jit(solution)/shard_map/t_2/ppermute | solution.py:34
  143.0 3.2 %collective-permute-done.29.refs_4_ = bf16[4,3072]{1,0:T(4,128)(2,1)S(1)} collective-permute-done((bf16[4,3072]{1,0:T(4,128)(2,1)S(1)}, bf16[4,3072]{1,0:T(4,128)(2,1)S(1)}, u32[]{:S(2)}, u32[]{:S(2)}) %collective-permute-start.29) | collective-permute-done | bytes 24608 | tf_op jit(solution)/shard_map/t_3/ppermute | solution.py:34
  147.3 2.3 %collective-permute-start.31 = (bf16[1,3072]{1,0:T(2,128)(2,1)S(1)}, bf16[1,3072]{1,0:T(2,128)(2,1)S(1)}, u32[]{:S(2)}, u32[]{:S(2)}) collective-permute-start(bf16[1,3072]{1,0:T(2,128)(2,1)S(1)} %get-tuple-element.60), channel_id=1, source_target_pairs={{0,8},{4,12},{8,0},{12,4},{1,9},{5,13},{9,1},{13,5},{2,10},{6,14},... | collective-permute-start | bytes 18440 | tf_op jit(solution)/shard_map/l_2/ppermute | solution.py:34
  149.5 7.3 %collective-permute-done.30.refs_2_ = bf16[1,3072]{1,0:T(2,128)(2,1)S(1)} collective-permute-done((bf16[1,3072]{1,0:T(2,128)(2,1)S(1)}, bf16[1,3072]{1,0:T(2,128)(2,1)S(1)}, u32[]{:S(2)}, u32[]{:S(2)}) %collective-permute-start.30) | collective-permute-done | bytes 6176 | tf_op jit(solution)/shard_map/l_1/ppermute | solution.py:34
  156.8 2.8 %settle.2.refs_7_ = bf16[384,1536]{1,0:T(8,128)(2,1)} custom-call(s32[3]{0:T(128)S(1)} %pad_add_fusion.refs_0_, s32[4,4]{1,0:T(4,128)S(1)} %copy-done.6, s32[4,4]{1,0:T(4,128)S(1)} %copy-done.7, bf16[192,768]{1,0:T(8,128)(2,1)S(1)} %get-tuple-element.53.refs_3_, bf16[192,768]{1,0:T(8,128)(2,1)S(1)} %collective-permute-done.21.refs_6_.refs_4_, ...), custom_call_target="tpu_custom_call" | custom-call | flops 452984832 | bytes 2000000 | tf_op jit(solution)/shard_map/settle/pallas_call | solution.py:473
  159.7 3.8 %collective-permute-done.31.refs_3_ = bf16[1,3072]{1,0:T(2,128)(2,1)S(1)} collective-permute-done((bf16[1,3072]{1,0:T(2,128)(2,1)S(1)}, bf16[1,3072]{1,0:T(2,128)(2,1)S(1)}, u32[]{:S(2)}, u32[]{:S(2)}) %collective-permute-start.31) | collective-permute-done | bytes 6176 | tf_op jit(solution)/shard_map/l_2/ppermute | solution.py:34
  165.5 2.8 %settle.3 = bf16[384,1536]{1,0:T(8,128)(2,1)} custom-call(s32[3]{0:T(128)S(1)} %pad_add_fusion.refs_0_, s32[4,4]{1,0:T(4,128)S(1)} %copy-done.6, s32[4,4]{1,0:T(4,128)S(1)} %copy-done.7, bf16[192,768]{1,0:T(8,128)(2,1)S(1)} %get-tuple-element.49.refs_3_, bf16[192,768]{1,0:T(8,128)(2,1)S(1)} %collective-permute-done.23.refs_4_, ...), custom_call_target="tpu_custom_call", output_to_operand_aliasing={{}: (7, {})} | custom-call | flops 452984832 | bytes 2000000 | tf_op jit(solution)/shard_map/settle/pallas_call | solution.py:473
  (81 shorter events, 34.6 us)
Async XLA Ops:
  2.0 19.3 %collective-permute-start = (bf16[384,768]{1,0:T(8,128)(2,1)S(1)}, bf16[384,768]{1,0:T(8,128)(2,1)S(1)}, u32[]{:S(2)}, u32[]{:S(2)}) collective-permute-start(bf16[384,768]{1,0:T(8,128)(2,1)S(1)} %get-tuple-element.63), channel_id=1, source_target_pairs={{0,4},{4,8},{8,12},{12,0},{1,5},{5,9},{9,13},{13,1},{2,6},{6,10},{... | collective-permute-start | bytes 1769480 | tf_op jit(solution)/shard_map/w0_1/ppermute | solution.py:34
  5.0 28.4 %collective-permute-start.1 = (bf16[384,768]{1,0:T(8,128)(2,1)S(1)}, bf16[384,768]{1,0:T(8,128)(2,1)S(1)}, u32[]{:S(2)}, u32[]{:S(2)}) collective-permute-start(bf16[384,768]{1,0:T(8,128)(2,1)S(1)} %get-tuple-element.62), channel_id=1, source_target_pairs={{0,4},{4,8},{8,12},{12,0},{1,5},{5,9},{9,13},{13,1},{2,6},{6,10},{... | collective-permute-start | bytes 1769480 | tf_op jit(solution)/shard_map/w1_1/ppermute | solution.py:34
  33.4 29.6 %collective-permute-start.3 = (bf16[784,768]{1,0:T(8,128)(2,1)S(1)}, bf16[784,768]{1,0:T(8,128)(2,1)S(1)}, u32[]{:S(2)}, u32[]{:S(2)}) collective-permute-start(bf16[784,768]{1,0:T(8,128)(2,1)S(1)} %get-tuple-element.33.refs_1_), channel_id=1, source_target_pairs={{0,2},{1,3},{2,0},{3,1},{4,6},{5,7},{6,4},{7,5},{8,10},{9,11},{10,... | collective-permute-start | bytes 3612680 | tf_op jit(solution)/shard_map/h_2/ppermute | solution.py:34
  35.1 18.1 %collective-permute-start.4 = (bf16[384,768]{1,0:T(8,128)(2,1)S(1)}, bf16[384,768]{1,0:T(8,128)(2,1)S(1)}, u32[]{:S(2)}, u32[]{:S(2)}) collective-permute-start(bf16[384,768]{1,0:T(8,128)(2,1)S(1)} %collective-permute-done.refs_7_.refs_6_), channel_id=1, source_target_pairs={{0,4},{4,8},{8,12},{12,0},{1,5},{5,9},{9,13},{13,1},{2,6},{6,10},{... | collective-permute-start | bytes 1769480 | tf_op jit(solution)/shard_map/w0_2/ppermute | solution.py:34
  35.1 27.8 %collective-permute-start.5 = (bf16[384,768]{1,0:T(8,128)(2,1)S(1)}, bf16[384,768]{1,0:T(8,128)(2,1)S(1)}, u32[]{:S(2)}, u32[]{:S(2)}) collective-permute-start(bf16[384,768]{1,0:T(8,128)(2,1)S(1)} %collective-permute-done.1.refs_9_), channel_id=1, source_target_pairs={{0,4},{4,8},{8,12},{12,0},{1,5},{5,9},{9,13},{13,1},{2,6},{6,10},{... | collective-permute-start | bytes 1769480 | tf_op jit(solution)/shard_map/w1_2/ppermute | solution.py:34
  36.5 26.5 %collective-permute-start.6 = (bf16[384,768]{1,0:T(8,128)(2,1)S(1)}, bf16[384,768]{1,0:T(8,128)(2,1)S(1)}, u32[]{:S(2)}, u32[]{:S(2)}) collective-permute-start(bf16[384,768]{1,0:T(8,128)(2,1)S(1)} %collective-permute-done.refs_7_.refs_6_), channel_id=1, source_target_pairs={{0,16},{16,0},{1,17},{17,1},{2,18},{18,2},{3,19},{19,3},{4,20},{20... | collective-permute-start | bytes 1769480 | tf_op jit(solution)/shard_map/y0_1/ppermute | solution.py:34
  38.0 24.9 %collective-permute-start.7 = (bf16[384,768]{1,0:T(8,128)(2,1)S(1)}, bf16[384,768]{1,0:T(8,128)(2,1)S(1)}, u32[]{:S(2)}, u32[]{:S(2)}) collective-permute-start(bf16[384,768]{1,0:T(8,128)(2,1)S(1)} %collective-permute-done.1.refs_9_), channel_id=1, source_target_pairs={{0,16},{16,0},{1,17},{17,1},{2,18},{18,2},{3,19},{19,3},{4,20},{20... | collective-permute-start | bytes 1769480 | tf_op jit(solution)/shard_map/y1_1/ppermute | solution.py:34
  63.1 21.6 %collective-permute-start.18 = (bf16[384,768]{1,0:T(8,128)(2,1)S(1)}, bf16[384,768]{1,0:T(8,128)(2,1)S(1)}, u32[]{:S(2)}, u32[]{:S(2)}) collective-permute-start(bf16[384,768]{1,0:T(8,128)(2,1)S(1)} %collective-permute-done.4.refs_8_), channel_id=1, source_target_pairs={{0,16},{16,0},{1,17},{17,1},{2,18},{18,2},{3,19},{19,3},{4,20},{20... | collective-permute-start | bytes 1769480 | tf_op jit(solution)/shard_map/y0_2/ppermute | solution.py:34
  64.6 20.0 %collective-permute-start.19 = (bf16[384,768]{1,0:T(8,128)(2,1)S(1)}, bf16[384,768]{1,0:T(8,128)(2,1)S(1)}, u32[]{:S(2)}, u32[]{:S(2)}) collective-permute-start(bf16[384,768]{1,0:T(8,128)(2,1)S(1)} %collective-permute-done.4.refs_8_), channel_id=1, source_target_pairs={{0,4},{4,8},{8,12},{12,0},{1,5},{5,9},{9,13},{13,1},{2,6},{6,10},{... | collective-permute-start | bytes 1769480 | tf_op jit(solution)/shard_map/w0_3/ppermute | solution.py:34
  67.0 15.4 %collective-permute-start.10 = (bf16[4,768]{1,0:T(4,128)(2,1)S(1)}, bf16[4,768]{1,0:T(4,128)(2,1)S(1)}, u32[]{:S(2)}, u32[]{:S(2)}) collective-permute-start(bf16[4,768]{1,0:T(4,128)(2,1)S(1)} %get-tuple-element.39), channel_id=1, source_target_pairs={{0,8},{4,12},{8,0},{12,4},{1,9},{5,13},{9,1},{13,5},{2,10},{6,14},... | collective-permute-start | bytes 18440 | tf_op jit(solution)/shard_map/g_2/ppermute | solution.py:34
  68.9 13.4 %collective-permute-start.11 = (bf16[4,768]{1,0:T(4,128)(2,1)S(1)}, bf16[4,768]{1,0:T(4,128)(2,1)S(1)}, u32[]{:S(2)}, u32[]{:S(2)}) collective-permute-start(bf16[4,768]{1,0:T(4,128)(2,1)S(1)} %get-tuple-element.40), channel_id=1, source_target_pairs={{0,12},{4,0},{8,4},{12,8},{1,13},{5,1},{9,5},{13,9},{2,14},{6,2},{... | collective-permute-start | bytes 18440 | tf_op jit(solution)/shard_map/g_3/ppermute | solution.py:34
  82.3 19.7 %collective-permute-start.12 = (bf16[384,768]{1,0:T(8,128)(2,1)S(1)}, bf16[384,768]{1,0:T(8,128)(2,1)S(1)}, u32[]{:S(2)}, u32[]{:S(2)}) collective-permute-start(bf16[384,768]{1,0:T(8,128)(2,1)S(1)} %collective-permute-done.5.refs_11_), channel_id=1, source_target_pairs={{0,4},{4,8},{8,12},{12,0},{1,5},{5,9},{9,13},{13,1},{2,6},{6,10},{... | collective-permute-start | bytes 1769480 | tf_op jit(solution)/shard_map/w1_3/ppermute | solution.py:34
  84.7 19.4 %collective-permute-start.20 = (bf16[384,768]{1,0:T(8,128)(2,1)S(1)}, bf16[384,768]{1,0:T(8,128)(2,1)S(1)}, u32[]{:S(2)}, u32[]{:S(2)}) collective-permute-start(bf16[384,768]{1,0:T(8,128)(2,1)S(1)} %collective-permute-done.19.refs_3_), channel_id=1, source_target_pairs={{0,16},{16,0},{1,17},{17,1},{2,18},{18,2},{3,19},{19,3},{4,20},{20... | collective-permute-start | bytes 1769480 | tf_op jit(solution)/shard_map/y0_3/ppermute | solution.py:34
  85.4 15.6 %collective-permute-start.13 = (bf16[16,1536]{1,0:T(8,128)(2,1)S(1)}, bf16[16,1536]{1,0:T(8,128)(2,1)S(1)}, u32[]{:S(2)}, u32[]{:S(2)}) collective-permute-start(bf16[16,1536]{1,0:T(8,128)(2,1)S(1)} %share.1.refs_1_), channel_id=1, source_target_pairs={{0,4},{4,8},{8,12},{12,0},{1,5},{5,9},{9,13},{13,1},{2,6},{6,10},{... | collective-permute-start | bytes 147464 | tf_op jit(solution)/shard_map/s_1/ppermute | solution.py:34
  86.6 15.4 %collective-permute-start.14 = (bf16[16,1536]{1,0:T(8,128)(2,1)S(1)}, bf16[16,1536]{1,0:T(8,128)(2,1)S(1)}, u32[]{:S(2)}, u32[]{:S(2)}) collective-permute-start(bf16[16,1536]{1,0:T(8,128)(2,1)S(1)} %share.1.refs_1_), channel_id=1, source_target_pairs={{0,8},{4,12},{8,0},{12,4},{1,9},{5,13},{9,1},{13,5},{2,10},{6,14},... | collective-permute-start | bytes 147464 | tf_op jit(solution)/shard_map/s_2/ppermute | solution.py:34
  89.5 12.6 %collective-permute-start.15 = (bf16[16,1536]{1,0:T(8,128)(2,1)S(1)}, bf16[16,1536]{1,0:T(8,128)(2,1)S(1)}, u32[]{:S(2)}, u32[]{:S(2)}) collective-permute-start(bf16[16,1536]{1,0:T(8,128)(2,1)S(1)} %share.1.refs_1_), channel_id=1, source_target_pairs={{0,12},{4,0},{8,4},{12,8},{1,13},{5,1},{9,5},{13,9},{2,14},{6,2},{... | collective-permute-start | bytes 147464 | tf_op jit(solution)/shard_map/s_3/ppermute | solution.py:34
  102.0 24.3 %collective-permute-start.16 = (bf16[384,768]{1,0:T(8,128)(2,1)S(1)}, bf16[384,768]{1,0:T(8,128)(2,1)S(1)}, u32[]{:S(2)}, u32[]{:S(2)}) collective-permute-start(bf16[384,768]{1,0:T(8,128)(2,1)S(1)} %collective-permute-done.5.refs_11_), channel_id=1, source_target_pairs={{0,16},{16,0},{1,17},{17,1},{2,18},{18,2},{3,19},{19,3},{4,20},{20... | collective-permute-start | bytes 1769480 | tf_op jit(solution)/shard_map/y1_2/ppermute | solution.py:34
  103.5 26.3 %collective-permute-start.17 = (bf16[384,768]{1,0:T(8,128)(2,1)S(1)}, bf16[384,768]{1,0:T(8,128)(2,1)S(1)}, u32[]{:S(2)}, u32[]{:S(2)}) collective-permute-start(bf16[384,768]{1,0:T(8,128)(2,1)S(1)} %collective-permute-done.12.refs_3_), channel_id=1, source_target_pairs={{0,16},{16,0},{1,17},{17,1},{2,18},{18,2},{3,19},{19,3},{4,20},{20... | collective-permute-start | bytes 1769480 | tf_op jit(solution)/shard_map/y1_3/ppermute | solution.py:34
  109.6 16.8 %collective-permute-start.22 = (bf16[192,768]{1,0:T(8,128)(2,1)S(1)}, bf16[192,768]{1,0:T(8,128)(2,1)S(1)}, u32[]{:S(2)}, u32[]{:S(2)}) collective-permute-start(bf16[192,768]{1,0:T(8,128)(2,1)S(1)} %get-tuple-element.48), channel_id=1, source_target_pairs={{0,12},{4,0},{8,4},{12,8},{1,13},{5,1},{9,5},{13,9},{2,14},{6,2},{... | collective-permute-start | bytes 884744 | tf_op jit(solution)/shard_map/m0_3/ppermute | solution.py:34
  111.9 35.4 %collective-permute-start.26 = (bf16[192,768]{1,0:T(8,128)(2,1)S(1)}, bf16[192,768]{1,0:T(8,128)(2,1)S(1)}, u32[]{:S(2)}, u32[]{:S(2)}) collective-permute-start(bf16[192,768]{1,0:T(8,128)(2,1)S(1)} %get-tuple-element.54), channel_id=1, source_target_pairs={{0,8},{4,12},{8,0},{12,4},{1,9},{5,13},{9,1},{13,5},{2,10},{6,14},... | collective-permute-start | bytes 884744 | tf_op jit(solution)/shard_map/m0_2/ppermute | solution.py:34
  133.8 30.9 %collective-permute-start.23 = (bf16[192,768]{1,0:T(8,128)(2,1)S(1)}, bf16[192,768]{1,0:T(8,128)(2,1)S(1)}, u32[]{:S(2)}, u32[]{:S(2)}) collective-permute-start(bf16[192,768]{1,0:T(8,128)(2,1)S(1)} %get-tuple-element.50), channel_id=1, source_target_pairs={{0,4},{4,8},{8,12},{12,0},{1,5},{5,9},{9,13},{13,1},{2,6},{6,10},{... | collective-permute-start | bytes 884744 | tf_op jit(solution)/shard_map/m1_1/ppermute | solution.py:34
  135.5 29.2 %collective-permute-start.24 = (bf16[192,768]{1,0:T(8,128)(2,1)S(1)}, bf16[192,768]{1,0:T(8,128)(2,1)S(1)}, u32[]{:S(2)}, u32[]{:S(2)}) collective-permute-start(bf16[192,768]{1,0:T(8,128)(2,1)S(1)} %get-tuple-element.51), channel_id=1, source_target_pairs={{0,8},{4,12},{8,0},{12,4},{1,9},{5,13},{9,1},{13,5},{2,10},{6,14},... | collective-permute-start | bytes 884744 | tf_op jit(solution)/shard_map/m1_2/ppermute | solution.py:34
  135.5 29.2 %collective-permute-start.25 = (bf16[192,768]{1,0:T(8,128)(2,1)S(1)}, bf16[192,768]{1,0:T(8,128)(2,1)S(1)}, u32[]{:S(2)}, u32[]{:S(2)}) collective-permute-start(bf16[192,768]{1,0:T(8,128)(2,1)S(1)} %get-tuple-element.52), channel_id=1, source_target_pairs={{0,12},{4,0},{8,4},{12,8},{1,13},{5,1},{9,5},{13,9},{2,14},{6,2},{... | collective-permute-start | bytes 884744 | tf_op jit(solution)/shard_map/m1_3/ppermute | solution.py:34
  147.3 16.2 %collective-permute-start.31 = (bf16[1,3072]{1,0:T(2,128)(2,1)S(1)}, bf16[1,3072]{1,0:T(2,128)(2,1)S(1)}, u32[]{:S(2)}, u32[]{:S(2)}) collective-permute-start(bf16[1,3072]{1,0:T(2,128)(2,1)S(1)} %get-tuple-element.60), channel_id=1, source_target_pairs={{0,8},{4,12},{8,0},{12,4},{1,9},{5,13},{9,1},{13,5},{2,10},{6,14},... | collective-permute-start | bytes 18440 | tf_op jit(solution)/shard_map/l_2/ppermute | solution.py:34
  (21 other events, 165.8 us)

commit v3 on v2

--- a/solution.py
+++ b/solution.py
@@ -9,7 +9,8 @@
 
 TOK = 384
 CHUNKS = 2
-VMEM_BYTES = 48 * 1024 * 1024
+VMEM_BYTES = 24 * 1024 * 1024
+EARLY_FLOPS = 4_000_000_000
 
 
 EPSILON = 1e-06
@@ -147,94 +148,99 @@
     )(place, counts, plan, qkv, resid, query_gain, key_gain, *after)
 
 
-def early_kernel(rows, chunks, place_ref, *refs):
+def early_kernel(rows, with_late, place_ref, *refs):
     head_refs = refs[:rows]
-    own_ref = refs[rows]
-    piece_refs = refs[rows + 1 : rows + 1 + 3 * chunks]
-    resid_ref, total_ref, late_ref = refs[rows + 1 + 3 * chunks :][:3]
+    own_ref, *piece_refs = refs[rows : rows + 4]
+    resid_ref, means_ref = refs[rows + 4 : rows + 6]
     held_ref, weight_ref, head_sems, weight_sems, late_sem = refs[-5:]
+    total_ref, late_ref = refs[-7:-5] if with_late else (refs[-6], None)
     my_row, my_part, my_group = place_ref[0], place_ref[1], place_ref[2]
     tiles, used, tile = weight_ref.shape
-    depth = held_ref.shape[1] // rows
+    depth = head_refs[0].shape[1]
     half = depth // 2
 
-    def head_copies():
-        copies = []
+    def head_copies(act):
         for x in range(rows):
             step = lax.rem(my_row - (x ^ my_part) + rows, rows)
             for s in range(2):
                 turned = jnp.where(step == 0, s, s ^ my_group)
                 start = pl.multiple_of(step * depth + turned * half, 128)
-                copies.append(
-                    pltpu.make_async_copy(
-                        head_refs[x].at[: held_ref.shape[0], s * half : (s + 1) * half],
-                        held_ref.at[:, pl.ds(start, half)],
-                        head_sems.at[x, s],
-                    )
+                copy = pltpu.make_async_copy(
+                    head_refs[x].at[: held_ref.shape[0], s * half : (s + 1) * half],
+                    held_ref.at[:, pl.ds(start, half)],
+                    head_sems.at[x, s],
                 )
-        return copies
-
-    def weight_copies(i):
-        chunk, column = i * chunks // tiles, i % (tiles // chunks) * tile
-        sources = [own_ref.at[:, i * tile : (i + 1) * tile]]
-        sources += [piece_refs[3 * chunk + n].at[:, column : column + tile] for n in range(3)]
+                act(copy)
+
+    def weight_copies(i, act):
+        column = i * tile
+        sources = [own_ref.at[:, column : column + tile]]
+        sources += [piece_ref.at[:, column : column + tile] for piece_ref in piece_refs]
         starts = [0, depth, depth + half, depth + 2 * half]
-        return [
-            pltpu.make_async_copy(
-                source, weight_ref.at[i, pl.ds(start, source.shape[0])], weight_sems.at[i, n]
+        for n, (source, start) in enumerate(zip(sources, starts)):
+            act(
+                pltpu.make_async_copy(
+                    source, weight_ref.at[i, pl.ds(start, source.shape[0])], weight_sems.at[i, n]
+                )
             )
-            for n, (source, start) in enumerate(zip(sources, starts))
-        ]
 
     i = pl.program_id(0)
-    late_copy = pltpu.make_async_copy(held_ref.at[:, used:], late_ref, late_sem)
 
     @pl.when(i == 0)
     def _():
-        for copy in head_copies():
-            copy.start()
+        head_copies(lambda copy: copy.start())
         for j in range(tiles):
-            for copy in weight_copies(j):
-                copy.start()
-        for copy in head_copies():
-            copy.wait()
-        late_copy.start()
+            weight_copies(j, lambda copy: copy.start())
+        head_copies(lambda copy: copy.wait())
+        if with_late:
+            pltpu.make_async_copy(held_ref.at[:, used:], late_ref, late_sem).start()
 
     for j in range(tiles):
 
         @pl.when(i == j)
         def _():
-            for copy in weight_copies(j):
-                copy.wait()
+            weight_copies(j, lambda copy: copy.wait())
 
     length = resid_ref.shape[0]
     for start in range(0, length, 256):
-        lines = slice(start, min(start + 256, length))
+        added = min(256, length - start)
+        last = start + added == length
+        lines = slice(start, None if last else start + added)
         total = dot32(held_ref[lines, :used], weight_ref[i])
-        total_ref[lines] = total + resid_ref[lines].astype(jnp.float32)
-
-    @pl.when(i == tiles - 1)
-    def _():
-        late_copy.wait()
-
-
-def project_early(place, heads, out_weight, pieces, resid):
-    rows, chunks = len(heads), len(pieces)
-    length, features = resid.shape
-    depth = heads[0].shape[1]
+        lines = slice(start, start + added)
+        total_ref[lines] = total[:added] + resid_ref[lines].astype(jnp.float32)
+        if last:
+            total_ref[length:] = total[added:] + means_ref[...]
+
+    if with_late:
+
+        @pl.when(i == tiles - 1)
+        def _():
+            pltpu.make_async_copy(held_ref.at[:, used:], late_ref, late_sem).wait()
+
+
+def project_early(place, heads, own, pieces, resid, means, chunk, with_late, after):
+    rows = len(heads)
+    length, depth = heads[0].shape
+    width = pieces[0].shape[1]
     used = depth * 5 // 2
     tile = 256
-    tiles = features // tile
-    flat = [piece for chunk in pieces for piece in chunk[:3]]
+    tiles = width // tile
     anywhere = pl.BlockSpec(memory_space=pl.ANY)
-    column = lambda x: pl.BlockSpec((x, tile), lambda i: (0, i))
+    late = [jax.ShapeDtypeStruct((length, rows * depth - used), jnp.bfloat16)] if with_late else []
     return pl.pallas_call(
-        lambda *refs: early_kernel(rows, chunks, *refs),
+        lambda place_ref, *refs: early_kernel(
+            rows, with_late, place_ref, *refs[: rows + 6], *refs[rows + 6 + len(after) :]
+        ),
         grid=(tiles,),
         in_specs=[pl.BlockSpec(memory_space=pltpu.SMEM)]
-        + [anywhere] * (rows + 1 + len(flat))
-        + [column(length)],
-        out_specs=[column(length), anywhere],
+        + [anywhere] * (rows + 4)
+        + [
+            pl.BlockSpec((x.shape[0], tile), lambda i: (0, chunk * tiles + i))
+            for x in (resid, means)
+        ]
+        + [anywhere] * len(after),
+        out_specs=[pl.BlockSpec((length, tile), lambda i: (0, i))] + [anywhere] * len(late),
         scratch_shapes=[
             pltpu.VMEM((length, rows * depth), jnp.bfloat16),
             pltpu.VMEM((tiles, used, tile), jnp.bfloat16),
@@ -242,16 +248,13 @@
             pltpu.SemaphoreType.DMA((tiles, 4)),
             pltpu.SemaphoreType.DMA,
         ],
-        out_shape=[
-            jax.ShapeDtypeStruct((length, features), jnp.float32),
-            jax.ShapeDtypeStruct((length, rows * depth - used), jnp.bfloat16),
-        ],
+        out_shape=[jax.ShapeDtypeStruct((length, width), jnp.float32)] + late,
         compiler_params=pltpu.CompilerParams(vmem_limit_bytes=VMEM_BYTES),
         cost_estimate=pl.CostEstimate(
-            flops=2 * length * used * features, bytes_accessed=12_000_000, transcendentals=0
+            flops=EARLY_FLOPS, bytes_accessed=1000, transcendentals=0
         ),
         name="project_early",
-    )(place, *heads, out_weight, *flat, resid)
+    )(place, *heads, own, *pieces, resid, means, *after)
 
 
 def late_kernel(rows, total_ref, late_ref, *refs):
@@ -266,17 +269,47 @@
         out_refs[k][...] = total.astype(jnp.bfloat16)
 
 
-def project_late(total, late, pieces, chunk, rows, span, after):
+def pool_kernel(rows, chunks, *refs):
+    late_ref, total_refs = refs[0], refs[1 : 1 + chunks]
+    piece_refs, pooled_ref = refs[1 + chunks : -1], refs[-1]
+    half, width = piece_refs[0].shape
+    for c in range(chunks):
+        total = total_refs[c][...]
+        for n in range(3):
+            columns = slice(n * half, (n + 1) * half)
+            total = total + dot32(late_ref[:, columns], piece_refs[3 * c + n][...])
+        pooled_ref[:, c * width : (c + 1) * width] = total[:rows].astype(jnp.bfloat16)
+
+
+def project_pooled(totals, late, pieces, rows, start):
+    chunks = len(totals)
+    extra = late.shape[0] - start
+    width = totals[0].shape[1]
+    flat = [piece for chunk in pieces for piece in chunk]
+    whole = lambda x: pl.BlockSpec(x.shape, lambda i: (0, 0))
+    tail = lambda x: pl.BlockSpec((extra, x.shape[1]), lambda i: (start // extra, 0))
+    return pl.pallas_call(
+        lambda *refs: pool_kernel(rows, chunks, *refs),
+        grid=(1,),
+        in_specs=[tail(late)] + [tail(x) for x in totals] + [whole(x) for x in flat],
+        out_specs=pl.BlockSpec((rows, chunks * width), lambda i: (0, 0)),
+        out_shape=jax.ShapeDtypeStruct((rows, chunks * width), jnp.bfloat16),
+        compiler_params=pltpu.CompilerParams(vmem_limit_bytes=VMEM_BYTES),
+        cost_estimate=pl.CostEstimate(flops=1000, bytes_accessed=1000, transcendentals=0),
+        name="project_pooled",
+    )(late, *totals, *flat)
+
+
+def project_late(total, late, pieces, rows, span, after):
     half, width = pieces[0].shape
     length = total.shape[0]
     tile = 256
     tiles = width // tile
-    first = chunk * tiles
     return pl.pallas_call(
         lambda *refs: late_kernel(rows, *refs),
         grid=(tiles,),
         in_specs=[
-            pl.BlockSpec((length, tile), lambda i: (0, first + i)),
+            pl.BlockSpec((length, tile), lambda i: (0, i)),
             pl.BlockSpec(late.shape, lambda i: (0, 0)),
         ]
         + [pl.BlockSpec((half, tile), lambda i: (0, i))] * 3
@@ -293,61 +326,6 @@
 
 def one_hot(hits):
     return hits.astype(jnp.float32).astype(jnp.bfloat16)
-
-
-def parts_kernel(rows, start, place_ref, *refs):
-    head_refs, out_refs = refs[:rows], refs[rows : 2 * rows]
-    tail_ref, sems = refs[2 * rows :]
-    copies = [
-        pltpu.make_async_copy(
-            head_refs[x].at[start : start + tail_ref.shape[1]], tail_ref.at[x], sems.at[x]
-        )
-        for x in range(rows)
-    ]
-    for copy in copies:
-        copy.start()
-    for copy in copies:
-        copy.wait()
-    for k in range(rows):
-        row = lax.rem(place_ref[0] + k, rows)
-        out_refs[k][...] = tail_ref[row ^ place_ref[1]][:rows]
-
-
-def head_parts(place, heads, start):
-    rows, (length, depth) = len(heads), heads[0].shape
-    return pl.pallas_call(
-        lambda *refs: parts_kernel(rows, start, *refs),
-        in_specs=[pl.BlockSpec(memory_space=pltpu.SMEM)]
-        + [pl.BlockSpec(memory_space=pl.ANY)] * rows,
-        out_specs=[pl.BlockSpec(memory_space=pltpu.VMEM)] * rows,
-        out_shape=[jax.ShapeDtypeStruct((rows, depth), jnp.bfloat16)] * rows,
-        scratch_shapes=[
-            pltpu.VMEM((rows, length - start, depth), jnp.bfloat16),
-            pltpu.SemaphoreType.DMA((rows,)),
-        ],
-        cost_estimate=pl.CostEstimate(flops=1000, bytes_accessed=1000, transcendentals=0),
-        compiler_params=pltpu.CompilerParams(vmem_limit_bytes=VMEM_BYTES),
-        name="head_parts",
-    )(place, *heads)
-
-
-def share_kernel(rows, place_ref, *refs):
-    got_refs = refs[:rows]
-    weight_ref, resid_ref = refs[rows : rows + 2]
-    share_ref = refs[-1]
-    my_row = place_ref[0]
-    count = rows * rows
-    image = lax.broadcasted_iota(jnp.int32, (count, rows), 0)
-    entry = lax.broadcasted_iota(jnp.int32, (count, rows), 1)
-    got = None
-    for k in range(rows):
-        row = lax.rem(my_row - k + rows, rows)
-        term = dot32(one_hot(image == row * rows + entry), got_refs[k][...])
-        got = term if got is None else got + term
-    mine = lax.broadcasted_iota(jnp.int32, (count, 1), 0) // rows == my_row
-    resid = jnp.concatenate([resid_ref[:rows]] * rows, axis=0)
-    share = dot32(got.astype(jnp.bfloat16), weight_ref[...]) + jnp.where(mine, resid, 0.0)
-    share_ref[...] = share.astype(jnp.bfloat16)
 
 
 def local_call(kernel, out_shape, operands, after, place, name, flops):
@@ -370,7 +348,7 @@
 
 
 def terms_kernel(rows, place_ref, *refs):
-    share_refs = refs[:rows]
+    pooled_refs = refs[:rows]
     weight_ref = refs[rows]
     out_refs = refs[-rows - 1 : -1]
     pooled_ref = refs[-1]
@@ -378,44 +356,46 @@
 
     @pl.when(pl.program_id(0) == 0)
     def _():
-        pooled = share_refs[0][...].astype(jnp.float32)
-        for k in range(1, rows):
-            pooled = pooled + share_refs[k][...].astype(jnp.float32)
-        wanted = lax.broadcasted_iota(jnp.int32, (count, count), 0)
-        image = lax.broadcasted_iota(jnp.int32, (count, count), 1)
+        wanted = lax.broadcasted_iota(jnp.int32, (count, rows), 0)
+        image = lax.broadcasted_iota(jnp.int32, (count, rows), 1)
         part = wanted // rows ^ place_ref[1]
-        order = one_hot(image == wanted % rows * rows + part)
-        pooled_ref[...] = dot32(order, pooled.astype(jnp.bfloat16)).astype(jnp.bfloat16)
+        pooled = None
+        for k in range(rows):
+            row = lax.rem(place_ref[0] - k + rows, rows)
+            order = one_hot((wanted % rows == row) & (image == part))
+            term = dot32(order, pooled_refs[k][...])
+            pooled = term if pooled is None else pooled + term
+        pooled_ref[...] = pooled.astype(jnp.bfloat16)
 
     terms = dot32(pooled_ref[...], weight_ref[...]).astype(jnp.bfloat16)
     for k in range(rows):
         out_refs[k][...] = terms[k * rows : (k + 1) * rows]
 
 
-def label_terms_by_part(place, shares, label_weight, after):
-    rows = len(shares)
-    count, features = shares[0].shape
-    classes = label_weight.shape[1]
+def label_terms_by_part(place, pooled, label_weight, after):
+    rows = len(pooled)
+    features, classes = label_weight.shape
     tile = 512
-    fixed = pl.BlockSpec((count, features), lambda i, *_: (0, 0))
     return pl.pallas_call(
         lambda *refs: terms_kernel(rows, *refs),
         grid_spec=pltpu.PrefetchScalarGridSpec(
             num_scalar_prefetch=1,
             grid=(classes // tile,),
-            in_specs=[fixed] * rows
+            in_specs=[pl.BlockSpec(x.shape, lambda i, *_: (0, 0)) for x in pooled]
             + [pl.BlockSpec((features, tile), lambda i, *_: (0, i))]
             + [pl.BlockSpec(memory_space=pl.ANY)] * len(after),
             out_specs=[pl.BlockSpec((rows, tile), lambda i, *_: (0, i))] * rows,
-            scratch_shapes=[pltpu.VMEM((count, features), jnp.bfloat16)],
+            scratch_shapes=[pltpu.VMEM((rows * rows, features), jnp.bfloat16)],
         ),
         out_shape=[jax.ShapeDtypeStruct((rows, classes), jnp.bfloat16)] * rows,
         compiler_params=pltpu.CompilerParams(vmem_limit_bytes=VMEM_BYTES),
         cost_estimate=pl.CostEstimate(
-            flops=2 * count * features * classes, bytes_accessed=12_000_000, transcendentals=0
+            flops=2 * rows * rows * features * classes,
+            bytes_accessed=12_000_000,
+            transcendentals=0,
         ),
         name="label_terms",
-    )(place, *shares, label_weight, *after)
+    )(place, *pooled, label_weight, *after)
 
 
 def probs_kernel(rows, place_ref, *refs):
@@ -529,9 +509,9 @@
         query_gain[None],
         key_gain[None],
         span,
-        moving[:1],
-    )
-    heads = after_all([heads], moving[1:])[0]
+        [],
+    )
+    heads = after_all([heads], moving)[0]
     across = send(heads, "mp", crossed(parts, 2), "h_2")
     beside = send(heads, "mp", crossed(parts, 1), "h_1")
 
@@ -544,44 +524,49 @@
     beyond = send(turned, "mp", crossed(parts, 1), "h_3")
     every_head = [heads, beside, across, beyond]
 
-    gathered = head_parts(place, every_head, rows * span)
-    gathered = [gathered[0]] + [
-        send(gathered[k], "dp", shifted(rows, k), f"g_{k}") for k in range(1, rows)
-    ]
-    image_count = rows * rows
-    share = local_call(
-        lambda *refs: share_kernel(rows, *refs),
-        jax.ShapeDtypeStruct((image_count, features), jnp.bfloat16),
-        [*gathered, out_weight, resid_means],
-        [],
-        place,
-        "share",
-        1000,
-    )
-    shares = [share] + [send(share, "dp", shifted(rows, k), f"s_{k}") for k in range(1, rows)]
-
-    total, late = project_early(place, every_head, out_weight, pieces, resid)
-    pieces, moving = [], following
+    totals, late, early, moving = [], None, pieces, following
+    pieces = []
     for c in range(CHUNKS):
-        x = after_all([moving[c]], [total, *gathered[1:]])[0] if c else moving[c]
+        after = totals
+        x = after_all([moving[c]], after)[0] if c else moving[c]
         x = send(x, "dp", shifted(rows, 1), f"w{c}_3")
-        y = after_all([moving[c]], [x, *shares[1:]])[0] if c else moving[c]
+        total, *more = project_early(
+            place,
+            every_head,
+            out_weight[:, c * width : (c + 1) * width],
+            early[c],
+            resid,
+            resid_means,
+            c,
+            c == 0,
+            [totals[0], pieces[0][1]] if c else [],
+        )
+        totals.append(total)
+        late = more[0] if more else late
+        y = after_all([moving[c]], [x, total, pieces[0][2]])[0] if c else moving[c]
         y = send(y, "groups", crossed(sharers, 1), f"y{c}_2")
-        z = after_all([x], [y, total, share])[0] if c == 0 else x
+        z = after_all([x], [total] if c else [total, y])[0]
         z = send(z, "groups", crossed(sharers, 1), f"y{c}_3")
         pieces.append([y, x, z])
 
-    classes = label_weight.shape[1]
     arrived = []
     for c in range(CHUNKS):
-        after = [terms[0], arrived[0][3]] if c else shares[1:]
-        blocks = project_late(total, late, pieces[c], c, rows, span, after)
+        if c == CHUNKS - 1:
+            pooled = project_pooled(totals, late, pieces, rows, rows * span)
+            pooled = [pooled] + [
+                send(pooled, "dp", shifted(rows, k), f"p_{k}") for k in range(1, rows)
+            ]
+        blocks = project_late(
+            totals[c], late, pieces[c], rows, span, arrived[0][1:] if c else []
+        )
+        if c == CHUNKS - 1:
+            blocks = after_all(blocks, pooled[1:])
         arrived.append(
             [blocks[0]] + [send(blocks[k], "dp", shifted(rows, k), f"m{c}_{k}") for k in range(1, rows)]
         )
-        if c == 0:
-            terms = label_terms_by_part(place, shares, label_weight, arrived[0][1:2])
-
+
+    classes = label_weight.shape[1]
+    terms = label_terms_by_part(place, pooled, label_weight, [])
     terms = [terms[0]] + [
         send(terms[k], "mp", crossed(parts, k), f"t_{k}") for k in range(1, parts)
     ]
@@ -606,8 +591,7 @@
     )
     mixed = None
     for c in range(CHUNKS):
-        after = [labels] if c == CHUNKS - 1 else []
-        mixed = settle(place, patch_counts, move_plan, arrived[c], c, features, mixed, after)
+        mixed = settle(place, patch_counts, move_plan, arrived[c], c, features, mixed, [])
     labels = labels[None]
     return (mixed[None], labels)
 

time: 169 us -> 162 us (0.959)
  waiting for transfers between devices: 74.6 us -> 86.3 us
  Pallas kernels: 45.9 us -> 35.2 us
  local copies, waits for them, and re-layouts: 10.1 us -> 4.83 us
  starting transfers between devices: 36.9 us -> 34.6 us
    ppermute x33 -> x30, waiting for transfers between devices: 74.6 us -> 86.3 us  [send(): return lax.ppermute(values, axis, pairs)]
    pallas_call x1, Pallas kernels: 6.55 us -> 3.31 us  [label_terms_by_part(): pl.pallas_call(lambda *refs: terms_kernel(rows, *refs), grid_spec=pltpu.P...]
    pallas_call x1, Pallas kernels: 10.7 us -> 7.56 us  [attend(): pl.pallas_call(lambda *refs: attend_kernel(rows, span, *refs), grid_spec=...]
    pallas_call x2, Pallas kernels: 7.88 us -> 5.52 us  [project_late(): pl.pallas_call(lambda *refs: late_kernel(rows, *refs), grid=(tiles,), in_...]
    ppermute x33 -> x30, starting transfers between devices: 36.9 us -> 34.6 us  [send(): return lax.ppermute(values, axis, pairs)]
    pad x1, local copies, waits for them, and re-layouts: 4.49 us -> 2.44 us  [on_device_rings(): jnp.pad(jnp.transpose(qkv_home[0], (1, 0, 2)), ((0, 0), (0, padded - slot...]
    unnamed x24 -> x20, local copies, waits for them, and re-layouts: 2.52 us -> 0.72 us
    pallas_call x2 -> x3, Pallas kernels: 12.1 us -> 11.3 us  [the longest x2 10.7 us: project_early(): pl.pallas_call(lambda place_ref, *refs: early_kernel(rows, with_late, pla...]
  transfers between devices with their start and end apart: 33 -> 30, of which waited for: 13 -> 16; matrix products, arithmetic and copies ran while one was open for 4% -> 2% of each run, Pallas kernels for 26% -> 20%
where the time goes in v3:
time: 162 us
  waiting for transfers between devices  86.3 us (53%)
  Pallas kernels  35.2 us (22%)
  starting transfers between devices  34.6 us (21%)
  local copies, waits for them, and re-layouts  4.83 us (3%)
    ppermute x30, waiting for transfers between devices, send(): return lax.ppermute(values, axis, pairs)  86.3 us
    ppermute x30, starting transfers between devices, send(): return lax.ppermute(values, axis, pairs)  34.6 us
    pallas_call x2, Pallas kernels, project_early(): pl.pallas_call(lambda place_ref, *refs: early_kernel(rows, with_late, pla...  10.7 us
    pallas_call x1, Pallas kernels, attend(): pl.pallas_call(lambda *refs: attend_kernel(rows, span, *refs), grid_spec=...  7.56 us
    pallas_call x2, Pallas kernels, settle(): pl.pallas_call(lambda *refs: settle_kernel(rows, *refs), grid_spec=pltpu....  5.67 us
    pallas_call x2, Pallas kernels, project_late(): pl.pallas_call(lambda *refs: late_kernel(rows, *refs), grid=(tiles,), in_...  5.52 us
    pallas_call x1, Pallas kernels, label_terms_by_part(): pl.pallas_call(lambda *refs: terms_kernel(rows, *refs), grid_spec=pltpu.P...  3.31 us
  transfers between devices with their start and end apart: 30, of which 16 were waited for; matrix products, arithmetic and copies ran while one was open for 2% of the time, Pallas kernels for 20%

profile of v3, /device:TPU:0, one launch (start us, length us, event | category | flops | bytes accessed | tf_op | source)
XLA Modules:
  0.0 161.9 jit_solution(1573903810306000286)
XLA Ops:
  2.0 3.1 %collective-permute-start = (bf16[384,768]{1,0:T(8,128)(2,1)S(1)}, bf16[384,768]{1,0:T(8,128)(2,1)S(1)}, u32[]{:S(2)}, u32[]{:S(2)}) collective-permute-start(bf16[384,768]{1,0:T(8,128)(2,1)S(1)} %get-tuple-element.67), channel_id=1, source_target_pairs={{0,4},{4,8},{8,12},{12,0},{1,5},{5,9},{9,13},{13,1},{2,6},{6,10},{... | collective-permute-start | bytes 1769480 | tf_op jit(solution)/shard_map/w0_1/ppermute | solution.py:35
  6.6 2.4 %pad.8.refs_3_ = bf16[3,960,768]{2,1,0:T(8,128)(2,1)S(1)} pad(bf16[3,764,768]{2,1,0:T(8,128)(2,1)} %bitcast.18, bf16[]{:T(256)} %constant.17.clone.1), padding=0_0x0_196x0_0 | pad | bytes 7944194 | tf_op jit(solution)/shard_map/jit(_pad)/pad | solution.py:502
  10.1 7.6 %attend.1 = (bf16[784,768]{1,0:T(8,128)(2,1)S(1)}, bf16[768,1536]{1,0:T(8,128)(2,1)S(1)}, f32[16,1536]{1,0:T(8,128)S(1)}) custom-call(s32[3]{0:T(128)S(1)} %pad_add_fusion.refs_0_.place_ref, s32[4,4]{1,0:T(4,128)S(1)} %copy-done.1, s32[4,4]{1,0:T(4,128)S(1)} %copy-done.2, bf16[3,960,768]{2,1,0:T(8,128)(2,1)S(1)} %pad.8.refs_3_, ...), custom_call_target="tpu_custom_call" | custom-call | flops 10000000000 | bytes 12000000 | tf_op jit(solution)/shard_map/attend/pallas_call | solution.py:124
  17.6 3.6 %collective-permute-done.refs_5_ = bf16[384,768]{1,0:T(8,128)(2,1)S(1)} collective-permute-done((bf16[384,768]{1,0:T(8,128)(2,1)S(1)}, bf16[384,768]{1,0:T(8,128)(2,1)S(1)}, u32[]{:S(2)}, u32[]{:S(2)}) %collective-permute-start) | collective-permute-done | bytes 589856 | tf_op jit(solution)/shard_map/w0_1/ppermute | solution.py:35
  21.2 11.8 %collective-permute-done.1.refs_5_ = bf16[384,768]{1,0:T(8,128)(2,1)S(1)} collective-permute-done((bf16[384,768]{1,0:T(8,128)(2,1)S(1)}, bf16[384,768]{1,0:T(8,128)(2,1)S(1)}, u32[]{:S(2)}, u32[]{:S(2)}) %collective-permute-start.1) | collective-permute-done | bytes 589856 | tf_op jit(solution)/shard_map/w1_1/ppermute | solution.py:35
  37.8 14.7 %collective-permute-done.4.refs_7_ = bf16[384,768]{1,0:T(8,128)(2,1)S(1)} collective-permute-done((bf16[384,768]{1,0:T(8,128)(2,1)S(1)}, bf16[384,768]{1,0:T(8,128)(2,1)S(1)}, u32[]{:S(2)}, u32[]{:S(2)}) %collective-permute-start.4) | collective-permute-done | bytes 589856 | tf_op jit(solution)/shard_map/w0_2/ppermute | solution.py:35
  52.6 10.4 %collective-permute-done.5.refs_7_ = bf16[384,768]{1,0:T(8,128)(2,1)S(1)} collective-permute-done((bf16[384,768]{1,0:T(8,128)(2,1)S(1)}, bf16[384,768]{1,0:T(8,128)(2,1)S(1)}, u32[]{:S(2)}, u32[]{:S(2)}) %collective-permute-start.5) | collective-permute-done | bytes 589856 | tf_op jit(solution)/shard_map/w1_2/ppermute | solution.py:35
  65.9 5.5 %project_early.2 = (f32[784,768]{1,0:T(8,128)S(1)}, bf16[784,1152]{1,0:T(8,128)(2,1)S(1)}) custom-call(s32[3]{0:T(128)S(1)} %pad_add_fusion.refs_0_.place_ref, bf16[784,768]{1,0:T(8,128)(2,1)S(1)} %get-tuple-element.34.refs_0_, bf16[784,768]{1,0:T(8,128)(2,1)S(1)} %collective-permute-done.2.refs_1_, bf16[784,768]{1,0:T(8,128)(2,1)S(1)} %collective-permute-done.3.refs_2_, ...), custom_call_target="tpu_custom_call" | custom-call | flops 4000000000 | bytes 1000 | tf_op jit(solution)/shard_map/project_early/pallas_call | solution.py:231
  72.8 8.2 %collective-permute-done.9.refs_11_.refs_3_.refs_4_ = bf16[384,768]{1,0:T(8,128)(2,1)S(1)} collective-permute-done((bf16[384,768]{1,0:T(8,128)(2,1)S(1)}, bf16[384,768]{1,0:T(8,128)(2,1)S(1)}, u32[]{:S(2)}, u32[]{:S(2)}) %collective-permute-start.9) | collective-permute-done | bytes 589856 | tf_op jit(solution)/shard_map/w0_3/ppermute | solution.py:35
  82.5 5.2 %project_early.3.refs_0_.refs_2_ = f32[784,768]{1,0:T(8,128)S(1)} custom-call(s32[3]{0:T(128)S(1)} %pad_add_fusion.refs_0_.place_ref, bf16[784,768]{1,0:T(8,128)(2,1)S(1)} %get-tuple-element.34.refs_0_, bf16[784,768]{1,0:T(8,128)(2,1)S(1)} %collective-permute-done.2.refs_1_, bf16[784,768]{1,0:T(8,128)(2,1)S(1)} %collective-permute-done.3.refs_2_, ...), custom_call_target="tpu_custom_call" | custom-call | flops 4000000000 | bytes 1000 | tf_op jit(solution)/shard_map/project_early/pallas_call | solution.py:231
  87.8 5.4 %collective-permute-done.10.refs_3_.refs_7_ = bf16[384,768]{1,0:T(8,128)(2,1)S(1)} collective-permute-done((bf16[384,768]{1,0:T(8,128)(2,1)S(1)}, bf16[384,768]{1,0:T(8,128)(2,1)S(1)}, u32[]{:S(2)}, u32[]{:S(2)}) %collective-permute-start.10) | collective-permute-done | bytes 589856 | tf_op jit(solution)/shard_map/w1_3/ppermute | solution.py:35
  97.0 2.8 %project_late.2 = (bf16[192,768]{1,0:T(8,128)(2,1)S(1)}, bf16[192,768]{1,0:T(8,128)(2,1)S(1)}, bf16[192,768]{1,0:T(8,128)(2,1)S(1)}, bf16[192,768]{1,0:T(8,128)(2,1)S(1)}) custom-call(f32[784,768]{1,0:T(8,128)S(1)} %get-tuple-element.38.refs_10_.refs_0_.refs_1_, bf16[784,1152]{1,0:T(8,128)(2,1)S(1)} %get-tuple-element.39.refs_1_.refs_0_, ...), custom_call_target="tpu_custom_call" | custom-call | flops 1387266048 | bytes 6000000 | tf_op jit(solution)/shard_map/project_late/pallas_call | solution.py:308
  103.9 5.5 %collective-permute-done.14.refs_4_.refs_8_ = bf16[384,768]{1,0:T(8,128)(2,1)S(1)} collective-permute-done((bf16[384,768]{1,0:T(8,128)(2,1)S(1)}, bf16[384,768]{1,0:T(8,128)(2,1)S(1)}, u32[]{:S(2)}, u32[]{:S(2)}) %collective-permute-start.14) | collective-permute-done | bytes 589856 | tf_op jit(solution)/shard_map/y1_3/ppermute | solution.py:35
  109.5 11.3 %collective-permute-done.13.refs_2_.refs_6_ = bf16[384,768]{1,0:T(8,128)(2,1)S(1)} collective-permute-done((bf16[384,768]{1,0:T(8,128)(2,1)S(1)}, bf16[384,768]{1,0:T(8,128)(2,1)S(1)}, u32[]{:S(2)}, u32[]{:S(2)}) %collective-permute-start.13) | collective-permute-done | bytes 589856 | tf_op jit(solution)/shard_map/y1_2/ppermute | solution.py:35
  125.2 2.8 %project_late.3 = (bf16[192,768]{1,0:T(8,128)(2,1)S(1)}, bf16[192,768]{1,0:T(8,128)(2,1)S(1)}, bf16[192,768]{1,0:T(8,128)(2,1)S(1)}, bf16[192,768]{1,0:T(8,128)(2,1)S(1)}) custom-call(f32[784,768]{1,0:T(8,128)S(1)} %project_early.3.refs_0_.refs_2_, bf16[784,1152]{1,0:T(8,128)(2,1)S(1)} %get-tuple-element.39.refs_1_.refs_0_, ...), custom_call_target="tpu_custom_call" | custom-call | flops 1387266048 | bytes 6000000 | tf_op jit(solution)/shard_map/project_late/pallas_call | solution.py:308
  128.0 3.0 %collective-permute-start.21 = (bf16[192,768]{1,0:T(8,128)(2,1)S(1)}, bf16[192,768]{1,0:T(8,128)(2,1)S(1)}, u32[]{:S(2)}, u32[]{:S(2)}) collective-permute-start(bf16[192,768]{1,0:T(8,128)(2,1)S(1)} %get-tuple-element.52), channel_id=1, source_target_pairs={{0,4},{4,8},{8,12},{12,0},{1,5},{5,9},{9,13},{13,1},{2,6},{6,10},{... | collective-permute-start | bytes 884744 | tf_op jit(solution)/shard_map/m1_1/ppermute | solution.py:35
  131.2 2.2 %collective-permute-start.23 = (bf16[192,768]{1,0:T(8,128)(2,1)S(1)}, bf16[192,768]{1,0:T(8,128)(2,1)S(1)}, u32[]{:S(2)}, u32[]{:S(2)}) collective-permute-start(bf16[192,768]{1,0:T(8,128)(2,1)S(1)} %get-tuple-element.54), channel_id=1, source_target_pairs={{0,12},{4,0},{8,4},{12,8},{1,13},{5,1},{9,5},{13,9},{2,14},{6,2},{... | collective-permute-start | bytes 884744 | tf_op jit(solution)/shard_map/m1_3/ppermute | solution.py:35
  133.4 3.3 %label_terms.1 = (bf16[4,3072]{1,0:T(4,128)(2,1)S(1)}, bf16[4,3072]{1,0:T(4,128)(2,1)S(1)}, bf16[4,3072]{1,0:T(4,128)(2,1)S(1)}, bf16[4,3072]{1,0:T(4,128)(2,1)S(1)}) custom-call(s32[3]{0:T(128)S(1)} %pad_add_fusion.refs_0_.place_ref, bf16[4,1536]{1,0:T(4,128)(2,1)S(1)} %project_pooled.1.refs_1_, bf16[4,1536]{1,0:T(4,128)(2,1)S(1)} %collective-permute-done.18.refs_2_, ...), custom_call_target="tpu_custom_call" | custom-call | flops 150994944 | bytes 12000000 | tf_op jit(solution)/shard_map/label_terms/pallas_call | solution.py:379
  138.6 2.0 %collective-permute-done.25.refs_3_ = bf16[4,3072]{1,0:T(4,128)(2,1)S(1)} collective-permute-done((bf16[4,3072]{1,0:T(4,128)(2,1)S(1)}, bf16[4,3072]{1,0:T(4,128)(2,1)S(1)}, u32[]{:S(2)}, u32[]{:S(2)}) %collective-permute-start.25) | collective-permute-done | bytes 24608 | tf_op jit(solution)/shard_map/t_2/ppermute | solution.py:35
  142.0 2.5 %collective-permute-start.28 = (bf16[1,3072]{1,0:T(2,128)(2,1)S(1)}, bf16[1,3072]{1,0:T(2,128)(2,1)S(1)}, u32[]{:S(2)}, u32[]{:S(2)}) collective-permute-start(bf16[1,3072]{1,0:T(2,128)(2,1)S(1)} %get-tuple-element.62), channel_id=1, source_target_pairs={{0,8},{4,12},{8,0},{12,4},{1,9},{5,13},{9,1},{13,5},{2,10},{6,14},... | collective-permute-start | bytes 18440 | tf_op jit(solution)/shard_map/l_2/ppermute | solution.py:35
  144.4 5.7 %collective-permute-done.27.refs_2_ = bf16[1,3072]{1,0:T(2,128)(2,1)S(1)} collective-permute-done((bf16[1,3072]{1,0:T(2,128)(2,1)S(1)}, bf16[1,3072]{1,0:T(2,128)(2,1)S(1)}, u32[]{:S(2)}, u32[]{:S(2)}) %collective-permute-start.27) | collective-permute-done | bytes 6176 | tf_op jit(solution)/shard_map/l_1/ppermute | solution.py:35
  150.2 2.8 %settle.2.refs_7_ = bf16[384,1536]{1,0:T(8,128)(2,1)} custom-call(s32[3]{0:T(128)S(1)} %pad_add_fusion.refs_0_.place_ref, s32[4,4]{1,0:T(4,128)S(1)} %copy-done.1, s32[4,4]{1,0:T(4,128)S(1)} %copy-done.2, bf16[192,768]{1,0:T(8,128)(2,1)S(1)} %get-tuple-element.55.refs_3_, bf16[192,768]{1,0:T(8,128)(2,1)S(1)} %collective-permute-done.15.refs_5_.refs_4_, ...), custom_call_target="tpu_custom_call" | custom-call | flops 452984832 | bytes 2000000 | tf_op jit(solution)/shard_map/settle/pallas_call | solution.py:453
  153.0 3.8 %collective-permute-done.28.refs_3_ = bf16[1,3072]{1,0:T(2,128)(2,1)S(1)} collective-permute-done((bf16[1,3072]{1,0:T(2,128)(2,1)S(1)}, bf16[1,3072]{1,0:T(2,128)(2,1)S(1)}, u32[]{:S(2)}, u32[]{:S(2)}) %collective-permute-start.28) | collective-permute-done | bytes 6176 | tf_op jit(solution)/shard_map/l_2/ppermute | solution.py:35
  159.0 2.9 %settle.3 = bf16[384,1536]{1,0:T(8,128)(2,1)} custom-call(s32[3]{0:T(128)S(1)} %pad_add_fusion.refs_0_.place_ref, s32[4,4]{1,0:T(4,128)S(1)} %copy-done.1, s32[4,4]{1,0:T(4,128)S(1)} %copy-done.2, bf16[192,768]{1,0:T(8,128)(2,1)S(1)} %get-tuple-element.51.refs_3_, ...), custom_call_target="tpu_custom_call", output_to_operand_aliasing={{}: (7, {})} | custom-call | flops 452984832 | bytes 2000000 | tf_op jit(solution)/shard_map/settle/pallas_call | solution.py:453
  (73 shorter events, 32.6 us)
Async XLA Ops:
  2.0 19.3 %collective-permute-start = (bf16[384,768]{1,0:T(8,128)(2,1)S(1)}, bf16[384,768]{1,0:T(8,128)(2,1)S(1)}, u32[]{:S(2)}, u32[]{:S(2)}) collective-permute-start(bf16[384,768]{1,0:T(8,128)(2,1)S(1)} %get-tuple-element.67), channel_id=1, source_target_pairs={{0,4},{4,8},{8,12},{12,0},{1,5},{5,9},{9,13},{13,1},{2,6},{6,10},{... | collective-permute-start | bytes 1769480 | tf_op jit(solution)/shard_map/w0_1/ppermute | solution.py:35
  5.0 28.0 %collective-permute-start.1 = (bf16[384,768]{1,0:T(8,128)(2,1)S(1)}, bf16[384,768]{1,0:T(8,128)(2,1)S(1)}, u32[]{:S(2)}, u32[]{:S(2)}) collective-permute-start(bf16[384,768]{1,0:T(8,128)(2,1)S(1)} %get-tuple-element.66), channel_id=1, source_target_pairs={{0,4},{4,8},{8,12},{12,0},{1,5},{5,9},{9,13},{13,1},{2,6},{6,10},{... | collective-permute-start | bytes 1769480 | tf_op jit(solution)/shard_map/w1_1/ppermute | solution.py:35
  33.0 29.9 %collective-permute-start.3 = (bf16[784,768]{1,0:T(8,128)(2,1)S(1)}, bf16[784,768]{1,0:T(8,128)(2,1)S(1)}, u32[]{:S(2)}, u32[]{:S(2)}) collective-permute-start(bf16[784,768]{1,0:T(8,128)(2,1)S(1)} %get-tuple-element.34.refs_0_), channel_id=1, source_target_pairs={{0,2},{1,3},{2,0},{3,1},{4,6},{5,7},{6,4},{7,5},{8,10},{9,11},{10,... | collective-permute-start | bytes 3612680 | tf_op jit(solution)/shard_map/h_2/ppermute | solution.py:35
  34.5 18.1 %collective-permute-start.4 = (bf16[384,768]{1,0:T(8,128)(2,1)S(1)}, bf16[384,768]{1,0:T(8,128)(2,1)S(1)}, u32[]{:S(2)}, u32[]{:S(2)}) collective-permute-start(bf16[384,768]{1,0:T(8,128)(2,1)S(1)} %collective-permute-done.refs_5_), channel_id=1, source_target_pairs={{0,4},{4,8},{8,12},{12,0},{1,5},{5,9},{9,13},{13,1},{2,6},{6,10},{... | collective-permute-start | bytes 1769480 | tf_op jit(solution)/shard_map/w0_2/ppermute | solution.py:35
  34.5 28.4 %collective-permute-start.5 = (bf16[384,768]{1,0:T(8,128)(2,1)S(1)}, bf16[384,768]{1,0:T(8,128)(2,1)S(1)}, u32[]{:S(2)}, u32[]{:S(2)}) collective-permute-start(bf16[384,768]{1,0:T(8,128)(2,1)S(1)} %collective-permute-done.1.refs_5_), channel_id=1, source_target_pairs={{0,4},{4,8},{8,12},{12,0},{1,5},{5,9},{9,13},{13,1},{2,6},{6,10},{... | collective-permute-start | bytes 1769480 | tf_op jit(solution)/shard_map/w1_2/ppermute | solution.py:35
  35.8 27.1 %collective-permute-start.6 = (bf16[384,768]{1,0:T(8,128)(2,1)S(1)}, bf16[384,768]{1,0:T(8,128)(2,1)S(1)}, u32[]{:S(2)}, u32[]{:S(2)}) collective-permute-start(bf16[384,768]{1,0:T(8,128)(2,1)S(1)} %collective-permute-done.refs_5_), channel_id=1, source_target_pairs={{0,16},{16,0},{1,17},{17,1},{2,18},{18,2},{3,19},{19,3},{4,20},{20... | collective-permute-start | bytes 1769480 | tf_op jit(solution)/shard_map/y0_1/ppermute | solution.py:35
  37.3 25.6 %collective-permute-start.7 = (bf16[384,768]{1,0:T(8,128)(2,1)S(1)}, bf16[384,768]{1,0:T(8,128)(2,1)S(1)}, u32[]{:S(2)}, u32[]{:S(2)}) collective-permute-start(bf16[384,768]{1,0:T(8,128)(2,1)S(1)} %collective-permute-done.1.refs_5_), channel_id=1, source_target_pairs={{0,16},{16,0},{1,17},{17,1},{2,18},{18,2},{3,19},{19,3},{4,20},{20... | collective-permute-start | bytes 1769480 | tf_op jit(solution)/shard_map/y1_1/ppermute | solution.py:35
  52.6 12.5 %collective-permute-start.2 = (bf16[784,768]{1,0:T(8,128)(2,1)S(1)}, bf16[784,768]{1,0:T(8,128)(2,1)S(1)}, u32[]{:S(2)}, u32[]{:S(2)}) collective-permute-start(bf16[784,768]{1,0:T(8,128)(2,1)S(1)} %get-tuple-element.34.refs_0_), channel_id=1, source_target_pairs={{0,1},{1,0},{2,3},{3,2},{4,5},{5,4},{6,7},{7,6},{8,9},{9,8},{10,11... | collective-permute-start | bytes 3612680 | tf_op jit(solution)/shard_map/h_1/ppermute | solution.py:35
  63.0 18.0 %collective-permute-start.9 = (bf16[384,768]{1,0:T(8,128)(2,1)S(1)}, bf16[384,768]{1,0:T(8,128)(2,1)S(1)}, u32[]{:S(2)}, u32[]{:S(2)}) collective-permute-start(bf16[384,768]{1,0:T(8,128)(2,1)S(1)} %collective-permute-done.4.refs_7_), channel_id=1, source_target_pairs={{0,4},{4,8},{8,12},{12,0},{1,5},{5,9},{9,13},{13,1},{2,6},{6,10},{... | collective-permute-start | bytes 1769480 | tf_op jit(solution)/shard_map/w0_3/ppermute | solution.py:35
  63.4 17.6 %collective-permute-start.11 = (bf16[384,768]{1,0:T(8,128)(2,1)S(1)}, bf16[384,768]{1,0:T(8,128)(2,1)S(1)}, u32[]{:S(2)}, u32[]{:S(2)}) collective-permute-start(bf16[384,768]{1,0:T(8,128)(2,1)S(1)} %collective-permute-done.4.refs_7_), channel_id=1, source_target_pairs={{0,16},{16,0},{1,17},{17,1},{2,18},{18,2},{3,19},{19,3},{4,20},{20... | collective-permute-start | bytes 1769480 | tf_op jit(solution)/shard_map/y0_2/ppermute | solution.py:35
  71.4 21.8 %collective-permute-start.10 = (bf16[384,768]{1,0:T(8,128)(2,1)S(1)}, bf16[384,768]{1,0:T(8,128)(2,1)S(1)}, u32[]{:S(2)}, u32[]{:S(2)}) collective-permute-start(bf16[384,768]{1,0:T(8,128)(2,1)S(1)} %collective-permute-done.5.refs_7_), channel_id=1, source_target_pairs={{0,4},{4,8},{8,12},{12,0},{1,5},{5,9},{9,13},{13,1},{2,6},{6,10},{... | collective-permute-start | bytes 1769480 | tf_op jit(solution)/shard_map/w1_3/ppermute | solution.py:35
  81.0 14.4 %collective-permute-start.12 = (bf16[384,768]{1,0:T(8,128)(2,1)S(1)}, bf16[384,768]{1,0:T(8,128)(2,1)S(1)}, u32[]{:S(2)}, u32[]{:S(2)}) collective-permute-start(bf16[384,768]{1,0:T(8,128)(2,1)S(1)} %collective-permute-done.9.refs_11_.refs_3_.refs_4_), channel_id=1, source_target_pairs={{0,16},{16,0},{1,17},{17,1},{2,18},{18,2},{3,19},{19,3},{4,20},{20... | collective-permute-start | bytes 1769480 | tf_op jit(solution)/shard_map/y0_3/ppermute | solution.py:35
  93.2 16.2 %collective-permute-start.14 = (bf16[384,768]{1,0:T(8,128)(2,1)S(1)}, bf16[384,768]{1,0:T(8,128)(2,1)S(1)}, u32[]{:S(2)}, u32[]{:S(2)}) collective-permute-start(bf16[384,768]{1,0:T(8,128)(2,1)S(1)} %collective-permute-done.10.refs_3_.refs_7_), channel_id=1, source_target_pairs={{0,16},{16,0},{1,17},{17,1},{2,18},{18,2},{3,19},{19,3},{4,20},{20... | collective-permute-start | bytes 1769480 | tf_op jit(solution)/shard_map/y1_3/ppermute | solution.py:35
  95.5 25.3 %collective-permute-start.13 = (bf16[384,768]{1,0:T(8,128)(2,1)S(1)}, bf16[384,768]{1,0:T(8,128)(2,1)S(1)}, u32[]{:S(2)}, u32[]{:S(2)}) collective-permute-start(bf16[384,768]{1,0:T(8,128)(2,1)S(1)} %collective-permute-done.5.refs_7_), channel_id=1, source_target_pairs={{0,16},{16,0},{1,17},{17,1},{2,18},{18,2},{3,19},{19,3},{4,20},{20... | collective-permute-start | bytes 1769480 | tf_op jit(solution)/shard_map/y1_2/ppermute | solution.py:35
  99.8 23.6 %collective-permute-start.15 = (bf16[192,768]{1,0:T(8,128)(2,1)S(1)}, bf16[192,768]{1,0:T(8,128)(2,1)S(1)}, u32[]{:S(2)}, u32[]{:S(2)}) collective-permute-start(bf16[192,768]{1,0:T(8,128)(2,1)S(1)} %get-tuple-element.44), channel_id=1, source_target_pairs={{0,4},{4,8},{8,12},{12,0},{1,5},{5,9},{9,13},{13,1},{2,6},{6,10},{... | collective-permute-start | bytes 884744 | tf_op jit(solution)/shard_map/m0_1/ppermute | solution.py:35
  101.5 23.7 %collective-permute-start.16 = (bf16[192,768]{1,0:T(8,128)(2,1)S(1)}, bf16[192,768]{1,0:T(8,128)(2,1)S(1)}, u32[]{:S(2)}, u32[]{:S(2)}) collective-permute-start(bf16[192,768]{1,0:T(8,128)(2,1)S(1)} %get-tuple-element.45), channel_id=1, source_target_pairs={{0,8},{4,12},{8,0},{12,4},{1,9},{5,13},{9,1},{13,5},{2,10},{6,14},... | collective-permute-start | bytes 884744 | tf_op jit(solution)/shard_map/m0_2/ppermute | solution.py:35
  103.2 22.0 %collective-permute-start.17 = (bf16[192,768]{1,0:T(8,128)(2,1)S(1)}, bf16[192,768]{1,0:T(8,128)(2,1)S(1)}, u32[]{:S(2)}, u32[]{:S(2)}) collective-permute-start(bf16[192,768]{1,0:T(8,128)(2,1)S(1)} %get-tuple-element.46), channel_id=1, source_target_pairs={{0,12},{4,0},{8,4},{12,8},{1,13},{5,1},{9,5},{13,9},{2,14},{6,2},{... | collective-permute-start | bytes 884744 | tf_op jit(solution)/shard_map/m0_3/ppermute | solution.py:35
  121.3 6.6 %collective-permute-start.18 = (bf16[4,1536]{1,0:T(4,128)(2,1)S(1)}, bf16[4,1536]{1,0:T(4,128)(2,1)S(1)}, u32[]{:S(2)}, u32[]{:S(2)}) collective-permute-start(bf16[4,1536]{1,0:T(4,128)(2,1)S(1)} %project_pooled.1.refs_1_), channel_id=1, source_target_pairs={{0,4},{4,8},{8,12},{12,0},{1,5},{5,9},{9,13},{13,1},{2,6},{6,10},{... | collective-permute-start | bytes 36872 | tf_op jit(solution)/shard_map/p_1/ppermute | solution.py:35
  128.0 31.0 %collective-permute-start.21 = (bf16[192,768]{1,0:T(8,128)(2,1)S(1)}, bf16[192,768]{1,0:T(8,128)(2,1)S(1)}, u32[]{:S(2)}, u32[]{:S(2)}) collective-permute-start(bf16[192,768]{1,0:T(8,128)(2,1)S(1)} %get-tuple-element.52), channel_id=1, source_target_pairs={{0,4},{4,8},{8,12},{12,0},{1,5},{5,9},{9,13},{13,1},{2,6},{6,10},{... | collective-permute-start | bytes 884744 | tf_op jit(solution)/shard_map/m1_1/ppermute | solution.py:35
  131.0 28.1 %collective-permute-start.22 = (bf16[192,768]{1,0:T(8,128)(2,1)S(1)}, bf16[192,768]{1,0:T(8,128)(2,1)S(1)}, u32[]{:S(2)}, u32[]{:S(2)}) collective-permute-start(bf16[192,768]{1,0:T(8,128)(2,1)S(1)} %get-tuple-element.53), channel_id=1, source_target_pairs={{0,8},{4,12},{8,0},{12,4},{1,9},{5,13},{9,1},{13,5},{2,10},{6,14},... | collective-permute-start | bytes 884744 | tf_op jit(solution)/shard_map/m1_2/ppermute | solution.py:35
  131.2 27.8 %collective-permute-start.23 = (bf16[192,768]{1,0:T(8,128)(2,1)S(1)}, bf16[192,768]{1,0:T(8,128)(2,1)S(1)}, u32[]{:S(2)}, u32[]{:S(2)}) collective-permute-start(bf16[192,768]{1,0:T(8,128)(2,1)S(1)} %get-tuple-element.54), channel_id=1, source_target_pairs={{0,12},{4,0},{8,4},{12,8},{1,13},{5,1},{9,5},{13,9},{2,14},{6,2},{... | collective-permute-start | bytes 884744 | tf_op jit(solution)/shard_map/m1_3/ppermute | solution.py:35
  141.9 8.3 %collective-permute-start.27 = (bf16[1,3072]{1,0:T(2,128)(2,1)S(1)}, bf16[1,3072]{1,0:T(2,128)(2,1)S(1)}, u32[]{:S(2)}, u32[]{:S(2)}) collective-permute-start(bf16[1,3072]{1,0:T(2,128)(2,1)S(1)} %get-tuple-element.61), channel_id=1, source_target_pairs={{0,4},{4,8},{8,12},{12,0},{1,5},{5,9},{9,13},{13,1},{2,6},{6,10},{... | collective-permute-start | bytes 18440 | tf_op jit(solution)/shard_map/l_1/ppermute | solution.py:35
  142.0 14.9 %collective-permute-start.28 = (bf16[1,3072]{1,0:T(2,128)(2,1)S(1)}, bf16[1,3072]{1,0:T(2,128)(2,1)S(1)}, u32[]{:S(2)}, u32[]{:S(2)}) collective-permute-start(bf16[1,3072]{1,0:T(2,128)(2,1)S(1)} %get-tuple-element.62), channel_id=1, source_target_pairs={{0,8},{4,12},{8,0},{12,4},{1,9},{5,13},{9,1},{13,5},{2,10},{6,14},... | collective-permute-start | bytes 18440 | tf_op jit(solution)/shard_map/l_2/ppermute | solution.py:35
  150.2 7.7 %collective-permute-start.29 = (bf16[1,3072]{1,0:T(2,128)(2,1)S(1)}, bf16[1,3072]{1,0:T(2,128)(2,1)S(1)}, u32[]{:S(2)}, u32[]{:S(2)}) collective-permute-start(bf16[1,3072]{1,0:T(2,128)(2,1)S(1)} %get-tuple-element.63), channel_id=1, source_target_pairs={{0,12},{4,0},{8,4},{12,8},{1,13},{5,1},{9,5},{13,9},{2,14},{6,2},{... | collective-permute-start | bytes 18440 | tf_op jit(solution)/shard_map/l_3/ppermute | solution.py:35
  (16 other events, 192.8 us)

commit v4 on v3

--- a/solution.py
+++ b/solution.py
@@ -580,18 +580,18 @@
         1000,
     )
     probs = [probs[0]] + [send(probs[k], "dp", shifted(rows, k), f"l_{k}") for k in range(1, rows)]
+    mixed = None
+    for c in range(CHUNKS):
+        mixed = settle(place, patch_counts, move_plan, arrived[c], c, features, mixed, [])
     labels = local_call(
         lambda *refs: labels_kernel(rows, *refs),
         jax.ShapeDtypeStruct((1, rows * classes), jnp.float32),
-        probs,
+        after_all(probs, [mixed]),
         [],
         place,
         "labels",
         1000,
     )
-    mixed = None
-    for c in range(CHUNKS):
-        mixed = settle(place, patch_counts, move_plan, arrived[c], c, features, mixed, [])
     labels = labels[None]
     return (mixed[None], labels)
 

time: 162 us -> 158 us (0.975)
  waiting for transfers between devices: 86.3 us -> 81.1 us
    ppermute x30, waiting for transfers between devices: 86.3 us -> 81.1 us  [send(): return lax.ppermute(values, axis, pairs)]
  transfers between devices with their start and end apart: 30 -> 30, of which waited for: 16 -> 13; matrix products, arithmetic and copies ran while one was open for 2% -> 2% of each run, Pallas kernels for 20% -> 22%
where the time goes in v4:
time: 158 us
  waiting for transfers between devices  81.1 us (51%)
  starting transfers between devices  36 us (23%)
  Pallas kernels  35.2 us (22%)
  local copies, waits for them, and re-layouts  4.83 us (3%)
    ppermute x30, waiting for transfers between devices, send(): return lax.ppermute(values, axis, pairs)  81.1 us
    ppermute x30, starting transfers between devices, send(): return lax.ppermute(values, axis, pairs)  36 us
    pallas_call x2, Pallas kernels, project_early(): pl.pallas_call(lambda place_ref, *refs: early_kernel(rows, with_late, pla...  10.7 us
    pallas_call x1, Pallas kernels, attend(): pl.pallas_call(lambda *refs: attend_kernel(rows, span, *refs), grid_spec=...  7.56 us
    pallas_call x2, Pallas kernels, settle(): pl.pallas_call(lambda *refs: settle_kernel(rows, *refs), grid_spec=pltpu....  5.66 us
    pallas_call x2, Pallas kernels, project_late(): pl.pallas_call(lambda *refs: late_kernel(rows, *refs), grid=(tiles,), in_...  5.52 us
    pallas_call x1, Pallas kernels, label_terms_by_part(): pl.pallas_call(lambda *refs: terms_kernel(rows, *refs), grid_spec=pltpu.P...  3.31 us
  transfers between devices with their start and end apart: 30, of which 13 were waited for; matrix products, arithmetic and copies ran while one was open for 2% of the time, Pallas kernels for 22%

profile of v4, /device:TPU:0, one launch (start us, length us, event | category | flops | bytes accessed | tf_op | source)
XLA Modules:
  0.0 158.0 jit_solution(6978566476443538759)
XLA Ops:
  2.0 3.1 %collective-permute-start = (bf16[384,768]{1,0:T(8,128)(2,1)S(1)}, bf16[384,768]{1,0:T(8,128)(2,1)S(1)}, u32[]{:S(2)}, u32[]{:S(2)}) collective-permute-start(bf16[384,768]{1,0:T(8,128)(2,1)S(1)} %get-tuple-element.75), channel_id=1, source_target_pairs={{0,4},{4,8},{8,12},{12,0},{1,5},{5,9},{9,13},{13,1},{2,6},{6,10},{... | collective-permute-start | bytes 1769480 | tf_op jit(solution)/shard_map/w0_1/ppermute | solution.py:35
  6.6 2.4 %pad.8.refs_3_ = bf16[3,960,768]{2,1,0:T(8,128)(2,1)S(1)} pad(bf16[3,764,768]{2,1,0:T(8,128)(2,1)} %bitcast.18, bf16[]{:T(256)} %constant.17.clone.1), padding=0_0x0_196x0_0 | pad | bytes 7944194 | tf_op jit(solution)/shard_map/jit(_pad)/pad | solution.py:502
  10.1 7.6 %attend.1 = (bf16[784,768]{1,0:T(8,128)(2,1)S(1)}, bf16[768,1536]{1,0:T(8,128)(2,1)S(1)}, f32[16,1536]{1,0:T(8,128)S(1)}) custom-call(s32[3]{0:T(128)S(1)} %pad_add_fusion.refs_0_.place_ref, s32[4,4]{1,0:T(4,128)S(1)} %copy-done.1, s32[4,4]{1,0:T(4,128)S(1)} %copy-done.2, bf16[3,960,768]{2,1,0:T(8,128)(2,1)S(1)} %pad.8.refs_3_, ...), custom_call_target="tpu_custom_call" | custom-call | flops 10000000000 | bytes 12000000 | tf_op jit(solution)/shard_map/attend/pallas_call | solution.py:124
  17.6 3.6 %collective-permute-done.refs_5_ = bf16[384,768]{1,0:T(8,128)(2,1)S(1)} collective-permute-done((bf16[384,768]{1,0:T(8,128)(2,1)S(1)}, bf16[384,768]{1,0:T(8,128)(2,1)S(1)}, u32[]{:S(2)}, u32[]{:S(2)}) %collective-permute-start) | collective-permute-done | bytes 589856 | tf_op jit(solution)/shard_map/w0_1/ppermute | solution.py:35
  21.2 11.8 %collective-permute-done.1.refs_5_ = bf16[384,768]{1,0:T(8,128)(2,1)S(1)} collective-permute-done((bf16[384,768]{1,0:T(8,128)(2,1)S(1)}, bf16[384,768]{1,0:T(8,128)(2,1)S(1)}, u32[]{:S(2)}, u32[]{:S(2)}) %collective-permute-start.1) | collective-permute-done | bytes 589856 | tf_op jit(solution)/shard_map/w1_1/ppermute | solution.py:35
  37.8 14.7 %collective-permute-done.4.refs_7_ = bf16[384,768]{1,0:T(8,128)(2,1)S(1)} collective-permute-done((bf16[384,768]{1,0:T(8,128)(2,1)S(1)}, bf16[384,768]{1,0:T(8,128)(2,1)S(1)}, u32[]{:S(2)}, u32[]{:S(2)}) %collective-permute-start.4) | collective-permute-done | bytes 589856 | tf_op jit(solution)/shard_map/w0_2/ppermute | solution.py:35
  52.6 10.4 %collective-permute-done.5.refs_7_ = bf16[384,768]{1,0:T(8,128)(2,1)S(1)} collective-permute-done((bf16[384,768]{1,0:T(8,128)(2,1)S(1)}, bf16[384,768]{1,0:T(8,128)(2,1)S(1)}, u32[]{:S(2)}, u32[]{:S(2)}) %collective-permute-start.5) | collective-permute-done | bytes 589856 | tf_op jit(solution)/shard_map/w1_2/ppermute | solution.py:35
  65.9 5.5 %project_early.2 = (f32[784,768]{1,0:T(8,128)S(1)}, bf16[784,1152]{1,0:T(8,128)(2,1)S(1)}) custom-call(s32[3]{0:T(128)S(1)} %pad_add_fusion.refs_0_.place_ref, bf16[784,768]{1,0:T(8,128)(2,1)S(1)} %get-tuple-element.38.refs_0_, bf16[784,768]{1,0:T(8,128)(2,1)S(1)} %collective-permute-done.2.refs_1_, bf16[784,768]{1,0:T(8,128)(2,1)S(1)} %collective-permute-done.3.refs_2_, ...), custom_call_target="tpu_custom_call" | custom-call | flops 4000000000 | bytes 1000 | tf_op jit(solution)/shard_map/project_early/pallas_call | solution.py:231
  72.8 8.2 %collective-permute-done.9.refs_11_.refs_3_.refs_4_ = bf16[384,768]{1,0:T(8,128)(2,1)S(1)} collective-permute-done((bf16[384,768]{1,0:T(8,128)(2,1)S(1)}, bf16[384,768]{1,0:T(8,128)(2,1)S(1)}, u32[]{:S(2)}, u32[]{:S(2)}) %collective-permute-start.9) | collective-permute-done | bytes 589856 | tf_op jit(solution)/shard_map/w0_3/ppermute | solution.py:35
  82.5 5.2 %project_early.3.refs_0_.refs_2_ = f32[784,768]{1,0:T(8,128)S(1)} custom-call(s32[3]{0:T(128)S(1)} %pad_add_fusion.refs_0_.place_ref, bf16[784,768]{1,0:T(8,128)(2,1)S(1)} %get-tuple-element.38.refs_0_, bf16[784,768]{1,0:T(8,128)(2,1)S(1)} %collective-permute-done.2.refs_1_, bf16[784,768]{1,0:T(8,128)(2,1)S(1)} %collective-permute-done.3.refs_2_, ...), custom_call_target="tpu_custom_call" | custom-call | flops 4000000000 | bytes 1000 | tf_op jit(solution)/shard_map/project_early/pallas_call | solution.py:231
  87.8 5.4 %collective-permute-done.10.refs_3_.refs_7_ = bf16[384,768]{1,0:T(8,128)(2,1)S(1)} collective-permute-done((bf16[384,768]{1,0:T(8,128)(2,1)S(1)}, bf16[384,768]{1,0:T(8,128)(2,1)S(1)}, u32[]{:S(2)}, u32[]{:S(2)}) %collective-permute-start.10) | collective-permute-done | bytes 589856 | tf_op jit(solution)/shard_map/w1_3/ppermute | solution.py:35
  97.0 2.8 %project_late.2 = (bf16[192,768]{1,0:T(8,128)(2,1)S(1)}, bf16[192,768]{1,0:T(8,128)(2,1)S(1)}, bf16[192,768]{1,0:T(8,128)(2,1)S(1)}, bf16[192,768]{1,0:T(8,128)(2,1)S(1)}) custom-call(f32[784,768]{1,0:T(8,128)S(1)} %get-tuple-element.42.refs_10_.refs_0_.refs_1_, bf16[784,1152]{1,0:T(8,128)(2,1)S(1)} %get-tuple-element.43.refs_1_.refs_0_, ...), custom_call_target="tpu_custom_call" | custom-call | flops 1387266048 | bytes 6000000 | tf_op jit(solution)/shard_map/project_late/pallas_call | solution.py:308
  103.9 5.5 %collective-permute-done.14.refs_4_.refs_8_ = bf16[384,768]{1,0:T(8,128)(2,1)S(1)} collective-permute-done((bf16[384,768]{1,0:T(8,128)(2,1)S(1)}, bf16[384,768]{1,0:T(8,128)(2,1)S(1)}, u32[]{:S(2)}, u32[]{:S(2)}) %collective-permute-start.14) | collective-permute-done | bytes 589856 | tf_op jit(solution)/shard_map/y1_3/ppermute | solution.py:35
  109.5 11.3 %collective-permute-done.13.refs_2_.refs_6_ = bf16[384,768]{1,0:T(8,128)(2,1)S(1)} collective-permute-done((bf16[384,768]{1,0:T(8,128)(2,1)S(1)}, bf16[384,768]{1,0:T(8,128)(2,1)S(1)}, u32[]{:S(2)}, u32[]{:S(2)}) %collective-permute-start.13) | collective-permute-done | bytes 589856 | tf_op jit(solution)/shard_map/y1_2/ppermute | solution.py:35
  123.3 1.8 %collective-permute-start.20 = (bf16[4,1536]{1,0:T(4,128)(2,1)S(1)}, bf16[4,1536]{1,0:T(4,128)(2,1)S(1)}, u32[]{:S(2)}, u32[]{:S(2)}) collective-permute-start(bf16[4,1536]{1,0:T(4,128)(2,1)S(1)} %project_pooled.1.refs_1_), channel_id=1, source_target_pairs={{0,12},{4,0},{8,4},{12,8},{1,13},{5,1},{9,5},{13,9},{2,14},{6,2},{... | collective-permute-start | bytes 36872 | tf_op jit(solution)/shard_map/p_3/ppermute | solution.py:35
  125.2 2.8 %project_late.3 = (bf16[192,768]{1,0:T(8,128)(2,1)S(1)}, bf16[192,768]{1,0:T(8,128)(2,1)S(1)}, bf16[192,768]{1,0:T(8,128)(2,1)S(1)}, bf16[192,768]{1,0:T(8,128)(2,1)S(1)}) custom-call(f32[784,768]{1,0:T(8,128)S(1)} %project_early.3.refs_0_.refs_2_, bf16[784,1152]{1,0:T(8,128)(2,1)S(1)} %get-tuple-element.43.refs_1_.refs_0_, ...), custom_call_target="tpu_custom_call" | custom-call | flops 1387266048 | bytes 6000000 | tf_op jit(solution)/shard_map/project_late/pallas_call | solution.py:308
  128.0 3.0 %collective-permute-start.21 = (bf16[192,768]{1,0:T(8,128)(2,1)S(1)}, bf16[192,768]{1,0:T(8,128)(2,1)S(1)}, u32[]{:S(2)}, u32[]{:S(2)}) collective-permute-start(bf16[192,768]{1,0:T(8,128)(2,1)S(1)} %get-tuple-element.56), channel_id=1, source_target_pairs={{0,4},{4,8},{8,12},{12,0},{1,5},{5,9},{9,13},{13,1},{2,6},{6,10},{... | collective-permute-start | bytes 884744 | tf_op jit(solution)/shard_map/m1_1/ppermute | solution.py:35
  131.2 2.2 %collective-permute-start.23 = (bf16[192,768]{1,0:T(8,128)(2,1)S(1)}, bf16[192,768]{1,0:T(8,128)(2,1)S(1)}, u32[]{:S(2)}, u32[]{:S(2)}) collective-permute-start(bf16[192,768]{1,0:T(8,128)(2,1)S(1)} %get-tuple-element.58), channel_id=1, source_target_pairs={{0,12},{4,0},{8,4},{12,8},{1,13},{5,1},{9,5},{13,9},{2,14},{6,2},{... | collective-permute-start | bytes 884744 | tf_op jit(solution)/shard_map/m1_3/ppermute | solution.py:35
  133.4 3.3 %label_terms.1 = (bf16[4,3072]{1,0:T(4,128)(2,1)S(1)}, bf16[4,3072]{1,0:T(4,128)(2,1)S(1)}, bf16[4,3072]{1,0:T(4,128)(2,1)S(1)}, bf16[4,3072]{1,0:T(4,128)(2,1)S(1)}) custom-call(s32[3]{0:T(128)S(1)} %pad_add_fusion.refs_0_.place_ref, bf16[4,1536]{1,0:T(4,128)(2,1)S(1)} %project_pooled.1.refs_1_, bf16[4,1536]{1,0:T(4,128)(2,1)S(1)} %collective-permute-done.18.refs_2_, ...), custom_call_target="tpu_custom_call" | custom-call | flops 150994944 | bytes 12000000 | tf_op jit(solution)/shard_map/label_terms/pallas_call | solution.py:379
  138.6 2.8 %settle.2.refs_7_ = bf16[384,1536]{1,0:T(8,128)(2,1)} custom-call(s32[3]{0:T(128)S(1)} %pad_add_fusion.refs_0_.place_ref, s32[4,4]{1,0:T(4,128)S(1)} %copy-done.1, s32[4,4]{1,0:T(4,128)S(1)} %copy-done.2, bf16[192,768]{1,0:T(8,128)(2,1)S(1)} %get-tuple-element.59.refs_3_, bf16[192,768]{1,0:T(8,128)(2,1)S(1)} %collective-permute-done.15.refs_5_.refs_4_, ...), custom_call_target="tpu_custom_call" | custom-call | flops 452984832 | bytes 2000000 | tf_op jit(solution)/shard_map/settle/pallas_call | solution.py:453
  142.2 2.5 %collective-permute-start.28 = (bf16[1,3072]{1,0:T(2,128)(2,1)S(1)}, bf16[1,3072]{1,0:T(2,128)(2,1)S(1)}, u32[]{:S(2)}, u32[]{:S(2)}) collective-permute-start(bf16[1,3072]{1,0:T(2,128)(2,1)S(1)} %get-tuple-element.66), channel_id=1, source_target_pairs={{0,8},{4,12},{8,0},{12,4},{1,9},{5,13},{9,1},{13,5},{2,10},{6,14},... | collective-permute-start | bytes 18440 | tf_op jit(solution)/shard_map/l_2/ppermute | solution.py:35
  146.0 4.0 %collective-permute-done.22.refs_5_ = bf16[192,768]{1,0:T(8,128)(2,1)S(1)} collective-permute-done((bf16[192,768]{1,0:T(8,128)(2,1)S(1)}, bf16[192,768]{1,0:T(8,128)(2,1)S(1)}, u32[]{:S(2)}, u32[]{:S(2)}) %collective-permute-start.22) | collective-permute-done | bytes 294944 | tf_op jit(solution)/shard_map/m1_2/ppermute | solution.py:35
  150.0 2.8 %settle.3 = bf16[384,1536]{1,0:T(8,128)(2,1)} custom-call(s32[3]{0:T(128)S(1)} %pad_add_fusion.refs_0_.place_ref, s32[4,4]{1,0:T(4,128)S(1)} %copy-done.1, s32[4,4]{1,0:T(4,128)S(1)} %copy-done.2, bf16[192,768]{1,0:T(8,128)(2,1)S(1)} %get-tuple-element.55.refs_3_, ...), custom_call_target="tpu_custom_call", output_to_operand_aliasing={{}: (7, {})} | custom-call | flops 452984832 | bytes 2000000 | tf_op jit(solution)/shard_map/settle/pallas_call | solution.py:453
  152.8 4.0 %collective-permute-done.28.refs_3_ = bf16[1,3072]{1,0:T(2,128)(2,1)S(1)} collective-permute-done((bf16[1,3072]{1,0:T(2,128)(2,1)S(1)}, bf16[1,3072]{1,0:T(2,128)(2,1)S(1)}, u32[]{:S(2)}, u32[]{:S(2)}) %collective-permute-start.28) | collective-permute-done | bytes 6176 | tf_op jit(solution)/shard_map/l_2/ppermute | solution.py:35
  (73 shorter events, 30.6 us)
Async XLA Ops:
  2.0 19.3 %collective-permute-start = (bf16[384,768]{1,0:T(8,128)(2,1)S(1)}, bf16[384,768]{1,0:T(8,128)(2,1)S(1)}, u32[]{:S(2)}, u32[]{:S(2)}) collective-permute-start(bf16[384,768]{1,0:T(8,128)(2,1)S(1)} %get-tuple-element.75), channel_id=1, source_target_pairs={{0,4},{4,8},{8,12},{12,0},{1,5},{5,9},{9,13},{13,1},{2,6},{6,10},{... | collective-permute-start | bytes 1769480 | tf_op jit(solution)/shard_map/w0_1/ppermute | solution.py:35
  5.0 28.0 %collective-permute-start.1 = (bf16[384,768]{1,0:T(8,128)(2,1)S(1)}, bf16[384,768]{1,0:T(8,128)(2,1)S(1)}, u32[]{:S(2)}, u32[]{:S(2)}) collective-permute-start(bf16[384,768]{1,0:T(8,128)(2,1)S(1)} %get-tuple-element.74), channel_id=1, source_target_pairs={{0,4},{4,8},{8,12},{12,0},{1,5},{5,9},{9,13},{13,1},{2,6},{6,10},{... | collective-permute-start | bytes 1769480 | tf_op jit(solution)/shard_map/w1_1/ppermute | solution.py:35
  33.0 29.9 %collective-permute-start.3 = (bf16[784,768]{1,0:T(8,128)(2,1)S(1)}, bf16[784,768]{1,0:T(8,128)(2,1)S(1)}, u32[]{:S(2)}, u32[]{:S(2)}) collective-permute-start(bf16[784,768]{1,0:T(8,128)(2,1)S(1)} %get-tuple-element.38.refs_0_), channel_id=1, source_target_pairs={{0,2},{1,3},{2,0},{3,1},{4,6},{5,7},{6,4},{7,5},{8,10},{9,11},{10,... | collective-permute-start | bytes 3612680 | tf_op jit(solution)/shard_map/h_2/ppermute | solution.py:35
  34.5 18.1 %collective-permute-start.4 = (bf16[384,768]{1,0:T(8,128)(2,1)S(1)}, bf16[384,768]{1,0:T(8,128)(2,1)S(1)}, u32[]{:S(2)}, u32[]{:S(2)}) collective-permute-start(bf16[384,768]{1,0:T(8,128)(2,1)S(1)} %collective-permute-done.refs_5_), channel_id=1, source_target_pairs={{0,4},{4,8},{8,12},{12,0},{1,5},{5,9},{9,13},{13,1},{2,6},{6,10},{... | collective-permute-start | bytes 1769480 | tf_op jit(solution)/shard_map/w0_2/ppermute | solution.py:35
  34.5 28.4 %collective-permute-start.5 = (bf16[384,768]{1,0:T(8,128)(2,1)S(1)}, bf16[384,768]{1,0:T(8,128)(2,1)S(1)}, u32[]{:S(2)}, u32[]{:S(2)}) collective-permute-start(bf16[384,768]{1,0:T(8,128)(2,1)S(1)} %collective-permute-done.1.refs_5_), channel_id=1, source_target_pairs={{0,4},{4,8},{8,12},{12,0},{1,5},{5,9},{9,13},{13,1},{2,6},{6,10},{... | collective-permute-start | bytes 1769480 | tf_op jit(solution)/shard_map/w1_2/ppermute | solution.py:35
  35.8 27.1 %collective-permute-start.6 = (bf16[384,768]{1,0:T(8,128)(2,1)S(1)}, bf16[384,768]{1,0:T(8,128)(2,1)S(1)}, u32[]{:S(2)}, u32[]{:S(2)}) collective-permute-start(bf16[384,768]{1,0:T(8,128)(2,1)S(1)} %collective-permute-done.refs_5_), channel_id=1, source_target_pairs={{0,16},{16,0},{1,17},{17,1},{2,18},{18,2},{3,19},{19,3},{4,20},{20... | collective-permute-start | bytes 1769480 | tf_op jit(solution)/shard_map/y0_1/ppermute | solution.py:35
  37.3 25.6 %collective-permute-start.7 = (bf16[384,768]{1,0:T(8,128)(2,1)S(1)}, bf16[384,768]{1,0:T(8,128)(2,1)S(1)}, u32[]{:S(2)}, u32[]{:S(2)}) collective-permute-start(bf16[384,768]{1,0:T(8,128)(2,1)S(1)} %collective-permute-done.1.refs_5_), channel_id=1, source_target_pairs={{0,16},{16,0},{1,17},{17,1},{2,18},{18,2},{3,19},{19,3},{4,20},{20... | collective-permute-start | bytes 1769480 | tf_op jit(solution)/shard_map/y1_1/ppermute | solution.py:35
  52.6 12.5 %collective-permute-start.2 = (bf16[784,768]{1,0:T(8,128)(2,1)S(1)}, bf16[784,768]{1,0:T(8,128)(2,1)S(1)}, u32[]{:S(2)}, u32[]{:S(2)}) collective-permute-start(bf16[784,768]{1,0:T(8,128)(2,1)S(1)} %get-tuple-element.38.refs_0_), channel_id=1, source_target_pairs={{0,1},{1,0},{2,3},{3,2},{4,5},{5,4},{6,7},{7,6},{8,9},{9,8},{10,11... | collective-permute-start | bytes 3612680 | tf_op jit(solution)/shard_map/h_1/ppermute | solution.py:35
  63.0 18.0 %collective-permute-start.9 = (bf16[384,768]{1,0:T(8,128)(2,1)S(1)}, bf16[384,768]{1,0:T(8,128)(2,1)S(1)}, u32[]{:S(2)}, u32[]{:S(2)}) collective-permute-start(bf16[384,768]{1,0:T(8,128)(2,1)S(1)} %collective-permute-done.4.refs_7_), channel_id=1, source_target_pairs={{0,4},{4,8},{8,12},{12,0},{1,5},{5,9},{9,13},{13,1},{2,6},{6,10},{... | collective-permute-start | bytes 1769480 | tf_op jit(solution)/shard_map/w0_3/ppermute | solution.py:35
  63.4 17.6 %collective-permute-start.11 = (bf16[384,768]{1,0:T(8,128)(2,1)S(1)}, bf16[384,768]{1,0:T(8,128)(2,1)S(1)}, u32[]{:S(2)}, u32[]{:S(2)}) collective-permute-start(bf16[384,768]{1,0:T(8,128)(2,1)S(1)} %collective-permute-done.4.refs_7_), channel_id=1, source_target_pairs={{0,16},{16,0},{1,17},{17,1},{2,18},{18,2},{3,19},{19,3},{4,20},{20... | collective-permute-start | bytes 1769480 | tf_op jit(solution)/shard_map/y0_2/ppermute | solution.py:35
  71.4 21.8 %collective-permute-start.10 = (bf16[384,768]{1,0:T(8,128)(2,1)S(1)}, bf16[384,768]{1,0:T(8,128)(2,1)S(1)}, u32[]{:S(2)}, u32[]{:S(2)}) collective-permute-start(bf16[384,768]{1,0:T(8,128)(2,1)S(1)} %collective-permute-done.5.refs_7_), channel_id=1, source_target_pairs={{0,4},{4,8},{8,12},{12,0},{1,5},{5,9},{9,13},{13,1},{2,6},{6,10},{... | collective-permute-start | bytes 1769480 | tf_op jit(solution)/shard_map/w1_3/ppermute | solution.py:35
  81.0 14.4 %collective-permute-start.12 = (bf16[384,768]{1,0:T(8,128)(2,1)S(1)}, bf16[384,768]{1,0:T(8,128)(2,1)S(1)}, u32[]{:S(2)}, u32[]{:S(2)}) collective-permute-start(bf16[384,768]{1,0:T(8,128)(2,1)S(1)} %collective-permute-done.9.refs_11_.refs_3_.refs_4_), channel_id=1, source_target_pairs={{0,16},{16,0},{1,17},{17,1},{2,18},{18,2},{3,19},{19,3},{4,20},{20... | collective-permute-start | bytes 1769480 | tf_op jit(solution)/shard_map/y0_3/ppermute | solution.py:35
  93.2 16.2 %collective-permute-start.14 = (bf16[384,768]{1,0:T(8,128)(2,1)S(1)}, bf16[384,768]{1,0:T(8,128)(2,1)S(1)}, u32[]{:S(2)}, u32[]{:S(2)}) collective-permute-start(bf16[384,768]{1,0:T(8,128)(2,1)S(1)} %collective-permute-done.10.refs_3_.refs_7_), channel_id=1, source_target_pairs={{0,16},{16,0},{1,17},{17,1},{2,18},{18,2},{3,19},{19,3},{4,20},{20... | collective-permute-start | bytes 1769480 | tf_op jit(solution)/shard_map/y1_3/ppermute | solution.py:35
  95.5 25.3 %collective-permute-start.13 = (bf16[384,768]{1,0:T(8,128)(2,1)S(1)}, bf16[384,768]{1,0:T(8,128)(2,1)S(1)}, u32[]{:S(2)}, u32[]{:S(2)}) collective-permute-start(bf16[384,768]{1,0:T(8,128)(2,1)S(1)} %collective-permute-done.5.refs_7_), channel_id=1, source_target_pairs={{0,16},{16,0},{1,17},{17,1},{2,18},{18,2},{3,19},{19,3},{4,20},{20... | collective-permute-start | bytes 1769480 | tf_op jit(solution)/shard_map/y1_2/ppermute | solution.py:35
  99.8 23.6 %collective-permute-start.15 = (bf16[192,768]{1,0:T(8,128)(2,1)S(1)}, bf16[192,768]{1,0:T(8,128)(2,1)S(1)}, u32[]{:S(2)}, u32[]{:S(2)}) collective-permute-start(bf16[192,768]{1,0:T(8,128)(2,1)S(1)} %get-tuple-element.48), channel_id=1, source_target_pairs={{0,4},{4,8},{8,12},{12,0},{1,5},{5,9},{9,13},{13,1},{2,6},{6,10},{... | collective-permute-start | bytes 884744 | tf_op jit(solution)/shard_map/m0_1/ppermute | solution.py:35
  101.5 23.7 %collective-permute-start.16 = (bf16[192,768]{1,0:T(8,128)(2,1)S(1)}, bf16[192,768]{1,0:T(8,128)(2,1)S(1)}, u32[]{:S(2)}, u32[]{:S(2)}) collective-permute-start(bf16[192,768]{1,0:T(8,128)(2,1)S(1)} %get-tuple-element.49), channel_id=1, source_target_pairs={{0,8},{4,12},{8,0},{12,4},{1,9},{5,13},{9,1},{13,5},{2,10},{6,14},... | collective-permute-start | bytes 884744 | tf_op jit(solution)/shard_map/m0_2/ppermute | solution.py:35
  103.2 22.0 %collective-permute-start.17 = (bf16[192,768]{1,0:T(8,128)(2,1)S(1)}, bf16[192,768]{1,0:T(8,128)(2,1)S(1)}, u32[]{:S(2)}, u32[]{:S(2)}) collective-permute-start(bf16[192,768]{1,0:T(8,128)(2,1)S(1)} %get-tuple-element.50), channel_id=1, source_target_pairs={{0,12},{4,0},{8,4},{12,8},{1,13},{5,1},{9,5},{13,9},{2,14},{6,2},{... | collective-permute-start | bytes 884744 | tf_op jit(solution)/shard_map/m0_3/ppermute | solution.py:35
  121.3 6.6 %collective-permute-start.18 = (bf16[4,1536]{1,0:T(4,128)(2,1)S(1)}, bf16[4,1536]{1,0:T(4,128)(2,1)S(1)}, u32[]{:S(2)}, u32[]{:S(2)}) collective-permute-start(bf16[4,1536]{1,0:T(4,128)(2,1)S(1)} %project_pooled.1.refs_1_), channel_id=1, source_target_pairs={{0,4},{4,8},{8,12},{12,0},{1,5},{5,9},{9,13},{13,1},{2,6},{6,10},{... | collective-permute-start | bytes 36872 | tf_op jit(solution)/shard_map/p_1/ppermute | solution.py:35
  128.0 16.7 %collective-permute-start.21 = (bf16[192,768]{1,0:T(8,128)(2,1)S(1)}, bf16[192,768]{1,0:T(8,128)(2,1)S(1)}, u32[]{:S(2)}, u32[]{:S(2)}) collective-permute-start(bf16[192,768]{1,0:T(8,128)(2,1)S(1)} %get-tuple-element.56), channel_id=1, source_target_pairs={{0,4},{4,8},{8,12},{12,0},{1,5},{5,9},{9,13},{13,1},{2,6},{6,10},{... | collective-permute-start | bytes 884744 | tf_op jit(solution)/shard_map/m1_1/ppermute | solution.py:35
  130.9 19.0 %collective-permute-start.22 = (bf16[192,768]{1,0:T(8,128)(2,1)S(1)}, bf16[192,768]{1,0:T(8,128)(2,1)S(1)}, u32[]{:S(2)}, u32[]{:S(2)}) collective-permute-start(bf16[192,768]{1,0:T(8,128)(2,1)S(1)} %get-tuple-element.57), channel_id=1, source_target_pairs={{0,8},{4,12},{8,0},{12,4},{1,9},{5,13},{9,1},{13,5},{2,10},{6,14},... | collective-permute-start | bytes 884744 | tf_op jit(solution)/shard_map/m1_2/ppermute | solution.py:35
  131.2 18.8 %collective-permute-start.23 = (bf16[192,768]{1,0:T(8,128)(2,1)S(1)}, bf16[192,768]{1,0:T(8,128)(2,1)S(1)}, u32[]{:S(2)}, u32[]{:S(2)}) collective-permute-start(bf16[192,768]{1,0:T(8,128)(2,1)S(1)} %get-tuple-element.58), channel_id=1, source_target_pairs={{0,12},{4,0},{8,4},{12,8},{1,13},{5,1},{9,5},{13,9},{2,14},{6,2},{... | collective-permute-start | bytes 884744 | tf_op jit(solution)/shard_map/m1_3/ppermute | solution.py:35
  142.1 10.7 %collective-permute-start.27 = (bf16[1,3072]{1,0:T(2,128)(2,1)S(1)}, bf16[1,3072]{1,0:T(2,128)(2,1)S(1)}, u32[]{:S(2)}, u32[]{:S(2)}) collective-permute-start(bf16[1,3072]{1,0:T(2,128)(2,1)S(1)} %get-tuple-element.65), channel_id=1, source_target_pairs={{0,4},{4,8},{8,12},{12,0},{1,5},{5,9},{9,13},{13,1},{2,6},{6,10},{... | collective-permute-start | bytes 18440 | tf_op jit(solution)/shard_map/l_1/ppermute | solution.py:35
  142.2 14.6 %collective-permute-start.28 = (bf16[1,3072]{1,0:T(2,128)(2,1)S(1)}, bf16[1,3072]{1,0:T(2,128)(2,1)S(1)}, u32[]{:S(2)}, u32[]{:S(2)}) collective-permute-start(bf16[1,3072]{1,0:T(2,128)(2,1)S(1)} %get-tuple-element.66), channel_id=1, source_target_pairs={{0,8},{4,12},{8,0},{12,4},{1,9},{5,13},{9,1},{13,5},{2,10},{6,14},... | collective-permute-start | bytes 18440 | tf_op jit(solution)/shard_map/l_2/ppermute | solution.py:35
  144.7 12.2 %collective-permute-start.29 = (bf16[1,3072]{1,0:T(2,128)(2,1)S(1)}, bf16[1,3072]{1,0:T(2,128)(2,1)S(1)}, u32[]{:S(2)}, u32[]{:S(2)}) collective-permute-start(bf16[1,3072]{1,0:T(2,128)(2,1)S(1)} %get-tuple-element.67), channel_id=1, source_target_pairs={{0,12},{4,0},{8,4},{12,8},{1,13},{5,1},{9,5},{13,9},{2,14},{6,2},{... | collective-permute-start | bytes 18440 | tf_op jit(solution)/shard_map/l_3/ppermute | solution.py:35
  (16 other events, 185.3 us)

commit v5 on v4

--- a/solution.py
+++ b/solution.py
@@ -259,13 +259,11 @@
 
 def late_kernel(rows, total_ref, late_ref, *refs):
     piece_refs, out_refs = refs[:3], refs[-rows:]
-    half = piece_refs[0].shape[0]
     span = out_refs[0].shape[0]
+    weights = jnp.concatenate([piece_ref[...] for piece_ref in piece_refs], axis=0)
     for k in range(rows):
         lines = slice(k * span, (k + 1) * span)
-        total = total_ref[lines, :]
-        for n in range(3):
-            total = total + dot32(late_ref[lines, n * half : (n + 1) * half], piece_refs[n][...])
+        total = total_ref[lines, :] + dot32(late_ref[lines, :], weights)
         out_refs[k][...] = total.astype(jnp.bfloat16)
 
 

time: 158 us -> 158 us (level)
  transfers between devices with their start and end apart: 30 -> 30, of which waited for: 13 -> 13; matrix products, arithmetic and copies ran while one was open for 2% -> 2% of each run, Pallas kernels for 22% -> 21%
where the time goes in v5:
time: 158 us
  waiting for transfers between devices  81.5 us (52%)
  starting transfers between devices  35.8 us (23%)
  Pallas kernels  34.7 us (22%)
  local copies, waits for them, and re-layouts  4.83 us (3%)
    ppermute x30, waiting for transfers between devices, send(): return lax.ppermute(values, axis, pairs)  81.5 us
    ppermute x30, starting transfers between devices, send(): return lax.ppermute(values, axis, pairs)  35.8 us
    pallas_call x2, Pallas kernels, project_early(): pl.pallas_call(lambda place_ref, *refs: early_kernel(rows, with_late, pla...  10.7 us
    pallas_call x1, Pallas kernels, attend(): pl.pallas_call(lambda *refs: attend_kernel(rows, span, *refs), grid_spec=...  7.56 us
    pallas_call x2, Pallas kernels, settle(): pl.pallas_call(lambda *refs: settle_kernel(rows, *refs), grid_spec=pltpu....  5.66 us
    pallas_call x2, Pallas kernels, project_late(): pl.pallas_call(lambda *refs: late_kernel(rows, *refs), grid=(tiles,), in_...  5.01 us
    pallas_call x1, Pallas kernels, label_terms_by_part(): pl.pallas_call(lambda *refs: terms_kernel(rows, *refs), grid_spec=pltpu.P...  3.3 us
  transfers between devices with their start and end apart: 30, of which 13 were waited for; matrix products, arithmetic and copies ran while one was open for 2% of the time, Pallas kernels for 21%

profile of v5, /device:TPU:0, one launch (start us, length us, event | category | flops | bytes accessed | tf_op | source)
XLA Modules:
  0.0 157.8 jit_solution(3109982752323891858)
XLA Ops:
  2.0 3.1 %collective-permute-start = (bf16[384,768]{1,0:T(8,128)(2,1)S(1)}, bf16[384,768]{1,0:T(8,128)(2,1)S(1)}, u32[]{:S(2)}, u32[]{:S(2)}) collective-permute-start(bf16[384,768]{1,0:T(8,128)(2,1)S(1)} %get-tuple-element.75), channel_id=1, source_target_pairs={{0,4},{4,8},{8,12},{12,0},{1,5},{5,9},{9,13},{13,1},{2,6},{6,10},{... | collective-permute-start | bytes 1769480 | tf_op jit(solution)/shard_map/w0_1/ppermute | solution.py:35
  6.6 2.4 %pad.8.refs_3_ = bf16[3,960,768]{2,1,0:T(8,128)(2,1)S(1)} pad(bf16[3,764,768]{2,1,0:T(8,128)(2,1)} %bitcast.18, bf16[]{:T(256)} %constant.17.clone.1), padding=0_0x0_196x0_0 | pad | bytes 7944194 | tf_op jit(solution)/shard_map/jit(_pad)/pad | solution.py:500
  10.1 7.6 %attend.1 = (bf16[784,768]{1,0:T(8,128)(2,1)S(1)}, bf16[768,1536]{1,0:T(8,128)(2,1)S(1)}, f32[16,1536]{1,0:T(8,128)S(1)}) custom-call(s32[3]{0:T(128)S(1)} %pad_add_fusion.refs_0_.place_ref, s32[4,4]{1,0:T(4,128)S(1)} %copy-done.1, s32[4,4]{1,0:T(4,128)S(1)} %copy-done.2, bf16[3,960,768]{2,1,0:T(8,128)(2,1)S(1)} %pad.8.refs_3_, ...), custom_call_target="tpu_custom_call" | custom-call | flops 10000000000 | bytes 12000000 | tf_op jit(solution)/shard_map/attend/pallas_call | solution.py:124
  17.6 3.6 %collective-permute-done.refs_5_ = bf16[384,768]{1,0:T(8,128)(2,1)S(1)} collective-permute-done((bf16[384,768]{1,0:T(8,128)(2,1)S(1)}, bf16[384,768]{1,0:T(8,128)(2,1)S(1)}, u32[]{:S(2)}, u32[]{:S(2)}) %collective-permute-start) | collective-permute-done | bytes 589856 | tf_op jit(solution)/shard_map/w0_1/ppermute | solution.py:35
  21.2 11.8 %collective-permute-done.1.refs_5_ = bf16[384,768]{1,0:T(8,128)(2,1)S(1)} collective-permute-done((bf16[384,768]{1,0:T(8,128)(2,1)S(1)}, bf16[384,768]{1,0:T(8,128)(2,1)S(1)}, u32[]{:S(2)}, u32[]{:S(2)}) %collective-permute-start.1) | collective-permute-done | bytes 589856 | tf_op jit(solution)/shard_map/w1_1/ppermute | solution.py:35
  37.8 14.7 %collective-permute-done.4.refs_7_ = bf16[384,768]{1,0:T(8,128)(2,1)S(1)} collective-permute-done((bf16[384,768]{1,0:T(8,128)(2,1)S(1)}, bf16[384,768]{1,0:T(8,128)(2,1)S(1)}, u32[]{:S(2)}, u32[]{:S(2)}) %collective-permute-start.4) | collective-permute-done | bytes 589856 | tf_op jit(solution)/shard_map/w0_2/ppermute | solution.py:35
  52.6 10.4 %collective-permute-done.5.refs_7_ = bf16[384,768]{1,0:T(8,128)(2,1)S(1)} collective-permute-done((bf16[384,768]{1,0:T(8,128)(2,1)S(1)}, bf16[384,768]{1,0:T(8,128)(2,1)S(1)}, u32[]{:S(2)}, u32[]{:S(2)}) %collective-permute-start.5) | collective-permute-done | bytes 589856 | tf_op jit(solution)/shard_map/w1_2/ppermute | solution.py:35
  65.9 5.5 %project_early.2 = (f32[784,768]{1,0:T(8,128)S(1)}, bf16[784,1152]{1,0:T(8,128)(2,1)S(1)}) custom-call(s32[3]{0:T(128)S(1)} %pad_add_fusion.refs_0_.place_ref, bf16[784,768]{1,0:T(8,128)(2,1)S(1)} %get-tuple-element.38.refs_0_, bf16[784,768]{1,0:T(8,128)(2,1)S(1)} %collective-permute-done.2.refs_1_, bf16[784,768]{1,0:T(8,128)(2,1)S(1)} %collective-permute-done.3.refs_2_, ...), custom_call_target="tpu_custom_call" | custom-call | flops 4000000000 | bytes 1000 | tf_op jit(solution)/shard_map/project_early/pallas_call | solution.py:231
  72.8 8.2 %collective-permute-done.9.refs_11_.refs_3_.refs_4_ = bf16[384,768]{1,0:T(8,128)(2,1)S(1)} collective-permute-done((bf16[384,768]{1,0:T(8,128)(2,1)S(1)}, bf16[384,768]{1,0:T(8,128)(2,1)S(1)}, u32[]{:S(2)}, u32[]{:S(2)}) %collective-permute-start.9) | collective-permute-done | bytes 589856 | tf_op jit(solution)/shard_map/w0_3/ppermute | solution.py:35
  82.5 5.2 %project_early.3.refs_0_.refs_2_ = f32[784,768]{1,0:T(8,128)S(1)} custom-call(s32[3]{0:T(128)S(1)} %pad_add_fusion.refs_0_.place_ref, bf16[784,768]{1,0:T(8,128)(2,1)S(1)} %get-tuple-element.38.refs_0_, bf16[784,768]{1,0:T(8,128)(2,1)S(1)} %collective-permute-done.2.refs_1_, bf16[784,768]{1,0:T(8,128)(2,1)S(1)} %collective-permute-done.3.refs_2_, ...), custom_call_target="tpu_custom_call" | custom-call | flops 4000000000 | bytes 1000 | tf_op jit(solution)/shard_map/project_early/pallas_call | solution.py:231
  87.8 5.4 %collective-permute-done.10.refs_3_.refs_7_ = bf16[384,768]{1,0:T(8,128)(2,1)S(1)} collective-permute-done((bf16[384,768]{1,0:T(8,128)(2,1)S(1)}, bf16[384,768]{1,0:T(8,128)(2,1)S(1)}, u32[]{:S(2)}, u32[]{:S(2)}) %collective-permute-start.10) | collective-permute-done | bytes 589856 | tf_op jit(solution)/shard_map/w1_3/ppermute | solution.py:35
  97.0 2.5 %project_late.2 = (bf16[192,768]{1,0:T(8,128)(2,1)S(1)}, bf16[192,768]{1,0:T(8,128)(2,1)S(1)}, bf16[192,768]{1,0:T(8,128)(2,1)S(1)}, bf16[192,768]{1,0:T(8,128)(2,1)S(1)}) custom-call(f32[784,768]{1,0:T(8,128)S(1)} %get-tuple-element.42.refs_10_.refs_0_.refs_1_, bf16[784,1152]{1,0:T(8,128)(2,1)S(1)} %get-tuple-element.43.refs_1_.refs_0_, ...), custom_call_target="tpu_custom_call" | custom-call | flops 1387266048 | bytes 6000000 | tf_op jit(solution)/shard_map/project_late/pallas_call | solution.py:306
  103.7 5.8 %collective-permute-done.14.refs_4_.refs_8_ = bf16[384,768]{1,0:T(8,128)(2,1)S(1)} collective-permute-done((bf16[384,768]{1,0:T(8,128)(2,1)S(1)}, bf16[384,768]{1,0:T(8,128)(2,1)S(1)}, u32[]{:S(2)}, u32[]{:S(2)}) %collective-permute-start.14) | collective-permute-done | bytes 589856 | tf_op jit(solution)/shard_map/y1_3/ppermute | solution.py:35
  109.5 11.3 %collective-permute-done.13.refs_2_.refs_6_ = bf16[384,768]{1,0:T(8,128)(2,1)S(1)} collective-permute-done((bf16[384,768]{1,0:T(8,128)(2,1)S(1)}, bf16[384,768]{1,0:T(8,128)(2,1)S(1)}, u32[]{:S(2)}, u32[]{:S(2)}) %collective-permute-start.13) | collective-permute-done | bytes 589856 | tf_op jit(solution)/shard_map/y1_2/ppermute | solution.py:35
  121.5 1.8 %collective-permute-start.19 = (bf16[4,1536]{1,0:T(4,128)(2,1)S(1)}, bf16[4,1536]{1,0:T(4,128)(2,1)S(1)}, u32[]{:S(2)}, u32[]{:S(2)}) collective-permute-start(bf16[4,1536]{1,0:T(4,128)(2,1)S(1)} %project_pooled.1.refs_1_), channel_id=1, source_target_pairs={{0,8},{4,12},{8,0},{12,4},{1,9},{5,13},{9,1},{13,5},{2,10},{6,14},... | collective-permute-start | bytes 36872 | tf_op jit(solution)/shard_map/p_2/ppermute | solution.py:35
  123.3 1.8 %collective-permute-start.20 = (bf16[4,1536]{1,0:T(4,128)(2,1)S(1)}, bf16[4,1536]{1,0:T(4,128)(2,1)S(1)}, u32[]{:S(2)}, u32[]{:S(2)}) collective-permute-start(bf16[4,1536]{1,0:T(4,128)(2,1)S(1)} %project_pooled.1.refs_1_), channel_id=1, source_target_pairs={{0,12},{4,0},{8,4},{12,8},{1,13},{5,1},{9,5},{13,9},{2,14},{6,2},{... | collective-permute-start | bytes 36872 | tf_op jit(solution)/shard_map/p_3/ppermute | solution.py:35
  125.2 2.5 %project_late.3 = (bf16[192,768]{1,0:T(8,128)(2,1)S(1)}, bf16[192,768]{1,0:T(8,128)(2,1)S(1)}, bf16[192,768]{1,0:T(8,128)(2,1)S(1)}, bf16[192,768]{1,0:T(8,128)(2,1)S(1)}) custom-call(f32[784,768]{1,0:T(8,128)S(1)} %project_early.3.refs_0_.refs_2_, bf16[784,1152]{1,0:T(8,128)(2,1)S(1)} %get-tuple-element.43.refs_1_.refs_0_, ...), custom_call_target="tpu_custom_call" | custom-call | flops 1387266048 | bytes 6000000 | tf_op jit(solution)/shard_map/project_late/pallas_call | solution.py:306
  127.7 2.7 %collective-permute-start.21 = (bf16[192,768]{1,0:T(8,128)(2,1)S(1)}, bf16[192,768]{1,0:T(8,128)(2,1)S(1)}, u32[]{:S(2)}, u32[]{:S(2)}) collective-permute-start(bf16[192,768]{1,0:T(8,128)(2,1)S(1)} %get-tuple-element.56), channel_id=1, source_target_pairs={{0,4},{4,8},{8,12},{12,0},{1,5},{5,9},{9,13},{13,1},{2,6},{6,10},{... | collective-permute-start | bytes 884744 | tf_op jit(solution)/shard_map/m1_1/ppermute | solution.py:35
  132.9 3.3 %label_terms.1 = (bf16[4,3072]{1,0:T(4,128)(2,1)S(1)}, bf16[4,3072]{1,0:T(4,128)(2,1)S(1)}, bf16[4,3072]{1,0:T(4,128)(2,1)S(1)}, bf16[4,3072]{1,0:T(4,128)(2,1)S(1)}) custom-call(s32[3]{0:T(128)S(1)} %pad_add_fusion.refs_0_.place_ref, bf16[4,1536]{1,0:T(4,128)(2,1)S(1)} %project_pooled.1.refs_1_, bf16[4,1536]{1,0:T(4,128)(2,1)S(1)} %collective-permute-done.18.refs_2_, ...), custom_call_target="tpu_custom_call" | custom-call | flops 150994944 | bytes 12000000 | tf_op jit(solution)/shard_map/label_terms/pallas_call | solution.py:377
  138.1 2.8 %settle.2.refs_7_ = bf16[384,1536]{1,0:T(8,128)(2,1)} custom-call(s32[3]{0:T(128)S(1)} %pad_add_fusion.refs_0_.place_ref, s32[4,4]{1,0:T(4,128)S(1)} %copy-done.1, s32[4,4]{1,0:T(4,128)S(1)} %copy-done.2, bf16[192,768]{1,0:T(8,128)(2,1)S(1)} %get-tuple-element.59.refs_3_, bf16[192,768]{1,0:T(8,128)(2,1)S(1)} %collective-permute-done.15.refs_5_.refs_4_, ...), custom_call_target="tpu_custom_call" | custom-call | flops 452984832 | bytes 2000000 | tf_op jit(solution)/shard_map/settle/pallas_call | solution.py:451
  142.1 2.1 %collective-permute-start.28 = (bf16[1,3072]{1,0:T(2,128)(2,1)S(1)}, bf16[1,3072]{1,0:T(2,128)(2,1)S(1)}, u32[]{:S(2)}, u32[]{:S(2)}) collective-permute-start(bf16[1,3072]{1,0:T(2,128)(2,1)S(1)} %get-tuple-element.66), channel_id=1, source_target_pairs={{0,8},{4,12},{8,0},{12,4},{1,9},{5,13},{9,1},{13,5},{2,10},{6,14},... | collective-permute-start | bytes 18440 | tf_op jit(solution)/shard_map/l_2/ppermute | solution.py:35
  145.5 4.2 %collective-permute-done.22.refs_5_ = bf16[192,768]{1,0:T(8,128)(2,1)S(1)} collective-permute-done((bf16[192,768]{1,0:T(8,128)(2,1)S(1)}, bf16[192,768]{1,0:T(8,128)(2,1)S(1)}, u32[]{:S(2)}, u32[]{:S(2)}) %collective-permute-start.22) | collective-permute-done | bytes 294944 | tf_op jit(solution)/shard_map/m1_2/ppermute | solution.py:35
  149.7 2.8 %settle.3 = bf16[384,1536]{1,0:T(8,128)(2,1)} custom-call(s32[3]{0:T(128)S(1)} %pad_add_fusion.refs_0_.place_ref, s32[4,4]{1,0:T(4,128)S(1)} %copy-done.1, s32[4,4]{1,0:T(4,128)S(1)} %copy-done.2, bf16[192,768]{1,0:T(8,128)(2,1)S(1)} %get-tuple-element.55.refs_3_, ...), custom_call_target="tpu_custom_call", output_to_operand_aliasing={{}: (7, {})} | custom-call | flops 452984832 | bytes 2000000 | tf_op jit(solution)/shard_map/settle/pallas_call | solution.py:451
  152.6 4.0 %collective-permute-done.28.refs_3_ = bf16[1,3072]{1,0:T(2,128)(2,1)S(1)} collective-permute-done((bf16[1,3072]{1,0:T(2,128)(2,1)S(1)}, bf16[1,3072]{1,0:T(2,128)(2,1)S(1)}, u32[]{:S(2)}, u32[]{:S(2)}) %collective-permute-start.28) | collective-permute-done | bytes 6176 | tf_op jit(solution)/shard_map/l_2/ppermute | solution.py:35
  (73 shorter events, 31.3 us)
Async XLA Ops:
  2.0 19.3 %collective-permute-start = (bf16[384,768]{1,0:T(8,128)(2,1)S(1)}, bf16[384,768]{1,0:T(8,128)(2,1)S(1)}, u32[]{:S(2)}, u32[]{:S(2)}) collective-permute-start(bf16[384,768]{1,0:T(8,128)(2,1)S(1)} %get-tuple-element.75), channel_id=1, source_target_pairs={{0,4},{4,8},{8,12},{12,0},{1,5},{5,9},{9,13},{13,1},{2,6},{6,10},{... | collective-permute-start | bytes 1769480 | tf_op jit(solution)/shard_map/w0_1/ppermute | solution.py:35
  5.0 28.0 %collective-permute-start.1 = (bf16[384,768]{1,0:T(8,128)(2,1)S(1)}, bf16[384,768]{1,0:T(8,128)(2,1)S(1)}, u32[]{:S(2)}, u32[]{:S(2)}) collective-permute-start(bf16[384,768]{1,0:T(8,128)(2,1)S(1)} %get-tuple-element.74), channel_id=1, source_target_pairs={{0,4},{4,8},{8,12},{12,0},{1,5},{5,9},{9,13},{13,1},{2,6},{6,10},{... | collective-permute-start | bytes 1769480 | tf_op jit(solution)/shard_map/w1_1/ppermute | solution.py:35
  33.0 29.9 %collective-permute-start.3 = (bf16[784,768]{1,0:T(8,128)(2,1)S(1)}, bf16[784,768]{1,0:T(8,128)(2,1)S(1)}, u32[]{:S(2)}, u32[]{:S(2)}) collective-permute-start(bf16[784,768]{1,0:T(8,128)(2,1)S(1)} %get-tuple-element.38.refs_0_), channel_id=1, source_target_pairs={{0,2},{1,3},{2,0},{3,1},{4,6},{5,7},{6,4},{7,5},{8,10},{9,11},{10,... | collective-permute-start | bytes 3612680 | tf_op jit(solution)/shard_map/h_2/ppermute | solution.py:35
  34.5 18.1 %collective-permute-start.4 = (bf16[384,768]{1,0:T(8,128)(2,1)S(1)}, bf16[384,768]{1,0:T(8,128)(2,1)S(1)}, u32[]{:S(2)}, u32[]{:S(2)}) collective-permute-start(bf16[384,768]{1,0:T(8,128)(2,1)S(1)} %collective-permute-done.refs_5_), channel_id=1, source_target_pairs={{0,4},{4,8},{8,12},{12,0},{1,5},{5,9},{9,13},{13,1},{2,6},{6,10},{... | collective-permute-start | bytes 1769480 | tf_op jit(solution)/shard_map/w0_2/ppermute | solution.py:35
  34.5 28.4 %collective-permute-start.5 = (bf16[384,768]{1,0:T(8,128)(2,1)S(1)}, bf16[384,768]{1,0:T(8,128)(2,1)S(1)}, u32[]{:S(2)}, u32[]{:S(2)}) collective-permute-start(bf16[384,768]{1,0:T(8,128)(2,1)S(1)} %collective-permute-done.1.refs_5_), channel_id=1, source_target_pairs={{0,4},{4,8},{8,12},{12,0},{1,5},{5,9},{9,13},{13,1},{2,6},{6,10},{... | collective-permute-start | bytes 1769480 | tf_op jit(solution)/shard_map/w1_2/ppermute | solution.py:35
  35.8 27.1 %collective-permute-start.6 = (bf16[384,768]{1,0:T(8,128)(2,1)S(1)}, bf16[384,768]{1,0:T(8,128)(2,1)S(1)}, u32[]{:S(2)}, u32[]{:S(2)}) collective-permute-start(bf16[384,768]{1,0:T(8,128)(2,1)S(1)} %collective-permute-done.refs_5_), channel_id=1, source_target_pairs={{0,16},{16,0},{1,17},{17,1},{2,18},{18,2},{3,19},{19,3},{4,20},{20... | collective-permute-start | bytes 1769480 | tf_op jit(solution)/shard_map/y0_1/ppermute | solution.py:35
  37.3 25.6 %collective-permute-start.7 = (bf16[384,768]{1,0:T(8,128)(2,1)S(1)}, bf16[384,768]{1,0:T(8,128)(2,1)S(1)}, u32[]{:S(2)}, u32[]{:S(2)}) collective-permute-start(bf16[384,768]{1,0:T(8,128)(2,1)S(1)} %collective-permute-done.1.refs_5_), channel_id=1, source_target_pairs={{0,16},{16,0},{1,17},{17,1},{2,18},{18,2},{3,19},{19,3},{4,20},{20... | collective-permute-start | bytes 1769480 | tf_op jit(solution)/shard_map/y1_1/ppermute | solution.py:35
  52.6 12.5 %collective-permute-start.2 = (bf16[784,768]{1,0:T(8,128)(2,1)S(1)}, bf16[784,768]{1,0:T(8,128)(2,1)S(1)}, u32[]{:S(2)}, u32[]{:S(2)}) collective-permute-start(bf16[784,768]{1,0:T(8,128)(2,1)S(1)} %get-tuple-element.38.refs_0_), channel_id=1, source_target_pairs={{0,1},{1,0},{2,3},{3,2},{4,5},{5,4},{6,7},{7,6},{8,9},{9,8},{10,11... | collective-permute-start | bytes 3612680 | tf_op jit(solution)/shard_map/h_1/ppermute | solution.py:35
  63.0 18.0 %collective-permute-start.9 = (bf16[384,768]{1,0:T(8,128)(2,1)S(1)}, bf16[384,768]{1,0:T(8,128)(2,1)S(1)}, u32[]{:S(2)}, u32[]{:S(2)}) collective-permute-start(bf16[384,768]{1,0:T(8,128)(2,1)S(1)} %collective-permute-done.4.refs_7_), channel_id=1, source_target_pairs={{0,4},{4,8},{8,12},{12,0},{1,5},{5,9},{9,13},{13,1},{2,6},{6,10},{... | collective-permute-start | bytes 1769480 | tf_op jit(solution)/shard_map/w0_3/ppermute | solution.py:35
  63.4 17.6 %collective-permute-start.11 = (bf16[384,768]{1,0:T(8,128)(2,1)S(1)}, bf16[384,768]{1,0:T(8,128)(2,1)S(1)}, u32[]{:S(2)}, u32[]{:S(2)}) collective-permute-start(bf16[384,768]{1,0:T(8,128)(2,1)S(1)} %collective-permute-done.4.refs_7_), channel_id=1, source_target_pairs={{0,16},{16,0},{1,17},{17,1},{2,18},{18,2},{3,19},{19,3},{4,20},{20... | collective-permute-start | bytes 1769480 | tf_op jit(solution)/shard_map/y0_2/ppermute | solution.py:35
  71.4 21.8 %collective-permute-start.10 = (bf16[384,768]{1,0:T(8,128)(2,1)S(1)}, bf16[384,768]{1,0:T(8,128)(2,1)S(1)}, u32[]{:S(2)}, u32[]{:S(2)}) collective-permute-start(bf16[384,768]{1,0:T(8,128)(2,1)S(1)} %collective-permute-done.5.refs_7_), channel_id=1, source_target_pairs={{0,4},{4,8},{8,12},{12,0},{1,5},{5,9},{9,13},{13,1},{2,6},{6,10},{... | collective-permute-start | bytes 1769480 | tf_op jit(solution)/shard_map/w1_3/ppermute | solution.py:35
  81.0 14.4 %collective-permute-start.12 = (bf16[384,768]{1,0:T(8,128)(2,1)S(1)}, bf16[384,768]{1,0:T(8,128)(2,1)S(1)}, u32[]{:S(2)}, u32[]{:S(2)}) collective-permute-start(bf16[384,768]{1,0:T(8,128)(2,1)S(1)} %collective-permute-done.9.refs_11_.refs_3_.refs_4_), channel_id=1, source_target_pairs={{0,16},{16,0},{1,17},{17,1},{2,18},{18,2},{3,19},{19,3},{4,20},{20... | collective-permute-start | bytes 1769480 | tf_op jit(solution)/shard_map/y0_3/ppermute | solution.py:35
  93.2 16.2 %collective-permute-start.14 = (bf16[384,768]{1,0:T(8,128)(2,1)S(1)}, bf16[384,768]{1,0:T(8,128)(2,1)S(1)}, u32[]{:S(2)}, u32[]{:S(2)}) collective-permute-start(bf16[384,768]{1,0:T(8,128)(2,1)S(1)} %collective-permute-done.10.refs_3_.refs_7_), channel_id=1, source_target_pairs={{0,16},{16,0},{1,17},{17,1},{2,18},{18,2},{3,19},{19,3},{4,20},{20... | collective-permute-start | bytes 1769480 | tf_op jit(solution)/shard_map/y1_3/ppermute | solution.py:35
  95.5 25.3 %collective-permute-start.13 = (bf16[384,768]{1,0:T(8,128)(2,1)S(1)}, bf16[384,768]{1,0:T(8,128)(2,1)S(1)}, u32[]{:S(2)}, u32[]{:S(2)}) collective-permute-start(bf16[384,768]{1,0:T(8,128)(2,1)S(1)} %collective-permute-done.5.refs_7_), channel_id=1, source_target_pairs={{0,16},{16,0},{1,17},{17,1},{2,18},{18,2},{3,19},{19,3},{4,20},{20... | collective-permute-start | bytes 1769480 | tf_op jit(solution)/shard_map/y1_2/ppermute | solution.py:35
  99.5 23.8 %collective-permute-start.15 = (bf16[192,768]{1,0:T(8,128)(2,1)S(1)}, bf16[192,768]{1,0:T(8,128)(2,1)S(1)}, u32[]{:S(2)}, u32[]{:S(2)}) collective-permute-start(bf16[192,768]{1,0:T(8,128)(2,1)S(1)} %get-tuple-element.48), channel_id=1, source_target_pairs={{0,4},{4,8},{8,12},{12,0},{1,5},{5,9},{9,13},{13,1},{2,6},{6,10},{... | collective-permute-start | bytes 884744 | tf_op jit(solution)/shard_map/m0_1/ppermute | solution.py:35
  101.2 23.9 %collective-permute-start.16 = (bf16[192,768]{1,0:T(8,128)(2,1)S(1)}, bf16[192,768]{1,0:T(8,128)(2,1)S(1)}, u32[]{:S(2)}, u32[]{:S(2)}) collective-permute-start(bf16[192,768]{1,0:T(8,128)(2,1)S(1)} %get-tuple-element.49), channel_id=1, source_target_pairs={{0,8},{4,12},{8,0},{12,4},{1,9},{5,13},{9,1},{13,5},{2,10},{6,14},... | collective-permute-start | bytes 884744 | tf_op jit(solution)/shard_map/m0_2/ppermute | solution.py:35
  102.9 22.3 %collective-permute-start.17 = (bf16[192,768]{1,0:T(8,128)(2,1)S(1)}, bf16[192,768]{1,0:T(8,128)(2,1)S(1)}, u32[]{:S(2)}, u32[]{:S(2)}) collective-permute-start(bf16[192,768]{1,0:T(8,128)(2,1)S(1)} %get-tuple-element.50), channel_id=1, source_target_pairs={{0,12},{4,0},{8,4},{12,8},{1,13},{5,1},{9,5},{13,9},{2,14},{6,2},{... | collective-permute-start | bytes 884744 | tf_op jit(solution)/shard_map/m0_3/ppermute | solution.py:35
  121.3 6.4 %collective-permute-start.18 = (bf16[4,1536]{1,0:T(4,128)(2,1)S(1)}, bf16[4,1536]{1,0:T(4,128)(2,1)S(1)}, u32[]{:S(2)}, u32[]{:S(2)}) collective-permute-start(bf16[4,1536]{1,0:T(4,128)(2,1)S(1)} %project_pooled.1.refs_1_), channel_id=1, source_target_pairs={{0,4},{4,8},{8,12},{12,0},{1,5},{5,9},{9,13},{13,1},{2,6},{6,10},{... | collective-permute-start | bytes 36872 | tf_op jit(solution)/shard_map/p_1/ppermute | solution.py:35
  127.7 16.4 %collective-permute-start.21 = (bf16[192,768]{1,0:T(8,128)(2,1)S(1)}, bf16[192,768]{1,0:T(8,128)(2,1)S(1)}, u32[]{:S(2)}, u32[]{:S(2)}) collective-permute-start(bf16[192,768]{1,0:T(8,128)(2,1)S(1)} %get-tuple-element.56), channel_id=1, source_target_pairs={{0,4},{4,8},{8,12},{12,0},{1,5},{5,9},{9,13},{13,1},{2,6},{6,10},{... | collective-permute-start | bytes 884744 | tf_op jit(solution)/shard_map/m1_1/ppermute | solution.py:35
  130.4 19.3 %collective-permute-start.22 = (bf16[192,768]{1,0:T(8,128)(2,1)S(1)}, bf16[192,768]{1,0:T(8,128)(2,1)S(1)}, u32[]{:S(2)}, u32[]{:S(2)}) collective-permute-start(bf16[192,768]{1,0:T(8,128)(2,1)S(1)} %get-tuple-element.57), channel_id=1, source_target_pairs={{0,8},{4,12},{8,0},{12,4},{1,9},{5,13},{9,1},{13,5},{2,10},{6,14},... | collective-permute-start | bytes 884744 | tf_op jit(solution)/shard_map/m1_2/ppermute | solution.py:35
  131.2 18.5 %collective-permute-start.23 = (bf16[192,768]{1,0:T(8,128)(2,1)S(1)}, bf16[192,768]{1,0:T(8,128)(2,1)S(1)}, u32[]{:S(2)}, u32[]{:S(2)}) collective-permute-start(bf16[192,768]{1,0:T(8,128)(2,1)S(1)} %get-tuple-element.58), channel_id=1, source_target_pairs={{0,12},{4,0},{8,4},{12,8},{1,13},{5,1},{9,5},{13,9},{2,14},{6,2},{... | collective-permute-start | bytes 884744 | tf_op jit(solution)/shard_map/m1_3/ppermute | solution.py:35
  141.6 11.0 %collective-permute-start.27 = (bf16[1,3072]{1,0:T(2,128)(2,1)S(1)}, bf16[1,3072]{1,0:T(2,128)(2,1)S(1)}, u32[]{:S(2)}, u32[]{:S(2)}) collective-permute-start(bf16[1,3072]{1,0:T(2,128)(2,1)S(1)} %get-tuple-element.65), channel_id=1, source_target_pairs={{0,4},{4,8},{8,12},{12,0},{1,5},{5,9},{9,13},{13,1},{2,6},{6,10},{... | collective-permute-start | bytes 18440 | tf_op jit(solution)/shard_map/l_1/ppermute | solution.py:35
  142.1 14.5 %collective-permute-start.28 = (bf16[1,3072]{1,0:T(2,128)(2,1)S(1)}, bf16[1,3072]{1,0:T(2,128)(2,1)S(1)}, u32[]{:S(2)}, u32[]{:S(2)}) collective-permute-start(bf16[1,3072]{1,0:T(2,128)(2,1)S(1)} %get-tuple-element.66), channel_id=1, source_target_pairs={{0,8},{4,12},{8,0},{12,4},{1,9},{5,13},{9,1},{13,5},{2,10},{6,14},... | collective-permute-start | bytes 18440 | tf_op jit(solution)/shard_map/l_2/ppermute | solution.py:35
  144.2 12.4 %collective-permute-start.29 = (bf16[1,3072]{1,0:T(2,128)(2,1)S(1)}, bf16[1,3072]{1,0:T(2,128)(2,1)S(1)}, u32[]{:S(2)}, u32[]{:S(2)}) collective-permute-start(bf16[1,3072]{1,0:T(2,128)(2,1)S(1)} %get-tuple-element.67), channel_id=1, source_target_pairs={{0,12},{4,0},{8,4},{12,8},{1,13},{5,1},{9,5},{13,9},{2,14},{6,2},{... | collective-permute-start | bytes 18440 | tf_op jit(solution)/shard_map/l_3/ppermute | solution.py:35
  (16 other events, 183.8 us)
